TPU v7x, 256 devices: a whole 4x4x8 slice. The times are simulated.
256 devices in a mesh: row: 8 (over x, core), col: 8 (over z), layer: 4 (over y).
Axes of the slice: x: 4, y: 4, z: 8, core: 2. Of those that a mesh axis runs over, the one named last changes fastest.
Arguments:
- amplitudes: float32 [512, 147456], P('col', ('row', 'layer')), may hold values from -6 to 6
- integrals: float32 [1024, 147456], P('col', ('row', 'layer')), may hold values from -0.015625 to 0.015625
Outputs:
- ladder: float32 [512, 1024], P(('row', 'layer'), 'col')
All inputs are finite; a program needn't handle non-finite values.
Results may differ from a plain program's by a relative error of at most 0.000082.
Values sent between devices are 32-bit elements; how exact they have to be, the bound alone decides.
No kernel may reach another device: no remote copies, remote signals or barrier semaphores. Data moves between devices by JAX's collectives and lax.ppermute only.
A program may use at most 64 MiB of HBM per device.

v0:
```python
import jax
import jax.numpy as jnp
from jax import lax
from jax.sharding import PartitionSpec as P


def contract_last(left, right):
    return lax.dot_general(
        left,
        right,
        (((1,), (1,)), ((), ())),
        precision=lax.Precision.HIGHEST,
        preferred_element_type=jnp.float32,
    )


def on_device(amplitudes, integrals):
    partial_sum = contract_last(lax.all_gather(amplitudes, "col", axis=0, tiled=True), integrals)
    return lax.psum_scatter(0.5 * partial_sum, ("row", "layer"), scatter_dimension=0, tiled=True)


def solution(mesh):
    in_specs = (P("col", ("row", "layer")), P("col", ("row", "layer")))
    out_specs = P(("row", "layer"), "col")
    return jax.shard_map(
        on_device, mesh=mesh, in_specs=in_specs, out_specs=out_specs, check_vma=False
    )
```

profile of v0, /device:TPU:1, one launch (start us, length us, event | category | flops | bytes accessed | tf_op | source)
XLA Modules:
  0.0 215.7 jit_solution(10695305505949290143)
XLA Ops:
  6.5 0.0 copy-start
  6.5 0.0 all-gather.2.cloned.1.call-start
  6.5 0.7 all-gather.2.cloned.1.call-update
  7.3 0.0 reduce-scatter.2.cloned.1.call-start
  7.3 109.6 %all-gather.2.cloned.1.call-done = f32[512,4608]{1,0:T(8,128)} async-done(((f32[64,4608]{1,0:T(8,128)}), f32[512,4608]{1,0:T(8,128)}) %all-gather.2.cloned.1.call-update) | async-done | bytes 9437200 | tf_op jit(solution)/shard_map/all_gather | solution.py:18
  117.0 0.0 copy-done
  117.0 10.7 %convolution_multiply_fusion = f32[512,128]{1,0:T(8,128)} fusion(f32[512,4608]{1,0:T(8,128)} %all-gather.2.cloned.1.call-done, f32[128,4608]{1,0:T(8,128)S(1)} %copy-done), kind=kOutput, calls=%fused_computation | convolution fusion | flops 3623944192 | bytes 12058624 | tf_op jit(solution)/shard_map/dot_general | solution.py:8
  127.6 0.0 reduce-scatter.2.cloned.1.call-update
  127.6 81.2 %reduce-scatter.2.cloned.1.call-done = f32[16,128]{1,0:T(8,128)} async-done(((f32[512,128]{1,0:T(8,128)}), f32[16,128]{1,0:T(8,128)}) %reduce-scatter.2.cloned.1.call-update) | async-done | bytes 8208 | tf_op jit(solution)/shard_map/reduce_scatter | solution.py:19
Async XLA Ops:
  6.5 110.4 %copy-start = (f32[128,4608]{1,0:T(8,128)S(1)}, f32[128,4608]{1,0:T(8,128)}, u32[]{:S(2)}) copy-start(f32[128,4608]{1,0:T(8,128)} %param.3) | copy-start | bytes 7077892
  6.5 110.4 %all-gather.2.cloned.1.call-start = ((), (), s32[]{:S(2)}) async-start(), calls=%async_computation.1 | async-start | bytes 10616832 | tf_op jit(solution)/shard_map/all_gather | solution.py:18
  7.3 201.6 %reduce-scatter.2.cloned.1.call-start = ((), (), s32[]{:S(2)}) async-start(), calls=%async_computation.2 | async-start | bytes 270336 | tf_op jit(solution)/shard_map/reduce_scatter | solution.py:19
Sparse Core Ops, SparseCore 0:
  9.1 107.7 all-gather.1
  127.8 81.0 reduce-scatter.1
where the time goes:
time: 217 us; the launch traced here: 216 us
  waiting for transfers between devices  192 us (88%)
  between operations  13.4 us (6%)
  matrix products  10.7 us (5%)
    all_gather x1, waiting for transfers between devices, on_device(): lax.all_gather(amplitudes, 'col', axis=0, tiled=True)  110 us
    reduce_scatter x1, waiting for transfers between devices, on_device(): lax.psum_scatter(0.5 * partial_sum, ('row', 'layer'), scatter_dimension=0...  81.2 us
    dot_general x1, matrix products, contract_last(): lax.dot_general(left, right, (((1,), (1,)), ((), ())), precision=lax.Prec...  10.7 us
  transfers between devices with their start and end apart: 2, of which 2 were waited for; matrix products, arithmetic and copies ran while one was open for 0% of the time, Pallas kernels for 0%

commit v1 on v0

--- a/solution.py
+++ b/solution.py
@@ -16,7 +16,10 @@
 
 def on_device(amplitudes, integrals):
     partial_sum = contract_last(lax.all_gather(amplitudes, "col", axis=0, tiled=True), integrals)
-    return lax.psum_scatter(0.5 * partial_sum, ("row", "layer"), scatter_dimension=0, tiled=True)
+    rows, columns = partial_sum.shape
+    shares = lax.axis_size(("row", "layer"))
+    blocks = (0.5 * partial_sum).reshape(shares, rows // shares, columns)
+    return lax.all_to_all(blocks, ("row", "layer"), 0, 0).sum(0)
 
 
 def solution(mesh):

time: 217 us -> 151 us (0.70)
  waiting for transfers between devices: 192 us -> 110 us
  blocking collectives: 0 us -> 16.1 us
    reduce_scatter x1 -> x0, waiting for transfers between devices: 81.2 us -> none  [on_device(): lax.psum_scatter(0.5 * partial_sum, ('row', 'layer'), scatter_dimension=0...]
    all_to_all x0 -> x1, blocking collectives: none -> 16.1 us  [on_device(): return lax.all_to_all(blocks, ('row', 'layer'), 0, 0).sum(0)]
  transfers between devices with their start and end apart: 2 -> 1, of which waited for: 2 -> 1; matrix products, arithmetic and copies ran while one was open for 0% -> 0% of each run, Pallas kernels for 0% -> 0%
where the time goes in v1:
time: 151 us
  waiting for transfers between devices  110 us (73%)
  blocking collectives  16.1 us (11%)
  between operations  13.4 us (9%)
  matrix products  10 us (7%)
    all_gather x1, waiting for transfers between devices, on_device(): lax.all_gather(amplitudes, 'col', axis=0, tiled=True)  110 us
    all_to_all x1, blocking collectives, on_device(): return lax.all_to_all(blocks, ('row', 'layer'), 0, 0).sum(0)  16.1 us
    dot_general x1, matrix products, contract_last(): lax.dot_general(left, right, (((1,), (1,)), ((), ())), precision=lax.Prec...  10 us
  transfers between devices with their start and end apart: 1, of which 1 were waited for; matrix products, arithmetic and copies ran while one was open for 0% of the time, Pallas kernels for 0%

profile of v1, /device:TPU:1, one launch (start us, length us, event | category | flops | bytes accessed | tf_op | source)
XLA Modules:
  0.0 150.6 jit_solution(2829328679407402660)
XLA Ops:
  6.5 0.0 copy-start
  6.5 0.0 all-gather.2.cloned.1.call-start
  6.5 0.7 all-gather.2.cloned.1.call-update
  7.3 109.7 %all-gather.2.cloned.1.call-done = f32[512,4608]{1,0:T(8,128)} async-done(((f32[64,4608]{1,0:T(8,128)}), f32[512,4608]{1,0:T(8,128)}) %all-gather.2.cloned.1.call-update) | async-done | bytes 9437200 | tf_op jit(solution)/shard_map/all_gather | solution.py:18
  117.0 0.0 copy-done
  117.0 10.0 %convolution_multiply_fusion = f32[512,128]{1,0:T(8,128)S(1)} fusion(f32[512,4608]{1,0:T(8,128)} %all-gather.2.cloned.1.call-done, f32[128,4608]{1,0:T(8,128)S(1)} %copy-done), kind=kOutput, calls=%fused_computation | convolution fusion | flops 3623944192 | bytes 12058624 | tf_op jit(solution)/shard_map/dot_general | solution.py:8
  127.0 16.1 %all_to_all.5 = f32[32,16,128]{2,1,0:T(8,128)S(1)} all-to-all(f32[32,16,128]{2,1,0:T(8,128)S(1)} %bitcast.3), channel_id=1, replica_groups=mesh['row'=8,'col'=8,'layer'=4] {'row','layer'}, dimensions={0} | all-to-all | bytes 524288 | tf_op jit(solution)/shard_map/all_to_all | solution.py:22
  143.1 0.6 reduce_sum.9
Async XLA Ops:
  6.5 110.4 %copy-start = (f32[128,4608]{1,0:T(8,128)S(1)}, f32[128,4608]{1,0:T(8,128)}, u32[]{:S(2)}) copy-start(f32[128,4608]{1,0:T(8,128)} %param.3) | copy-start | bytes 7077892
  6.5 110.4 %all-gather.2.cloned.1.call-start = ((), (), s32[]{:S(2)}) async-start(), calls=%async_computation.1 | async-start | bytes 10616832 | tf_op jit(solution)/shard_map/all_gather | solution.py:18
Sparse Core Ops, SparseCore 0:
  9.1 107.7 all-gather.1

commit v2 on v1

--- a/solution.py
+++ b/solution.py
@@ -15,10 +15,31 @@
 
 
 def on_device(amplitudes, integrals):
-    partial_sum = contract_last(lax.all_gather(amplitudes, "col", axis=0, tiled=True), integrals)
-    rows, columns = partial_sum.shape
+    levels = lax.axis_size("col")
+    half = amplitudes.shape[1] // 2
+    far = levels // 2
+    a_parts = [amplitudes[:, :half], amplitudes[:, half:]]
+    b_parts = [integrals[:, :half], integrals[:, half:]]
+    hop_up = [(i, (i + 1) % levels) for i in range(levels)]
+    hop_down = [(i, (i - 1) % levels) for i in range(levels)]
+
+    terms = [[] for _ in range(levels)]
+    terms[0] = [contract_last(a, b) for a, b in zip(a_parts, b_parts)]
+    up, down = list(a_parts), list(a_parts)
+    for hop in range(1, far):
+        for i in (0, 1):
+            up[i] = lax.ppermute(up[i], "col", hop_up)
+            down[1 - i] = lax.ppermute(down[1 - i], "col", hop_down)
+        for i in (0, 1):
+            terms[-hop % levels].append(contract_last(up[i], b_parts[i]))
+            terms[hop].append(contract_last(down[1 - i], b_parts[1 - i]))
+    terms[far].append(contract_last(lax.ppermute(up[0], "col", hop_up), b_parts[0]))
+    terms[far].append(contract_last(lax.ppermute(down[1], "col", hop_down), b_parts[1]))
+
+    by_distance = jnp.stack([0.5 * (t[0] + t[1]) for t in terms])
+    partial_sum = jnp.roll(by_distance, lax.axis_index("col"), axis=0)
     shares = lax.axis_size(("row", "layer"))
-    blocks = (0.5 * partial_sum).reshape(shares, rows // shares, columns)
+    blocks = partial_sum.reshape(shares, -1, partial_sum.shape[-1])
     return lax.all_to_all(blocks, ("row", "layer"), 0, 0).sum(0)
 
 

time: 151 us -> 128 us (0.85)
  waiting for transfers between devices: 110 us -> 51.2 us
  starting transfers between devices: 0.01 us -> 25.9 us
  matrix products: 10 us -> 28.4 us
  between operations: 13.4 us -> 0.14 us
  local copies, waits for them, and re-layouts: 0.01 us -> 2.58 us
  blocking collectives: 16.1 us -> 18.5 us
    all_gather x1 -> x0, waiting for transfers between devices: 110 us -> none  [on_device(): lax.all_gather(amplitudes, 'col', axis=0, tiled=True)]
    ppermute x0 -> x14, waiting for transfers between devices: none -> 51.2 us  [the longest x6 30.1 us: on_device(): down[1 - i] = lax.ppermute(down[1 - i], 'col', hop_down)]
    ppermute x0 -> x14, starting transfers between devices: none -> 25.9 us  [the longest x6 22.5 us: on_device(): down[1 - i] = lax.ppermute(down[1 - i], 'col', hop_down)]
    dot_general x1 -> x16, matrix products: 10 us -> 28.4 us  [contract_last(): lax.dot_general(left, right, (((1,), (1,)), ((), ())), precision=lax.Prec...]
    slice x0 -> x1, local copies, waits for them, and re-layouts: none -> 2.51 us  [on_device(): a_parts = [amplitudes[:, :half], amplitudes[:, half:]]]
    all_to_all x1, blocking collectives: 16.1 us -> 18.5 us  [on_device(): return lax.all_to_all(blocks, ('row', 'layer'), 0, 0).sum(0)]
  transfers between devices with their start and end apart: 1 -> 14, of which waited for: 1 -> 8; matrix products, arithmetic and copies ran while one was open for 0% -> 17% of each run, Pallas kernels for 0% -> 0%
where the time goes in v2:
time: 128 us; the launch traced here: 127 us
  waiting for transfers between devices  51.2 us (40%)
  matrix products  28.4 us (22%)
  starting transfers between devices  25.9 us (20%)
  blocking collectives  18.5 us (14%)
  local copies, waits for them, and re-layouts  2.58 us (2%)
    ppermute x6, waiting for transfers between devices, on_device(): down[1 - i] = lax.ppermute(down[1 - i], 'col', hop_down)  30.1 us
    dot_general x16, matrix products, contract_last(): lax.dot_general(left, right, (((1,), (1,)), ((), ())), precision=lax.Prec...  28.4 us
    ppermute x6, starting transfers between devices, on_device(): down[1 - i] = lax.ppermute(down[1 - i], 'col', hop_down)  22.5 us
    all_to_all x1, blocking collectives, on_device(): return lax.all_to_all(blocks, ('row', 'layer'), 0, 0).sum(0)  18.5 us
    ppermute x6, waiting for transfers between devices, on_device(): up[i] = lax.ppermute(up[i], 'col', hop_up)  11 us
    ppermute x1, waiting for transfers between devices, on_device(): lax.ppermute(down[1], 'col', hop_down)  6.82 us
    ppermute x1, starting transfers between devices, on_device(): lax.ppermute(down[1], 'col', hop_down)  3.41 us
    ppermute x1, waiting for transfers between devices, on_device(): lax.ppermute(up[0], 'col', hop_up)  3.28 us
  transfers between devices with their start and end apart: 14, of which 8 were waited for; matrix products, arithmetic and copies ran while one was open for 17% of the time, Pallas kernels for 0%

profile of v2, /device:TPU:1, one launch (start us, length us, event | category | flops | bytes accessed | tf_op | source)
XLA Modules:
  0.0 127.4 jit_solution(3356734277726742138)
XLA Ops:
  0.0 0.0 copy-start
  0.0 2.5 %fusion.42 = (f32[64,2304]{1,0:T(8,128)}, f32[64,2304]{1,0:T(8,128)}) fusion(f32[64,4608]{1,0:T(8,128)} %param.2), kind=kLoop, calls=%fused_computation.67 | loop fusion | bytes 2359296 | tf_op jit(solution)/shard_map/slice | solution.py:21
  2.5 0.0 copy-start.1
  2.5 6.4 %collective-permute-start = (f32[64,2304]{1,0:T(8,128)}, f32[64,2304]{1,0:T(8,128)}, u32[]{:S(2)}, u32[]{:S(2)}) collective-permute-start(f32[64,2304]{1,0:T(8,128)} %get-tuple-element.5), channel_id=1, source_target_pairs={{0,28},{4,0},{8,4},{12,8},{16,12},{20,16},{24,20},{28,24},{1,29},{... | collective-permute-start | bytes 1769480 | tf_op jit(solution)/shard_map/ppermute | solution.py:32
  8.9 0.0 collective-permute-start.11
  8.9 2.7 %collective-permute-start.1 = (f32[64,2304]{1,0:T(8,128)}, f32[64,2304]{1,0:T(8,128)}, u32[]{:S(2)}, u32[]{:S(2)}) collective-permute-start(f32[64,2304]{1,0:T(8,128)} %get-tuple-element.6), channel_id=1, source_target_pairs={{0,28},{4,0},{8,4},{12,8},{16,12},{20,16},{24,20},{28,24},{1,29},{... | collective-permute-start | bytes 1769480 | tf_op jit(solution)/shard_map/ppermute | solution.py:32
  11.6 0.0 collective-permute-start.6
  11.6 0.0 copy-done
  11.6 3.0 %fusion.38 = f32[64,128]{1,0:T(8,128)} fusion(f32[128,4608]{1,0:T(8,128)S(1)} %copy-done, f32[64,4608]{1,0:T(8,128)} %param.2), kind=kOutput, calls=%fused_computation.46 | convolution fusion | flops 226492416 | bytes 1802240 | tf_op jit(solution)/shard_map/dot_general | solution.py:8
  14.6 0.0 copy-done.1
  14.6 2.1 %constant_dynamic-update-slice_fusion.15 = (f32[16,64,128]{2,1,0:T(8,128)S(1)}, f32[1,64,128]{2,1,0:T(8,128)S(1)}) fusion(f32[64,128]{1,0:T(8,128)} %fusion.38, f32[128,4608]{1,0:T(8,128)S(1)} %copy-done, f32[64,4608]{1,0:T(8,128)S(1)} %copy-done.1), kind=kOutput, calls=%fused_computation.63 | convolution fusion | flops 226508800 | bytes 1867776 | tf_op jit(solution)/shard_map/dot_general | solution.py:8
  16.7 4.5 %collective-permute-done = f32[64,2304]{1,0:T(8,128)} collective-permute-done((f32[64,2304]{1,0:T(8,128)}, f32[64,2304]{1,0:T(8,128)}, u32[]{:S(2)}, u32[]{:S(2)}) %collective-permute-start) | collective-permute-done | bytes 589856 | tf_op jit(solution)/shard_map/ppermute | solution.py:32
  21.2 3.4 %collective-permute-start.2 = (f32[64,2304]{1,0:T(8,128)}, f32[64,2304]{1,0:T(8,128)S(1)}, u32[]{:S(2)}, u32[]{:S(2)}) collective-permute-start(f32[64,2304]{1,0:T(8,128)} %collective-permute-done), channel_id=1, source_target_pairs={{0,28},{4,0},{8,4},{12,8},{16,12},{20,16},{24,20},{28,24},{1,29},{... | collective-permute-start | bytes 1769480 | tf_op jit(solution)/shard_map/ppermute | solution.py:32
  24.6 0.0 collective-permute-done.11
  24.6 0.0 collective-permute-start.12
  24.6 2.4 %fusion.16 = f32[64,128]{1,0:T(8,128)S(1)} fusion(f32[64,2304]{1,0:T(8,128)} %collective-permute-done.11, f32[128,4608]{1,0:T(8,128)S(1)} %copy-done), kind=kOutput, calls=%fused_computation.24 | convolution fusion | flops 226492416 | bytes 1802240 | tf_op jit(solution)/shard_map/dot_general | solution.py:8
  27.1 6.8 %collective-permute-done.1 = f32[64,2304]{1,0:T(8,128)} collective-permute-done((f32[64,2304]{1,0:T(8,128)}, f32[64,2304]{1,0:T(8,128)}, u32[]{:S(2)}, u32[]{:S(2)}) %collective-permute-start.1) | collective-permute-done | bytes 589856 | tf_op jit(solution)/shard_map/ppermute | solution.py:32
  33.9 3.4 %collective-permute-start.3 = (f32[64,2304]{1,0:T(8,128)}, f32[64,2304]{1,0:T(8,128)S(1)}, u32[]{:S(2)}, u32[]{:S(2)}) collective-permute-start(f32[64,2304]{1,0:T(8,128)} %collective-permute-done.1), channel_id=1, source_target_pairs={{0,28},{4,0},{8,4},{12,8},{16,12},{20,16},{24,20},{28,24},{1,29},{... | collective-permute-start | bytes 1769480 | tf_op jit(solution)/shard_map/ppermute | solution.py:32
  37.3 0.0 collective-permute-done.6
  37.3 0.0 collective-permute-start.7
  37.3 2.4 %fusion.36 = f32[64,128]{1,0:T(8,128)S(1)} fusion(f32[64,2304]{1,0:T(8,128)} %collective-permute-done.1, f32[128,4608]{1,0:T(8,128)S(1)} %copy-done), kind=kOutput, calls=%fused_computation.44 | convolution fusion | flops 226492416 | bytes 1802240 | tf_op jit(solution)/shard_map/dot_general | solution.py:8
  39.7 2.4 %constant_dynamic-update-slice_fusion.14 = (f32[16,64,128]{2,1,0:T(8,128)S(1)}, f32[1,64,128]{2,1,0:T(8,128)S(1)}) fusion(f32[16,64,128]{2,1,0:T(8,128)S(1)} %get-tuple-element.7, f32[64,128]{1,0:T(8,128)S(1)} %fusion.36, f32[64,2304]{1,0:T(8,128)} %collective-permute-done, f32[128,4608]{1,0:T(8,128)S(1)} %copy-done), kind=kOutput, calls=%fused_computation.62 | convolution fusion | flops 226508800 | bytes 1867776 | tf_op jit(solution)/shard_map/dot_general | solution.py:8
  42.2 4.4 %collective-permute-done.2 = f32[64,2304]{1,0:T(8,128)S(1)} collective-permute-done((f32[64,2304]{1,0:T(8,128)}, f32[64,2304]{1,0:T(8,128)S(1)}, u32[]{:S(2)}, u32[]{:S(2)}) %collective-permute-start.2) | collective-permute-done | bytes 589856 | tf_op jit(solution)/shard_map/ppermute | solution.py:32
  46.5 3.3 %collective-permute-start.4 = (f32[64,2304]{1,0:T(8,128)S(1)}, f32[64,2304]{1,0:T(8,128)S(1)}, u32[]{:S(2)}, u32[]{:S(2)}) collective-permute-start(f32[64,2304]{1,0:T(8,128)S(1)} %collective-permute-done.2), channel_id=1, source_target_pairs={{0,28},{4,0},{8,4},{12,8},{16,12},{20,16},{24,20},{28,24},{1,29},{... | collective-permute-start | bytes 1769480 | tf_op jit(solution)/shard_map/ppermute | solution.py:32
  49.8 0.0 collective-permute-done.12
  49.8 0.0 collective-permute-start.13
  49.8 1.3 %fusion.18 = f32[64,128]{1,0:T(8,128)S(1)} fusion(f32[64,2304]{1,0:T(8,128)S(1)} %collective-permute-done.12, f32[128,4608]{1,0:T(8,128)S(1)} %copy-done), kind=kOutput, calls=%fused_computation.26 | convolution fusion | flops 226492416 | bytes 1802240 | tf_op jit(solution)/shard_map/dot_general | solution.py:8
  51.2 8.0 %collective-permute-done.3 = f32[64,2304]{1,0:T(8,128)S(1)} collective-permute-done((f32[64,2304]{1,0:T(8,128)}, f32[64,2304]{1,0:T(8,128)S(1)}, u32[]{:S(2)}, u32[]{:S(2)}) %collective-permute-start.3) | collective-permute-done | bytes 589856 | tf_op jit(solution)/shard_map/ppermute | solution.py:32
  59.1 3.3 %collective-permute-start.5 = (f32[64,2304]{1,0:T(8,128)S(1)}, f32[64,2304]{1,0:T(8,128)S(1)}, u32[]{:S(2)}, u32[]{:S(2)}) collective-permute-start(f32[64,2304]{1,0:T(8,128)S(1)} %collective-permute-done.3), channel_id=1, source_target_pairs={{0,28},{4,0},{8,4},{12,8},{16,12},{20,16},{24,20},{28,24},{1,29},{... | collective-permute-start | bytes 1769480 | tf_op jit(solution)/shard_map/ppermute | solution.py:32
  62.5 0.0 collective-permute-done.7
  62.5 0.0 collective-permute-start.8
  62.5 1.3 %fusion.34 = f32[64,128]{1,0:T(8,128)S(1)} fusion(f32[64,2304]{1,0:T(8,128)S(1)} %collective-permute-done.3, f32[128,4608]{1,0:T(8,128)S(1)} %copy-done), kind=kOutput, calls=%fused_computation.42 | convolution fusion | flops 226492416 | bytes 1802240 | tf_op jit(solution)/shard_map/dot_general | solution.py:8
  63.8 1.4 %constant_dynamic-update-slice_fusion.13 = (f32[16,64,128]{2,1,0:T(8,128)S(1)}, f32[1,64,128]{2,1,0:T(8,128)S(1)}) fusion(f32[16,64,128]{2,1,0:T(8,128)S(1)} %get-tuple-element.9, f32[64,128]{1,0:T(8,128)S(1)} %fusion.34, f32[64,2304]{1,0:T(8,128)S(1)} %collective-permute-done.2, f32[128,4608]{1,0:T(8,128)S(1)} %copy-done), kind=kOutput, calls=%fused_computation.61 | convolution fusion | flops 226508800 | bytes 1867776 | tf_op jit(solution)/shard_map/dot_general | solution.py:8
  65.2 6.5 %collective-permute-done.4 = f32[64,2304]{1,0:T(8,128)S(1)} collective-permute-done((f32[64,2304]{1,0:T(8,128)S(1)}, f32[64,2304]{1,0:T(8,128)S(1)}, u32[]{:S(2)}, u32[]{:S(2)}) %collective-permute-start.4) | collective-permute-done | bytes 589856 | tf_op jit(solution)/shard_map/ppermute | solution.py:32
  71.7 3.4 %collective-permute-start.10 = (f32[64,2304]{1,0:T(8,128)S(1)}, f32[64,2304]{1,0:T(8,128)S(1)}, u32[]{:S(2)}, u32[]{:S(2)}) collective-permute-start(f32[64,2304]{1,0:T(8,128)S(1)} %collective-permute-done.4), channel_id=1, source_target_pairs={{0,28},{4,0},{8,4},{12,8},{16,12},{20,16},{24,20},{28,24},{1,29},{... | collective-permute-start | bytes 1769480 | tf_op jit(solution)/shard_map/ppermute | solution.py:37
  75.1 0.0 collective-permute-done.13
  75.1 1.3 %fusion.20 = f32[64,128]{1,0:T(8,128)S(1)} fusion(f32[64,2304]{1,0:T(8,128)S(1)} %collective-permute-done.13, f32[128,4608]{1,0:T(8,128)S(1)} %copy-done), kind=kOutput, calls=%fused_computation.28 | convolution fusion | flops 226492416 | bytes 1802240 | tf_op jit(solution)/shard_map/dot_general | solution.py:8
  76.4 11.0 %collective-permute-done.8 = f32[64,2304]{1,0:T(8,128)S(1)} collective-permute-done((f32[64,2304]{1,0:T(8,128)S(1)}, f32[64,2304]{1,0:T(8,128)S(1)}, u32[]{:S(2)}, u32[]{:S(2)}) %collective-permute-start.8) | collective-permute-done | bytes 589856 | tf_op jit(solution)/shard_map/ppermute | solution.py:31
  87.4 0.0 collective-permute-start.9
  87.4 0.0 collective-permute-done.5
  87.4 1.3 %fusion.32 = f32[64,128]{1,0:T(8,128)S(1)} fusion(f32[64,2304]{1,0:T(8,128)S(1)} %collective-permute-done.5, f32[128,4608]{1,0:T(8,128)S(1)} %copy-done), kind=kOutput, calls=%fused_computation.40 | convolution fusion | flops 226492416 | bytes 1802240 | tf_op jit(solution)/shard_map/dot_general | solution.py:8
  88.8 1.4 %constant_dynamic-update-slice_fusion.12 = (f32[16,64,128]{2,1,0:T(8,128)S(1)}, f32[1,64,128]{2,1,0:T(8,128)S(1)}) fusion(f32[16,64,128]{2,1,0:T(8,128)S(1)} %get-tuple-element.11, f32[64,128]{1,0:T(8,128)S(1)} %fusion.32, f32[64,2304]{1,0:T(8,128)S(1)} %collective-permute-done.4, f32[128,4608]{1,0:T(8,128)S(1)} %copy-done), kind=kOutput, calls=%fused_computation.60 | convolution fusion | flops 226508800 | bytes 1867776 | tf_op jit(solution)/shard_map/dot_general | solution.py:8
  90.1 6.8 %collective-permute-done.10 = f32[64,2304]{1,0:T(8,128)S(1)} collective-permute-done((f32[64,2304]{1,0:T(8,128)S(1)}, f32[64,2304]{1,0:T(8,128)S(1)}, u32[]{:S(2)}, u32[]{:S(2)}) %collective-permute-start.10) | collective-permute-done | bytes 589856 | tf_op jit(solution)/shard_map/ppermute | solution.py:37
  97.0 1.3 %fusion.22 = f32[64,128]{1,0:T(8,128)S(1)} fusion(f32[64,2304]{1,0:T(8,128)S(1)} %collective-permute-done.10, f32[128,4608]{1,0:T(8,128)S(1)} %copy-done), kind=kOutput, calls=%fused_computation.30 | convolution fusion | flops 226492416 | bytes 1802240 | tf_op jit(solution)/shard_map/dot_general | solution.py:8
  98.3 3.3 %collective-permute-done.9 = f32[64,2304]{1,0:T(8,128)S(1)} collective-permute-done((f32[64,2304]{1,0:T(8,128)S(1)}, f32[64,2304]{1,0:T(8,128)S(1)}, u32[]{:S(2)}, u32[]{:S(2)}) %collective-permute-start.9) | collective-permute-done | bytes 589856 | tf_op jit(solution)/shard_map/ppermute | solution.py:36
  101.6 1.4 %constant_dynamic-update-slice_fusion.11 = (f32[16,64,128]{2,1,0:T(8,128)S(1)}, f32[1,64,128]{2,1,0:T(8,128)S(1)}) fusion(f32[16,64,128]{2,1,0:T(8,128)S(1)} %get-tuple-element.13, f32[64,128]{1,0:T(8,128)S(1)} %fusion.22, f32[64,2304]{1,0:T(8,128)S(1)} %collective-permute-done.9, f32[128,4608]{1,0:T(8,128)S(1)} %copy-done), kind=kOutput, calls=%fused_computation.59 | convolution fusion | flops 226508800 | bytes 1867776 | tf_op jit(solution)/shard_map/dot_general | solution.py:8
  102.9 1.4 %constant_dynamic-update-slice_fusion.10 = (f32[16,64,128]{2,1,0:T(8,128)S(1)}, f32[1,64,128]{2,1,0:T(8,128)S(1)}) fusion(f32[16,64,128]{2,1,0:T(8,128)S(1)} %get-tuple-element.15, f32[64,128]{1,0:T(8,128)S(1)} %fusion.20, f32[64,2304]{1,0:T(8,128)S(1)} %collective-permute-done.8, f32[128,4608]{1,0:T(8,128)S(1)} %copy-done), kind=kOutput, calls=%fused_computation.58 | convolution fusion | flops 226508800 | bytes 1867776 | tf_op jit(solution)/shard_map/dot_general | solution.py:8
  104.3 1.4 %constant_dynamic-update-slice_fusion.9 = (f32[16,64,128]{2,1,0:T(8,128)S(1)}, f32[1,64,128]{2,1,0:T(8,128)S(1)}) fusion(f32[16,64,128]{2,1,0:T(8,128)S(1)} %get-tuple-element.17, f32[64,128]{1,0:T(8,128)S(1)} %fusion.18, f32[64,2304]{1,0:T(8,128)S(1)} %collective-permute-done.7, f32[128,4608]{1,0:T(8,128)S(1)} %copy-done), kind=kOutput, calls=%fused_computation.57 | convolution fusion | flops 226508800 | bytes 1867776 | tf_op jit(solution)/shard_map/dot_general | solution.py:8
  105.7 2.4 %constant_dynamic-update-slice_fusion.8 = (f32[16,64,128]{2,1,0:T(8,128)S(1)}, f32[1,64,128]{2,1,0:T(8,128)S(1)}) fusion(f32[16,64,128]{2,1,0:T(8,128)S(1)} %get-tuple-element.19, f32[64,128]{1,0:T(8,128)S(1)} %fusion.16, f32[64,2304]{1,0:T(8,128)} %collective-permute-done.6, f32[128,4608]{1,0:T(8,128)S(1)} %copy-done), kind=kOutput, calls=%fused_computation.56 | convolution fusion | flops 226508800 | bytes 1867776 | tf_op jit(solution)/shard_map/dot_general | solution.py:8
  108.2 18.5 %all_to_all.5 = f32[32,16,128]{2,1,0:T(8,128)S(1)} all-to-all(f32[32,16,128]{2,1,0:T(8,128)S(1)} %bitcast.31), channel_id=1, replica_groups=mesh['row'=8,'col'=8,'layer'=4] {'row','layer'}, dimensions={0} | all-to-all | bytes 524288 | tf_op jit(solution)/shard_map/all_to_all | solution.py:43
  126.7 0.6 reduce_sum.9
  (9 shorter events, 0.1 us)
Async XLA Ops:
  0.0 11.6 %copy-start = (f32[128,4608]{1,0:T(8,128)S(1)}, f32[128,4608]{1,0:T(8,128)}, u32[]{:S(2)}) copy-start(f32[128,4608]{1,0:T(8,128)} %param.3) | copy-start | bytes 7077892
  2.5 12.1 %copy-start.1 = (f32[64,4608]{1,0:T(8,128)S(1)}, f32[64,4608]{1,0:T(8,128)}, u32[]{:S(2)}) copy-start(f32[64,4608]{1,0:T(8,128)} %param.2) | copy-start | bytes 3538948
  2.5 18.7 %collective-permute-start = (f32[64,2304]{1,0:T(8,128)}, f32[64,2304]{1,0:T(8,128)}, u32[]{:S(2)}, u32[]{:S(2)}) collective-permute-start(f32[64,2304]{1,0:T(8,128)} %get-tuple-element.5), channel_id=1, source_target_pairs={{0,28},{4,0},{8,4},{12,8},{16,12},{20,16},{24,20},{28,24},{1,29},{... | collective-permute-start | bytes 1769480 | tf_op jit(solution)/shard_map/ppermute | solution.py:32
  8.9 15.7 %collective-permute-start.11 = (f32[64,2304]{1,0:T(8,128)}, f32[64,2304]{1,0:T(8,128)}, u32[]{:S(2)}, u32[]{:S(2)}) collective-permute-start(f32[64,2304]{1,0:T(8,128)} %get-tuple-element.5), channel_id=1, source_target_pairs={{0,4},{4,8},{8,12},{12,16},{16,20},{20,24},{24,28},{28,0},{1,5},{5... | collective-permute-start | bytes 1769480 | tf_op jit(solution)/shard_map/ppermute | solution.py:31
  8.9 24.9 %collective-permute-start.1 = (f32[64,2304]{1,0:T(8,128)}, f32[64,2304]{1,0:T(8,128)}, u32[]{:S(2)}, u32[]{:S(2)}) collective-permute-start(f32[64,2304]{1,0:T(8,128)} %get-tuple-element.6), channel_id=1, source_target_pairs={{0,28},{4,0},{8,4},{12,8},{16,12},{20,16},{24,20},{28,24},{1,29},{... | collective-permute-start | bytes 1769480 | tf_op jit(solution)/shard_map/ppermute | solution.py:32
  11.6 25.7 %collective-permute-start.6 = (f32[64,2304]{1,0:T(8,128)}, f32[64,2304]{1,0:T(8,128)}, u32[]{:S(2)}, u32[]{:S(2)}) collective-permute-start(f32[64,2304]{1,0:T(8,128)} %get-tuple-element.6), channel_id=1, source_target_pairs={{0,4},{4,8},{8,12},{12,16},{16,20},{20,24},{24,28},{28,0},{1,5},{5... | collective-permute-start | bytes 1769480 | tf_op jit(solution)/shard_map/ppermute | solution.py:31
  21.2 25.3 %collective-permute-start.2 = (f32[64,2304]{1,0:T(8,128)}, f32[64,2304]{1,0:T(8,128)S(1)}, u32[]{:S(2)}, u32[]{:S(2)}) collective-permute-start(f32[64,2304]{1,0:T(8,128)} %collective-permute-done), channel_id=1, source_target_pairs={{0,28},{4,0},{8,4},{12,8},{16,12},{20,16},{24,20},{28,24},{1,29},{... | collective-permute-start | bytes 1769480 | tf_op jit(solution)/shard_map/ppermute | solution.py:32
  24.6 25.2 %collective-permute-start.12 = (f32[64,2304]{1,0:T(8,128)}, f32[64,2304]{1,0:T(8,128)S(1)}, u32[]{:S(2)}, u32[]{:S(2)}) collective-permute-start(f32[64,2304]{1,0:T(8,128)} %collective-permute-done.11), channel_id=1, source_target_pairs={{0,4},{4,8},{8,12},{12,16},{16,20},{20,24},{24,28},{28,0},{1,5},{5... | collective-permute-start | bytes 1769480 | tf_op jit(solution)/shard_map/ppermute | solution.py:31
  33.9 25.3 %collective-permute-start.3 = (f32[64,2304]{1,0:T(8,128)}, f32[64,2304]{1,0:T(8,128)S(1)}, u32[]{:S(2)}, u32[]{:S(2)}) collective-permute-start(f32[64,2304]{1,0:T(8,128)} %collective-permute-done.1), channel_id=1, source_target_pairs={{0,28},{4,0},{8,4},{12,8},{16,12},{20,16},{24,20},{28,24},{1,29},{... | collective-permute-start | bytes 1769480 | tf_op jit(solution)/shard_map/ppermute | solution.py:32
  37.3 25.2 %collective-permute-start.7 = (f32[64,2304]{1,0:T(8,128)}, f32[64,2304]{1,0:T(8,128)S(1)}, u32[]{:S(2)}, u32[]{:S(2)}) collective-permute-start(f32[64,2304]{1,0:T(8,128)} %collective-permute-done.6), channel_id=1, source_target_pairs={{0,4},{4,8},{8,12},{12,16},{16,20},{20,24},{24,28},{28,0},{1,5},{5... | collective-permute-start | bytes 1769480 | tf_op jit(solution)/shard_map/ppermute | solution.py:31
  46.5 25.2 %collective-permute-start.4 = (f32[64,2304]{1,0:T(8,128)S(1)}, f32[64,2304]{1,0:T(8,128)S(1)}, u32[]{:S(2)}, u32[]{:S(2)}) collective-permute-start(f32[64,2304]{1,0:T(8,128)S(1)} %collective-permute-done.2), channel_id=1, source_target_pairs={{0,28},{4,0},{8,4},{12,8},{16,12},{20,16},{24,20},{28,24},{1,29},{... | collective-permute-start | bytes 1769480 | tf_op jit(solution)/shard_map/ppermute | solution.py:32
  49.8 25.3 %collective-permute-start.13 = (f32[64,2304]{1,0:T(8,128)S(1)}, f32[64,2304]{1,0:T(8,128)S(1)}, u32[]{:S(2)}, u32[]{:S(2)}) collective-permute-start(f32[64,2304]{1,0:T(8,128)S(1)} %collective-permute-done.12), channel_id=1, source_target_pairs={{0,4},{4,8},{8,12},{12,16},{16,20},{20,24},{24,28},{28,0},{1,5},{5... | collective-permute-start | bytes 1769480 | tf_op jit(solution)/shard_map/ppermute | solution.py:31
  59.1 28.3 %collective-permute-start.5 = (f32[64,2304]{1,0:T(8,128)S(1)}, f32[64,2304]{1,0:T(8,128)S(1)}, u32[]{:S(2)}, u32[]{:S(2)}) collective-permute-start(f32[64,2304]{1,0:T(8,128)S(1)} %collective-permute-done.3), channel_id=1, source_target_pairs={{0,28},{4,0},{8,4},{12,8},{16,12},{20,16},{24,20},{28,24},{1,29},{... | collective-permute-start | bytes 1769480 | tf_op jit(solution)/shard_map/ppermute | solution.py:32
  62.5 25.0 %collective-permute-start.8 = (f32[64,2304]{1,0:T(8,128)S(1)}, f32[64,2304]{1,0:T(8,128)S(1)}, u32[]{:S(2)}, u32[]{:S(2)}) collective-permute-start(f32[64,2304]{1,0:T(8,128)S(1)} %collective-permute-done.7), channel_id=1, source_target_pairs={{0,4},{4,8},{8,12},{12,16},{16,20},{20,24},{24,28},{28,0},{1,5},{5... | collective-permute-start | bytes 1769480 | tf_op jit(solution)/shard_map/ppermute | solution.py:31
  71.7 25.3 %collective-permute-start.10 = (f32[64,2304]{1,0:T(8,128)S(1)}, f32[64,2304]{1,0:T(8,128)S(1)}, u32[]{:S(2)}, u32[]{:S(2)}) collective-permute-start(f32[64,2304]{1,0:T(8,128)S(1)} %collective-permute-done.4), channel_id=1, source_target_pairs={{0,28},{4,0},{8,4},{12,8},{16,12},{20,16},{24,20},{28,24},{1,29},{... | collective-permute-start | bytes 1769480 | tf_op jit(solution)/shard_map/ppermute | solution.py:37
  87.4 14.2 %collective-permute-start.9 = (f32[64,2304]{1,0:T(8,128)S(1)}, f32[64,2304]{1,0:T(8,128)S(1)}, u32[]{:S(2)}, u32[]{:S(2)}) collective-permute-start(f32[64,2304]{1,0:T(8,128)S(1)} %collective-permute-done.8), channel_id=1, source_target_pairs={{0,4},{4,8},{8,12},{12,16},{16,20},{20,24},{24,28},{28,0},{1,5},{5... | collective-permute-start | bytes 1769480 | tf_op jit(solution)/shard_map/ppermute | solution.py:36

commit v3 on v1

v3 whole, which is shorter than its diff:
```python
import jax
import jax.numpy as jnp
from jax import lax
from jax.experimental import pallas as pl
from jax.experimental.pallas import tpu as pltpu
from jax.sharding import PartitionSpec as P


def multiply(blocks, places, b, before):
    count = len(blocks)
    height = blocks[0].shape[0]
    levels = before.shape[0]

    def kernel(*refs):
        b_ref, old, out = refs[count:]
        level = lax.axis_index("col")
        out[...] = old[...]
        left = jnp.concatenate([ref[...] for ref in refs[:count]], axis=0)
        product = 0.5 * lax.dot_general(
            left,
            b_ref[...],
            (((1,), (1,)), ((), ())),
            precision=lax.Precision.HIGHEST,
            preferred_element_type=jnp.float32,
        )
        for i, (distance, half) in enumerate(places):
            index = lax.rem(level + distance % levels, levels)
            out[index, half * height : (half + 1) * height] = product[i * height : (i + 1) * height]

    return pl.pallas_call(
        kernel,
        out_shape=jax.ShapeDtypeStruct(before.shape, jnp.float32),
        in_specs=[pl.BlockSpec(memory_space=pltpu.VMEM)] * (count + 2),
        out_specs=pl.BlockSpec(memory_space=pltpu.VMEM),
        input_output_aliases={count + 1: 0},
        compiler_params=pltpu.CompilerParams(vmem_limit_bytes=32 * 1024 * 1024),
    )(*blocks, b, before)


def on_device(amplitudes, integrals):
    levels = lax.axis_size("col")
    rows, columns = amplitudes.shape[0], integrals.shape[0]
    height = rows // 2
    hop_up = [(i, (i + 1) % levels) for i in range(levels)]
    hop_down = [(i, (i - 1) % levels) for i in range(levels)]

    first = amplitudes[:height]
    later, first = lax.optimization_barrier((amplitudes, first))
    second = later[height:]

    product = jnp.zeros((levels, rows, columns), jnp.float32)
    up, down = [first, second], [first, second]
    product = multiply([first, second], [(0, 0), (0, 1)], integrals, product)
    for hop in range(1, levels // 2):
        for i in (0, 1):
            up[i] = lax.ppermute(up[i], "col", hop_up)
            down[1 - i] = lax.ppermute(down[1 - i], "col", hop_down)
            product = multiply([up[i], down[1 - i]], [(-hop, i), (hop, 1 - i)], integrals, product)
    up_half = lax.ppermute(up[0], "col", hop_up)
    down_half = lax.ppermute(down[1], "col", hop_down)
    far = levels // 2
    product = multiply([up_half, down_half], [(far, 0), (far, 1)], integrals, product)

    shares = lax.axis_size(("row", "layer"))
    blocks = product.reshape(shares, -1, columns)
    return lax.all_to_all(blocks, ("row", "layer"), 0, 0).sum(0)


def solution(mesh):
    in_specs = (P("col", ("row", "layer")), P("col", ("row", "layer")))
    out_specs = P(("row", "layer"), "col")
    return jax.shard_map(
        on_device, mesh=mesh, in_specs=in_specs, out_specs=out_specs, check_vma=False
    )
```

time: 151 us -> 121 us (0.80)
  waiting for transfers between devices: 110 us -> 54.5 us
  starting transfers between devices: 0.01 us -> 24.8 us
  Pallas kernels: 0 us -> 20.6 us
  between operations: 13.4 us -> 0.05 us
  matrix products: 10 us -> 0 us
  local copies, waits for them, and re-layouts: 0.01 us -> 2.38 us
    all_gather x1 -> x0, waiting for transfers between devices: 110 us -> none  [on_device(): lax.all_gather(amplitudes, 'col', axis=0, tiled=True)]
    ppermute x0 -> x14, waiting for transfers between devices: none -> 54.5 us  [the longest x6 24.6 us: on_device(): up[i] = lax.ppermute(up[i], 'col', hop_up)]
    ppermute x0 -> x14, starting transfers between devices: none -> 24.8 us  [the longest x6 21.4 us: on_device(): down[1 - i] = lax.ppermute(down[1 - i], 'col', hop_down)]
    pallas_call x0 -> x8, Pallas kernels: none -> 20.6 us  [multiply(): pl.pallas_call(kernel, out_shape=jax.ShapeDtypeStruct(before.shape, jnp.f...]
    dot_general x1 -> x0, matrix products: 10 us -> none  [contract_last(): lax.dot_general(left, right, (((1,), (1,)), ((), ())), precision=lax.Prec...]
    slice x0 -> x2, local copies, waits for them, and re-layouts: none -> 2.36 us  [the longest x1 1.25 us: on_device(): first = amplitudes[:height]]
  transfers between devices with their start and end apart: 1 -> 14, of which waited for: 1 -> 7; matrix products, arithmetic and copies ran while one was open for 0% -> 0% of each run, Pallas kernels for 0% -> 15%
where the time goes in v3:
time: 121 us
  waiting for transfers between devices  54.5 us (45%)
  starting transfers between devices  24.8 us (20%)
  Pallas kernels  20.6 us (17%)
  blocking collectives  17.6 us (15%)
  local copies, waits for them, and re-layouts  2.38 us (2%)
    ppermute x6, waiting for transfers between devices, on_device(): up[i] = lax.ppermute(up[i], 'col', hop_up)  24.6 us
    ppermute x6, waiting for transfers between devices, on_device(): down[1 - i] = lax.ppermute(down[1 - i], 'col', hop_down)  23 us
    ppermute x6, starting transfers between devices, on_device(): down[1 - i] = lax.ppermute(down[1 - i], 'col', hop_down)  21.4 us
    pallas_call x8, Pallas kernels, multiply(): pl.pallas_call(kernel, out_shape=jax.ShapeDtypeStruct(before.shape, jnp.f...  20.6 us
    all_to_all x1, blocking collectives, on_device(): return lax.all_to_all(blocks, ('row', 'layer'), 0, 0).sum(0)  17.6 us
    ppermute x1, waiting for transfers between devices, on_device(): down_half = lax.ppermute(down[1], 'col', hop_down)  3.74 us
    ppermute x1, starting transfers between devices, on_device(): down_half = lax.ppermute(down[1], 'col', hop_down)  3.41 us
    ppermute x1, waiting for transfers between devices, on_device(): up_half = lax.ppermute(up[0], 'col', hop_up)  3.09 us
  transfers between devices with their start and end apart: 14, of which 7 were waited for; matrix products, arithmetic and copies ran while one was open for 0% of the time, Pallas kernels for 15%

profile of v3, /device:TPU:1, one launch (start us, length us, event | category | flops | bytes accessed | tf_op | source)
XLA Modules:
  0.0 120.5 jit_solution(17309297516632083633)
XLA Ops:
  0.0 0.0 copy-start
  0.0 1.3 %slice.6.refs_0_ = f32[32,4608]{1,0:T(8,128)S(1)} slice(f32[64,4608]{1,0:T(8,128)} %param.2), slice={[0:32], [0:4608]} | slice | bytes 1179648 | tf_op jit(solution)/shard_map/slice | solution.py:47
  1.3 1.1 slice.7.refs_1_
  2.4 6.5 %collective-permute-start.4 = (f32[32,4608]{1,0:T(8,128)S(1)}, f32[32,4608]{1,0:T(8,128)S(1)}, u32[]{:S(2)}, u32[]{:S(2)}) collective-permute-start(f32[32,4608]{1,0:T(8,128)S(1)} %slice.7.refs_1_), channel_id=1, source_target_pairs={{0,28},{4,0},{8,4},{12,8},{16,12},{20,16},{24,20},{28,24},{1,29},{... | collective-permute-start | bytes 1769480 | tf_op jit(solution)/shard_map/ppermute | solution.py:57
  8.9 0.0 collective-permute-start
  8.9 0.0 collective-permute-start.8
  8.9 2.7 %collective-permute-start.11 = (f32[32,4608]{1,0:T(8,128)S(1)}, f32[32,4608]{1,0:T(8,128)S(1)}, u32[]{:S(2)}, u32[]{:S(2)}) collective-permute-start(f32[32,4608]{1,0:T(8,128)S(1)} %slice.6.refs_0_), channel_id=1, source_target_pairs={{0,28},{4,0},{8,4},{12,8},{16,12},{20,16},{24,20},{28,24},{1,29},{... | collective-permute-start | bytes 1769480 | tf_op jit(solution)/shard_map/ppermute | solution.py:57
  11.6 9.3 %collective-permute-done.4.refs_1_ = f32[32,4608]{1,0:T(8,128)S(1)} collective-permute-done((f32[32,4608]{1,0:T(8,128)S(1)}, f32[32,4608]{1,0:T(8,128)S(1)}, u32[]{:S(2)}, u32[]{:S(2)}) %collective-permute-start.4) | collective-permute-done | bytes 589856 | tf_op jit(solution)/shard_map/ppermute | solution.py:57
  20.8 3.4 %collective-permute-start.5 = (f32[32,4608]{1,0:T(8,128)S(1)}, f32[32,4608]{1,0:T(8,128)S(1)}, u32[]{:S(2)}, u32[]{:S(2)}) collective-permute-start(f32[32,4608]{1,0:T(8,128)S(1)} %collective-permute-done.4.refs_1_), channel_id=1, source_target_pairs={{0,28},{4,0},{8,4},{12,8},{16,12},{20,16},{24,20},{28,24},{1,29},{... | collective-permute-start | bytes 1769480 | tf_op jit(solution)/shard_map/ppermute | solution.py:57
  24.3 0.0 collective-permute-done.refs_0_
  24.3 0.0 collective-permute-start.1
  24.3 12.3 %collective-permute-done.8.refs_0_ = f32[32,4608]{1,0:T(8,128)S(1)} collective-permute-done((f32[32,4608]{1,0:T(8,128)S(1)}, f32[32,4608]{1,0:T(8,128)S(1)}, u32[]{:S(2)}, u32[]{:S(2)}) %collective-permute-start.8) | collective-permute-done | bytes 589856 | tf_op jit(solution)/shard_map/ppermute | solution.py:56
  36.6 0.0 collective-permute-start.9
  36.6 0.0 collective-permute-done.11.refs_1_
  36.6 2.7 %collective-permute-start.12 = (f32[32,4608]{1,0:T(8,128)S(1)}, f32[32,4608]{1,0:T(8,128)S(1)}, u32[]{:S(2)}, u32[]{:S(2)}) collective-permute-start(f32[32,4608]{1,0:T(8,128)S(1)} %collective-permute-done.11.refs_1_), channel_id=1, source_target_pairs={{0,28},{4,0},{8,4},{12,8},{16,12},{20,16},{24,20},{28,24},{1,29},{... | collective-permute-start | bytes 1769480 | tf_op jit(solution)/shard_map/ppermute | solution.py:57
  39.3 6.9 %collective-permute-done.5.refs_1_ = f32[32,4608]{1,0:T(8,128)S(1)} collective-permute-done((f32[32,4608]{1,0:T(8,128)S(1)}, f32[32,4608]{1,0:T(8,128)S(1)}, u32[]{:S(2)}, u32[]{:S(2)}) %collective-permute-start.5) | collective-permute-done | bytes 589856 | tf_op jit(solution)/shard_map/ppermute | solution.py:57
  46.1 3.4 %collective-permute-start.6 = (f32[32,4608]{1,0:T(8,128)S(1)}, f32[32,4608]{1,0:T(8,128)S(1)}, u32[]{:S(2)}, u32[]{:S(2)}) collective-permute-start(f32[32,4608]{1,0:T(8,128)S(1)} %collective-permute-done.5.refs_1_), channel_id=1, source_target_pairs={{0,28},{4,0},{8,4},{12,8},{16,12},{20,16},{24,20},{28,24},{1,29},{... | collective-permute-start | bytes 1769480 | tf_op jit(solution)/shard_map/ppermute | solution.py:57
  49.5 0.0 collective-permute-done.1.refs_0_
  49.5 0.0 collective-permute-start.2
  49.5 12.3 %collective-permute-done.9.refs_0_ = f32[32,4608]{1,0:T(8,128)S(1)} collective-permute-done((f32[32,4608]{1,0:T(8,128)S(1)}, f32[32,4608]{1,0:T(8,128)S(1)}, u32[]{:S(2)}, u32[]{:S(2)}) %collective-permute-start.9) | collective-permute-done | bytes 589856 | tf_op jit(solution)/shard_map/ppermute | solution.py:56
  61.9 0.0 collective-permute-start.10
  61.9 0.0 collective-permute-done.12.refs_1_
  61.9 2.7 %collective-permute-start.13 = (f32[32,4608]{1,0:T(8,128)S(1)}, f32[32,4608]{1,0:T(8,128)S(1)}, u32[]{:S(2)}, u32[]{:S(2)}) collective-permute-start(f32[32,4608]{1,0:T(8,128)S(1)} %collective-permute-done.12.refs_1_), channel_id=1, source_target_pairs={{0,28},{4,0},{8,4},{12,8},{16,12},{20,16},{24,20},{28,24},{1,29},{... | collective-permute-start | bytes 1769480 | tf_op jit(solution)/shard_map/ppermute | solution.py:57
  64.5 6.9 %collective-permute-done.6.refs_1_ = f32[32,4608]{1,0:T(8,128)S(1)} collective-permute-done((f32[32,4608]{1,0:T(8,128)S(1)}, f32[32,4608]{1,0:T(8,128)S(1)}, u32[]{:S(2)}, u32[]{:S(2)}) %collective-permute-start.6) | collective-permute-done | bytes 589856 | tf_op jit(solution)/shard_map/ppermute | solution.py:57
  71.4 3.4 %collective-permute-start.7 = (f32[32,4608]{1,0:T(8,128)S(1)}, f32[32,4608]{1,0:T(8,128)S(1)}, u32[]{:S(2)}, u32[]{:S(2)}) collective-permute-start(f32[32,4608]{1,0:T(8,128)S(1)} %collective-permute-done.6.refs_1_), channel_id=1, source_target_pairs={{0,28},{4,0},{8,4},{12,8},{16,12},{20,16},{24,20},{28,24},{1,29},{... | collective-permute-start | bytes 1769480 | tf_op jit(solution)/shard_map/ppermute | solution.py:60
  74.8 0.0 collective-permute-done.2.refs_0_
  74.8 0.0 collective-permute-start.3
  74.8 0.0 copy-done
  74.9 2.6 %shard_map.28.refs_3_ = f32[8,64,128]{2,1,0:T(8,128)S(1)} custom-call(f32[32,4608]{1,0:T(8,128)S(1)} %slice.6.refs_0_, f32[32,4608]{1,0:T(8,128)S(1)} %slice.7.refs_1_, f32[128,4608]{1,0:T(8,128)S(1)} %copy-done, f32[8,64,128]{2,1,0:T(8,128)S(1)} %broadcast_in_dim.3.refs_3_), custom_call_target="tpu_custom_call", output_to_operand_aliasing={{}: (3, {})} | custom-call | tf_op jit(solution)/shard_map/pallas_call | solution.py:30
  77.4 2.6 %shard_map.29.refs_3_ = f32[8,64,128]{2,1,0:T(8,128)S(1)} custom-call(f32[32,4608]{1,0:T(8,128)S(1)} %collective-permute-done.refs_0_, f32[32,4608]{1,0:T(8,128)S(1)} %collective-permute-done.4.refs_1_, f32[128,4608]{1,0:T(8,128)S(1)} %copy-done, f32[8,64,128]{2,1,0:T(8,128)S(1)} %shard_map.28.refs_3_), custom_call_target="tpu_custom_call", output_to_operand_aliasing={{}: (3, {})} | custom-call | tf_op jit(solution)/shard_map/pallas_call | solution.py:30
  80.0 2.5 %shard_map.30.refs_3_ = f32[8,64,128]{2,1,0:T(8,128)S(1)} custom-call(f32[32,4608]{1,0:T(8,128)S(1)} %collective-permute-done.8.refs_0_, f32[32,4608]{1,0:T(8,128)S(1)} %collective-permute-done.11.refs_1_, f32[128,4608]{1,0:T(8,128)S(1)} %copy-done, f32[8,64,128]{2,1,0:T(8,128)S(1)} %shard_map.29.refs_3_), custom_call_target="tpu_custom_call", output_to_operand_aliasing={{}: (3, {})} | custom-call | tf_op jit(solution)/shard_map/pallas_call | solution.py:30
  82.5 2.6 %shard_map.31.refs_3_ = f32[8,64,128]{2,1,0:T(8,128)S(1)} custom-call(f32[32,4608]{1,0:T(8,128)S(1)} %collective-permute-done.1.refs_0_, f32[32,4608]{1,0:T(8,128)S(1)} %collective-permute-done.5.refs_1_, f32[128,4608]{1,0:T(8,128)S(1)} %copy-done, f32[8,64,128]{2,1,0:T(8,128)S(1)} %shard_map.30.refs_3_), custom_call_target="tpu_custom_call", output_to_operand_aliasing={{}: (3, {})} | custom-call | tf_op jit(solution)/shard_map/pallas_call | solution.py:30
  85.1 2.6 %shard_map.32.refs_3_ = f32[8,64,128]{2,1,0:T(8,128)S(1)} custom-call(f32[32,4608]{1,0:T(8,128)S(1)} %collective-permute-done.9.refs_0_, f32[32,4608]{1,0:T(8,128)S(1)} %collective-permute-done.12.refs_1_, f32[128,4608]{1,0:T(8,128)S(1)} %copy-done, f32[8,64,128]{2,1,0:T(8,128)S(1)} %shard_map.31.refs_3_), custom_call_target="tpu_custom_call", output_to_operand_aliasing={{}: (3, {})} | custom-call | tf_op jit(solution)/shard_map/pallas_call | solution.py:30
  87.6 2.5 %shard_map.33.refs_3_ = f32[8,64,128]{2,1,0:T(8,128)S(1)} custom-call(f32[32,4608]{1,0:T(8,128)S(1)} %collective-permute-done.2.refs_0_, f32[32,4608]{1,0:T(8,128)S(1)} %collective-permute-done.6.refs_1_, f32[128,4608]{1,0:T(8,128)S(1)} %copy-done, f32[8,64,128]{2,1,0:T(8,128)S(1)} %shard_map.32.refs_3_), custom_call_target="tpu_custom_call", output_to_operand_aliasing={{}: (3, {})} | custom-call | tf_op jit(solution)/shard_map/pallas_call | solution.py:30
  90.2 0.0 collective-permute-done.10.refs_0_
  90.2 0.0 collective-permute-done.13.refs_1_
  90.2 2.8 %shard_map.34.refs_3_ = f32[8,64,128]{2,1,0:T(8,128)S(1)} custom-call(f32[32,4608]{1,0:T(8,128)S(1)} %collective-permute-done.10.refs_0_, f32[32,4608]{1,0:T(8,128)S(1)} %collective-permute-done.13.refs_1_, f32[128,4608]{1,0:T(8,128)S(1)} %copy-done, f32[8,64,128]{2,1,0:T(8,128)S(1)} %shard_map.33.refs_3_), custom_call_target="tpu_custom_call", output_to_operand_aliasing={{}: (3, {})} | custom-call | tf_op jit(solution)/shard_map/pallas_call | solution.py:30
  93.0 3.7 %collective-permute-done.7.refs_1_ = f32[32,4608]{1,0:T(8,128)S(1)} collective-permute-done((f32[32,4608]{1,0:T(8,128)S(1)}, f32[32,4608]{1,0:T(8,128)S(1)}, u32[]{:S(2)}, u32[]{:S(2)}) %collective-permute-start.7) | collective-permute-done | bytes 589856 | tf_op jit(solution)/shard_map/ppermute | solution.py:60
  96.7 3.1 %collective-permute-done.3.refs_0_ = f32[32,4608]{1,0:T(8,128)S(1)} collective-permute-done((f32[32,4608]{1,0:T(8,128)S(1)}, f32[32,4608]{1,0:T(8,128)S(1)}, u32[]{:S(2)}, u32[]{:S(2)}) %collective-permute-start.3) | collective-permute-done | bytes 589856 | tf_op jit(solution)/shard_map/ppermute | solution.py:59
  99.8 2.6 %shard_map.35 = f32[8,64,128]{2,1,0:T(8,128)S(1)} custom-call(f32[32,4608]{1,0:T(8,128)S(1)} %collective-permute-done.3.refs_0_, f32[32,4608]{1,0:T(8,128)S(1)} %collective-permute-done.7.refs_1_, f32[128,4608]{1,0:T(8,128)S(1)} %copy-done, f32[8,64,128]{2,1,0:T(8,128)S(1)} %shard_map.34.refs_3_), custom_call_target="tpu_custom_call", output_to_operand_aliasing={{}: (3, {})} | custom-call | tf_op jit(solution)/shard_map/pallas_call | solution.py:30
  102.3 17.6 %all_to_all.5 = f32[32,16,128]{2,1,0:T(8,128)S(1)} all-to-all(f32[32,16,128]{2,1,0:T(8,128)S(1)} %bitcast.1), channel_id=1, replica_groups=mesh['row'=8,'col'=8,'layer'=4] {'row','layer'}, dimensions={0} | all-to-all | bytes 524288 | tf_op jit(solution)/shard_map/all_to_all | solution.py:66
  119.9 0.6 reduce_sum.9
  (1 shorter events, 0.0 us)
Async XLA Ops:
  0.0 74.8 %copy-start = (f32[128,4608]{1,0:T(8,128)S(1)}, f32[128,4608]{1,0:T(8,128)}, u32[]{:S(2)}) copy-start(f32[128,4608]{1,0:T(8,128)} %refs_2_.15) | copy-start | bytes 7077892
  2.4 18.5 %collective-permute-start.4 = (f32[32,4608]{1,0:T(8,128)S(1)}, f32[32,4608]{1,0:T(8,128)S(1)}, u32[]{:S(2)}, u32[]{:S(2)}) collective-permute-start(f32[32,4608]{1,0:T(8,128)S(1)} %slice.7.refs_1_), channel_id=1, source_target_pairs={{0,28},{4,0},{8,4},{12,8},{16,12},{20,16},{24,20},{28,24},{1,29},{... | collective-permute-start | bytes 1769480 | tf_op jit(solution)/shard_map/ppermute | solution.py:57
  8.9 15.4 %collective-permute-start = (f32[32,4608]{1,0:T(8,128)S(1)}, f32[32,4608]{1,0:T(8,128)S(1)}, u32[]{:S(2)}, u32[]{:S(2)}) collective-permute-start(f32[32,4608]{1,0:T(8,128)S(1)} %slice.6.refs_0_), channel_id=1, source_target_pairs={{0,4},{4,8},{8,12},{12,16},{16,20},{20,24},{24,28},{28,0},{1,5},{5... | collective-permute-start | bytes 1769480 | tf_op jit(solution)/shard_map/ppermute | solution.py:56
  8.9 27.7 %collective-permute-start.8 = (f32[32,4608]{1,0:T(8,128)S(1)}, f32[32,4608]{1,0:T(8,128)S(1)}, u32[]{:S(2)}, u32[]{:S(2)}) collective-permute-start(f32[32,4608]{1,0:T(8,128)S(1)} %slice.7.refs_1_), channel_id=1, source_target_pairs={{0,4},{4,8},{8,12},{12,16},{16,20},{20,24},{24,28},{28,0},{1,5},{5... | collective-permute-start | bytes 1769480 | tf_op jit(solution)/shard_map/ppermute | solution.py:56
  8.9 27.7 %collective-permute-start.11 = (f32[32,4608]{1,0:T(8,128)S(1)}, f32[32,4608]{1,0:T(8,128)S(1)}, u32[]{:S(2)}, u32[]{:S(2)}) collective-permute-start(f32[32,4608]{1,0:T(8,128)S(1)} %slice.6.refs_0_), channel_id=1, source_target_pairs={{0,28},{4,0},{8,4},{12,8},{16,12},{20,16},{24,20},{28,24},{1,29},{... | collective-permute-start | bytes 1769480 | tf_op jit(solution)/shard_map/ppermute | solution.py:57
  20.8 25.3 %collective-permute-start.5 = (f32[32,4608]{1,0:T(8,128)S(1)}, f32[32,4608]{1,0:T(8,128)S(1)}, u32[]{:S(2)}, u32[]{:S(2)}) collective-permute-start(f32[32,4608]{1,0:T(8,128)S(1)} %collective-permute-done.4.refs_1_), channel_id=1, source_target_pairs={{0,28},{4,0},{8,4},{12,8},{16,12},{20,16},{24,20},{28,24},{1,29},{... | collective-permute-start | bytes 1769480 | tf_op jit(solution)/shard_map/ppermute | solution.py:57
  24.3 25.3 %collective-permute-start.1 = (f32[32,4608]{1,0:T(8,128)S(1)}, f32[32,4608]{1,0:T(8,128)S(1)}, u32[]{:S(2)}, u32[]{:S(2)}) collective-permute-start(f32[32,4608]{1,0:T(8,128)S(1)} %collective-permute-done.refs_0_), channel_id=1, source_target_pairs={{0,4},{4,8},{8,12},{12,16},{16,20},{20,24},{24,28},{28,0},{1,5},{5... | collective-permute-start | bytes 1769480 | tf_op jit(solution)/shard_map/ppermute | solution.py:56
  36.6 25.3 %collective-permute-start.9 = (f32[32,4608]{1,0:T(8,128)S(1)}, f32[32,4608]{1,0:T(8,128)S(1)}, u32[]{:S(2)}, u32[]{:S(2)}) collective-permute-start(f32[32,4608]{1,0:T(8,128)S(1)} %collective-permute-done.8.refs_0_), channel_id=1, source_target_pairs={{0,4},{4,8},{8,12},{12,16},{16,20},{20,24},{24,28},{28,0},{1,5},{5... | collective-permute-start | bytes 1769480 | tf_op jit(solution)/shard_map/ppermute | solution.py:56
  36.6 25.3 %collective-permute-start.12 = (f32[32,4608]{1,0:T(8,128)S(1)}, f32[32,4608]{1,0:T(8,128)S(1)}, u32[]{:S(2)}, u32[]{:S(2)}) collective-permute-start(f32[32,4608]{1,0:T(8,128)S(1)} %collective-permute-done.11.refs_1_), channel_id=1, source_target_pairs={{0,28},{4,0},{8,4},{12,8},{16,12},{20,16},{24,20},{28,24},{1,29},{... | collective-permute-start | bytes 1769480 | tf_op jit(solution)/shard_map/ppermute | solution.py:57
  46.1 25.3 %collective-permute-start.6 = (f32[32,4608]{1,0:T(8,128)S(1)}, f32[32,4608]{1,0:T(8,128)S(1)}, u32[]{:S(2)}, u32[]{:S(2)}) collective-permute-start(f32[32,4608]{1,0:T(8,128)S(1)} %collective-permute-done.5.refs_1_), channel_id=1, source_target_pairs={{0,28},{4,0},{8,4},{12,8},{16,12},{20,16},{24,20},{28,24},{1,29},{... | collective-permute-start | bytes 1769480 | tf_op jit(solution)/shard_map/ppermute | solution.py:57
  49.5 25.3 %collective-permute-start.2 = (f32[32,4608]{1,0:T(8,128)S(1)}, f32[32,4608]{1,0:T(8,128)S(1)}, u32[]{:S(2)}, u32[]{:S(2)}) collective-permute-start(f32[32,4608]{1,0:T(8,128)S(1)} %collective-permute-done.1.refs_0_), channel_id=1, source_target_pairs={{0,4},{4,8},{8,12},{12,16},{16,20},{20,24},{24,28},{28,0},{1,5},{5... | collective-permute-start | bytes 1769480 | tf_op jit(solution)/shard_map/ppermute | solution.py:56
  61.9 28.3 %collective-permute-start.10 = (f32[32,4608]{1,0:T(8,128)S(1)}, f32[32,4608]{1,0:T(8,128)S(1)}, u32[]{:S(2)}, u32[]{:S(2)}) collective-permute-start(f32[32,4608]{1,0:T(8,128)S(1)} %collective-permute-done.9.refs_0_), channel_id=1, source_target_pairs={{0,4},{4,8},{8,12},{12,16},{16,20},{20,24},{24,28},{28,0},{1,5},{5... | collective-permute-start | bytes 1769480 | tf_op jit(solution)/shard_map/ppermute | solution.py:56
  61.9 28.3 %collective-permute-start.13 = (f32[32,4608]{1,0:T(8,128)S(1)}, f32[32,4608]{1,0:T(8,128)S(1)}, u32[]{:S(2)}, u32[]{:S(2)}) collective-permute-start(f32[32,4608]{1,0:T(8,128)S(1)} %collective-permute-done.12.refs_1_), channel_id=1, source_target_pairs={{0,28},{4,0},{8,4},{12,8},{16,12},{20,16},{24,20},{28,24},{1,29},{... | collective-permute-start | bytes 1769480 | tf_op jit(solution)/shard_map/ppermute | solution.py:57
  71.4 25.3 %collective-permute-start.7 = (f32[32,4608]{1,0:T(8,128)S(1)}, f32[32,4608]{1,0:T(8,128)S(1)}, u32[]{:S(2)}, u32[]{:S(2)}) collective-permute-start(f32[32,4608]{1,0:T(8,128)S(1)} %collective-permute-done.6.refs_1_), channel_id=1, source_target_pairs={{0,28},{4,0},{8,4},{12,8},{16,12},{20,16},{24,20},{28,24},{1,29},{... | collective-permute-start | bytes 1769480 | tf_op jit(solution)/shard_map/ppermute | solution.py:60
  74.8 25.0 %collective-permute-start.3 = (f32[32,4608]{1,0:T(8,128)S(1)}, f32[32,4608]{1,0:T(8,128)S(1)}, u32[]{:S(2)}, u32[]{:S(2)}) collective-permute-start(f32[32,4608]{1,0:T(8,128)S(1)} %collective-permute-done.2.refs_0_), channel_id=1, source_target_pairs={{0,4},{4,8},{8,12},{12,16},{16,20},{20,24},{24,28},{28,0},{1,5},{5... | collective-permute-start | bytes 1769480 | tf_op jit(solution)/shard_map/ppermute | solution.py:59

commit v4 on v3

--- a/solution.py
+++ b/solution.py
@@ -4,6 +4,18 @@
 from jax.experimental import pallas as pl
 from jax.experimental.pallas import tpu as pltpu
 from jax.sharding import PartitionSpec as P
+
+def transposed(array):
+    def kernel(src, out):
+        out[...] = src[...].T
+
+    return pl.pallas_call(
+        kernel,
+        out_shape=jax.ShapeDtypeStruct(array.shape[::-1], array.dtype),
+        in_specs=[pl.BlockSpec(memory_space=pltpu.VMEM)],
+        out_specs=pl.BlockSpec(memory_space=pltpu.VMEM),
+        compiler_params=pltpu.CompilerParams(vmem_limit_bytes=32 * 1024 * 1024),
+    )(array)
 
 
 def multiply(blocks, places, b, before):
@@ -16,10 +28,9 @@
         level = lax.axis_index("col")
         out[...] = old[...]
         left = jnp.concatenate([ref[...] for ref in refs[:count]], axis=0)
-        product = 0.5 * lax.dot_general(
+        product = 0.5 * jnp.dot(
             left,
             b_ref[...],
-            (((1,), (1,)), ((), ())),
             precision=lax.Precision.HIGHEST,
             preferred_element_type=jnp.float32,
         )
@@ -40,26 +51,25 @@
 def on_device(amplitudes, integrals):
     levels = lax.axis_size("col")
     rows, columns = amplitudes.shape[0], integrals.shape[0]
-    height = rows // 2
     hop_up = [(i, (i + 1) % levels) for i in range(levels)]
     hop_down = [(i, (i - 1) % levels) for i in range(levels)]
 
-    first = amplitudes[:height]
-    later, first = lax.optimization_barrier((amplitudes, first))
-    second = later[height:]
+    height = rows // 2
+    first, second = lax.optimization_barrier((amplitudes[:height], amplitudes[height:]))
+    b = transposed(integrals)
 
     product = jnp.zeros((levels, rows, columns), jnp.float32)
     up, down = [first, second], [first, second]
-    product = multiply([first, second], [(0, 0), (0, 1)], integrals, product)
+    product = multiply([first, second], [(0, 0), (0, 1)], b, product)
     for hop in range(1, levels // 2):
         for i in (0, 1):
             up[i] = lax.ppermute(up[i], "col", hop_up)
             down[1 - i] = lax.ppermute(down[1 - i], "col", hop_down)
-            product = multiply([up[i], down[1 - i]], [(-hop, i), (hop, 1 - i)], integrals, product)
+            product = multiply([up[i], down[1 - i]], [(-hop, i), (hop, 1 - i)], b, product)
     up_half = lax.ppermute(up[0], "col", hop_up)
     down_half = lax.ppermute(down[1], "col", hop_down)
     far = levels // 2
-    product = multiply([up_half, down_half], [(far, 0), (far, 1)], integrals, product)
+    product = multiply([up_half, down_half], [(far, 0), (far, 1)], b, product)
 
     shares = lax.axis_size(("row", "layer"))
     blocks = product.reshape(shares, -1, columns)

time: 121 us -> 116 us (0.959)
  Pallas kernels: 20.6 us -> 11 us
  waiting for transfers between devices: 54.5 us -> 62.9 us
  starting transfers between devices: 24.8 us -> 22.6 us
    ppermute x6, waiting for transfers between devices: 24.6 us -> 51.6 us  [on_device(): up[i] = lax.ppermute(up[i], 'col', hop_up)]
    ppermute x6, waiting for transfers between devices: 23 us -> 0.02 us  [on_device(): down[1 - i] = lax.ppermute(down[1 - i], 'col', hop_down)]
    pallas_call x8, Pallas kernels: 20.6 us -> 10.3 us  [multiply(): pl.pallas_call(kernel, out_shape=jax.ShapeDtypeStruct(before.shape, jnp.f...]
    ppermute x1, waiting for transfers between devices: 3.09 us -> 11.3 us  [on_device(): up_half = lax.ppermute(up[0], 'col', hop_up)]
    ppermute x6, starting transfers between devices: 21.4 us -> 17.4 us  [on_device(): down[1 - i] = lax.ppermute(down[1 - i], 'col', hop_down)]
    ppermute x1, waiting for transfers between devices: 3.74 us -> 0.01 us  [on_device(): down_half = lax.ppermute(down[1], 'col', hop_down)]
    ppermute x6, starting transfers between devices: 0.02 us -> 2.56 us  [on_device(): up[i] = lax.ppermute(up[i], 'col', hop_up)]
  transfers between devices with their start and end apart: 14 -> 14, of which waited for: 7 -> 7; matrix products, arithmetic and copies ran while one was open for 0% -> 0% of each run, Pallas kernels for 15% -> 8%
where the time goes in v4:
time: 116 us
  waiting for transfers between devices  62.9 us (54%)
  starting transfers between devices  22.6 us (19%)
  blocking collectives  16.9 us (15%)
  Pallas kernels  11 us (9%)
  local copies, waits for them, and re-layouts  1.5 us (1%)
    ppermute x6, waiting for transfers between devices, on_device(): up[i] = lax.ppermute(up[i], 'col', hop_up)  51.6 us
    ppermute x6, starting transfers between devices, on_device(): down[1 - i] = lax.ppermute(down[1 - i], 'col', hop_down)  17.4 us
    all_to_all x1, blocking collectives, on_device(): return lax.all_to_all(blocks, ('row', 'layer'), 0, 0).sum(0)  16.9 us
    ppermute x1, waiting for transfers between devices, on_device(): up_half = lax.ppermute(up[0], 'col', hop_up)  11.3 us
    pallas_call x8, Pallas kernels, multiply(): pl.pallas_call(kernel, out_shape=jax.ShapeDtypeStruct(before.shape, jnp.f...  10.3 us
    ppermute x1, starting transfers between devices, on_device(): down_half = lax.ppermute(down[1], 'col', hop_down)  2.67 us
    ppermute x6, starting transfers between devices, on_device(): up[i] = lax.ppermute(up[i], 'col', hop_up)  2.56 us
  transfers between devices with their start and end apart: 14, of which 7 were waited for; matrix products, arithmetic and copies ran while one was open for 0% of the time, Pallas kernels for 8%

profile of v4, /device:TPU:1, one launch (start us, length us, event | category | flops | bytes accessed | tf_op | source)
XLA Modules:
  0.0 115.7 jit_solution(2738605105929953705)
XLA Ops:
  0.0 0.0 copy-start
  0.0 1.5 %fusion = (f32[32,4608]{1,0:T(8,128)S(1)}, f32[32,4608]{1,0:T(8,128)S(1)}) fusion(f32[64,4608]{1,0:T(8,128)} %param.2), kind=kLoop, calls=%fused_computation | loop fusion | bytes 2359296 | tf_op jit(solution)/shard_map/slice | solution.py:58
  1.5 2.5 %collective-permute-start = (f32[32,4608]{1,0:T(8,128)S(1)}, f32[32,4608]{1,0:T(8,128)S(1)}, u32[]{:S(2)}, u32[]{:S(2)}) collective-permute-start(f32[32,4608]{1,0:T(8,128)S(1)} %get-tuple-element.7.refs_0_), channel_id=1, source_target_pairs={{0,4},{4,8},{8,12},{12,16},{16,20},{20,24},{24,28},{28,0},{1,5},{5... | collective-permute-start | bytes 1769480 | tf_op jit(solution)/shard_map/ppermute | solution.py:66
  4.0 4.0 %collective-permute-start.4 = (f32[32,4608]{1,0:T(8,128)S(1)}, f32[32,4608]{1,0:T(8,128)S(1)}, u32[]{:S(2)}, u32[]{:S(2)}) collective-permute-start(f32[32,4608]{1,0:T(8,128)S(1)} %get-tuple-element.8.refs_1_), channel_id=1, source_target_pairs={{0,28},{4,0},{8,4},{12,8},{16,12},{20,16},{24,20},{28,24},{1,29},{... | collective-permute-start | bytes 1769480 | tf_op jit(solution)/shard_map/ppermute | solution.py:67
  8.1 0.0 collective-permute-start.8
  8.1 2.7 %collective-permute-start.11 = (f32[32,4608]{1,0:T(8,128)S(1)}, f32[32,4608]{1,0:T(8,128)S(1)}, u32[]{:S(2)}, u32[]{:S(2)}) collective-permute-start(f32[32,4608]{1,0:T(8,128)S(1)} %get-tuple-element.7.refs_0_), channel_id=1, source_target_pairs={{0,28},{4,0},{8,4},{12,8},{16,12},{20,16},{24,20},{28,24},{1,29},{... | collective-permute-start | bytes 1769480 | tf_op jit(solution)/shard_map/ppermute | solution.py:67
  10.7 10.3 %collective-permute-done.refs_0_ = f32[32,4608]{1,0:T(8,128)S(1)} collective-permute-done((f32[32,4608]{1,0:T(8,128)S(1)}, f32[32,4608]{1,0:T(8,128)S(1)}, u32[]{:S(2)}, u32[]{:S(2)}) %collective-permute-start) | collective-permute-done | bytes 589856 | tf_op jit(solution)/shard_map/ppermute | solution.py:66
  21.0 0.0 collective-permute-start.1
  21.0 0.0 collective-permute-done.4.refs_1_
  21.0 2.7 %collective-permute-start.5 = (f32[32,4608]{1,0:T(8,128)S(1)}, f32[32,4608]{1,0:T(8,128)S(1)}, u32[]{:S(2)}, u32[]{:S(2)}) collective-permute-start(f32[32,4608]{1,0:T(8,128)S(1)} %collective-permute-done.4.refs_1_), channel_id=1, source_target_pairs={{0,28},{4,0},{8,4},{12,8},{16,12},{20,16},{24,20},{28,24},{1,29},{... | collective-permute-start | bytes 1769480 | tf_op jit(solution)/shard_map/ppermute | solution.py:67
  23.7 10.0 %collective-permute-done.8.refs_0_ = f32[32,4608]{1,0:T(8,128)S(1)} collective-permute-done((f32[32,4608]{1,0:T(8,128)S(1)}, f32[32,4608]{1,0:T(8,128)S(1)}, u32[]{:S(2)}, u32[]{:S(2)}) %collective-permute-start.8) | collective-permute-done | bytes 589856 | tf_op jit(solution)/shard_map/ppermute | solution.py:66
  33.7 0.0 collective-permute-start.9
  33.7 0.0 collective-permute-done.11.refs_1_
  33.7 2.7 %collective-permute-start.12 = (f32[32,4608]{1,0:T(8,128)S(1)}, f32[32,4608]{1,0:T(8,128)S(1)}, u32[]{:S(2)}, u32[]{:S(2)}) collective-permute-start(f32[32,4608]{1,0:T(8,128)S(1)} %collective-permute-done.11.refs_1_), channel_id=1, source_target_pairs={{0,28},{4,0},{8,4},{12,8},{16,12},{20,16},{24,20},{28,24},{1,29},{... | collective-permute-start | bytes 1769480 | tf_op jit(solution)/shard_map/ppermute | solution.py:67
  36.3 10.0 %collective-permute-done.1.refs_0_ = f32[32,4608]{1,0:T(8,128)S(1)} collective-permute-done((f32[32,4608]{1,0:T(8,128)S(1)}, f32[32,4608]{1,0:T(8,128)S(1)}, u32[]{:S(2)}, u32[]{:S(2)}) %collective-permute-start.1) | collective-permute-done | bytes 589856 | tf_op jit(solution)/shard_map/ppermute | solution.py:66
  46.3 0.0 collective-permute-start.2
  46.3 0.0 collective-permute-done.5.refs_1_
  46.3 2.7 %collective-permute-start.6 = (f32[32,4608]{1,0:T(8,128)S(1)}, f32[32,4608]{1,0:T(8,128)S(1)}, u32[]{:S(2)}, u32[]{:S(2)}) collective-permute-start(f32[32,4608]{1,0:T(8,128)S(1)} %collective-permute-done.5.refs_1_), channel_id=1, source_target_pairs={{0,28},{4,0},{8,4},{12,8},{16,12},{20,16},{24,20},{28,24},{1,29},{... | collective-permute-start | bytes 1769480 | tf_op jit(solution)/shard_map/ppermute | solution.py:67
  49.0 10.0 %collective-permute-done.9.refs_0_ = f32[32,4608]{1,0:T(8,128)S(1)} collective-permute-done((f32[32,4608]{1,0:T(8,128)S(1)}, f32[32,4608]{1,0:T(8,128)S(1)}, u32[]{:S(2)}, u32[]{:S(2)}) %collective-permute-start.9) | collective-permute-done | bytes 589856 | tf_op jit(solution)/shard_map/ppermute | solution.py:66
  58.9 0.0 collective-permute-start.10
  58.9 0.0 collective-permute-done.12.refs_1_
  58.9 2.7 %collective-permute-start.13 = (f32[32,4608]{1,0:T(8,128)S(1)}, f32[32,4608]{1,0:T(8,128)S(1)}, u32[]{:S(2)}, u32[]{:S(2)}) collective-permute-start(f32[32,4608]{1,0:T(8,128)S(1)} %collective-permute-done.12.refs_1_), channel_id=1, source_target_pairs={{0,28},{4,0},{8,4},{12,8},{16,12},{20,16},{24,20},{28,24},{1,29},{... | collective-permute-start | bytes 1769480 | tf_op jit(solution)/shard_map/ppermute | solution.py:67
  61.6 10.0 %collective-permute-done.2.refs_0_ = f32[32,4608]{1,0:T(8,128)S(1)} collective-permute-done((f32[32,4608]{1,0:T(8,128)S(1)}, f32[32,4608]{1,0:T(8,128)S(1)}, u32[]{:S(2)}, u32[]{:S(2)}) %collective-permute-start.2) | collective-permute-done | bytes 589856 | tf_op jit(solution)/shard_map/ppermute | solution.py:66
  71.6 0.0 collective-permute-start.3
  71.6 0.0 collective-permute-done.6.refs_1_
  71.6 2.7 %collective-permute-start.7 = (f32[32,4608]{1,0:T(8,128)S(1)}, f32[32,4608]{1,0:T(8,128)S(1)}, u32[]{:S(2)}, u32[]{:S(2)}) collective-permute-start(f32[32,4608]{1,0:T(8,128)S(1)} %collective-permute-done.6.refs_1_), channel_id=1, source_target_pairs={{0,28},{4,0},{8,4},{12,8},{16,12},{20,16},{24,20},{28,24},{1,29},{... | collective-permute-start | bytes 1769480 | tf_op jit(solution)/shard_map/ppermute | solution.py:70
  74.3 0.0 copy-done
  74.3 0.7 shard_map.28.refs_2_
  75.0 1.3 %shard_map.29.refs_3_ = f32[8,64,128]{2,1,0:T(8,128)S(1)} custom-call(f32[32,4608]{1,0:T(8,128)S(1)} %get-tuple-element.7.refs_0_, f32[32,4608]{1,0:T(8,128)S(1)} %get-tuple-element.8.refs_1_, f32[4608,128]{1,0:T(8,128)S(1)} %shard_map.28.refs_2_, f32[8,64,128]{2,1,0:T(8,128)S(1)} %broadcast_in_dim.3.refs_3_), custom_call_target="tpu_custom_call", output_to_operand_aliasing={{}: (3, {})} | custom-call | tf_op jit(solution)/shard_map/pallas_call | solution.py:41
  76.3 1.3 %shard_map.30.refs_3_ = f32[8,64,128]{2,1,0:T(8,128)S(1)} custom-call(f32[32,4608]{1,0:T(8,128)S(1)} %collective-permute-done.refs_0_, f32[32,4608]{1,0:T(8,128)S(1)} %collective-permute-done.4.refs_1_, f32[4608,128]{1,0:T(8,128)S(1)} %shard_map.28.refs_2_, f32[8,64,128]{2,1,0:T(8,128)S(1)} %shard_map.29.refs_3_), custom_call_target="tpu_custom_call", output_to_operand_aliasing={{}: (3, {})} | custom-call | tf_op jit(solution)/shard_map/pallas_call | solution.py:41
  77.6 1.3 %shard_map.31.refs_3_ = f32[8,64,128]{2,1,0:T(8,128)S(1)} custom-call(f32[32,4608]{1,0:T(8,128)S(1)} %collective-permute-done.8.refs_0_, f32[32,4608]{1,0:T(8,128)S(1)} %collective-permute-done.11.refs_1_, f32[4608,128]{1,0:T(8,128)S(1)} %shard_map.28.refs_2_, f32[8,64,128]{2,1,0:T(8,128)S(1)} %shard_map.30.refs_3_), custom_call_target="tpu_custom_call", output_to_operand_aliasing={{}: (3, {})} | custom-call | tf_op jit(solution)/shard_map/pallas_call | solution.py:41
  78.9 1.3 %shard_map.32.refs_3_ = f32[8,64,128]{2,1,0:T(8,128)S(1)} custom-call(f32[32,4608]{1,0:T(8,128)S(1)} %collective-permute-done.1.refs_0_, f32[32,4608]{1,0:T(8,128)S(1)} %collective-permute-done.5.refs_1_, f32[4608,128]{1,0:T(8,128)S(1)} %shard_map.28.refs_2_, f32[8,64,128]{2,1,0:T(8,128)S(1)} %shard_map.31.refs_3_), custom_call_target="tpu_custom_call", output_to_operand_aliasing={{}: (3, {})} | custom-call | tf_op jit(solution)/shard_map/pallas_call | solution.py:41
  80.2 1.3 %shard_map.33.refs_3_ = f32[8,64,128]{2,1,0:T(8,128)S(1)} custom-call(f32[32,4608]{1,0:T(8,128)S(1)} %collective-permute-done.9.refs_0_, f32[32,4608]{1,0:T(8,128)S(1)} %collective-permute-done.12.refs_1_, f32[4608,128]{1,0:T(8,128)S(1)} %shard_map.28.refs_2_, f32[8,64,128]{2,1,0:T(8,128)S(1)} %shard_map.32.refs_3_), custom_call_target="tpu_custom_call", output_to_operand_aliasing={{}: (3, {})} | custom-call | tf_op jit(solution)/shard_map/pallas_call | solution.py:41
  81.5 1.3 %shard_map.34.refs_3_ = f32[8,64,128]{2,1,0:T(8,128)S(1)} custom-call(f32[32,4608]{1,0:T(8,128)S(1)} %collective-permute-done.2.refs_0_, f32[32,4608]{1,0:T(8,128)S(1)} %collective-permute-done.6.refs_1_, f32[4608,128]{1,0:T(8,128)S(1)} %shard_map.28.refs_2_, f32[8,64,128]{2,1,0:T(8,128)S(1)} %shard_map.33.refs_3_), custom_call_target="tpu_custom_call", output_to_operand_aliasing={{}: (3, {})} | custom-call | tf_op jit(solution)/shard_map/pallas_call | solution.py:41
  82.8 1.5 %collective-permute-done.10.refs_0_ = f32[32,4608]{1,0:T(8,128)S(1)} collective-permute-done((f32[32,4608]{1,0:T(8,128)S(1)}, f32[32,4608]{1,0:T(8,128)S(1)}, u32[]{:S(2)}, u32[]{:S(2)}) %collective-permute-start.10) | collective-permute-done | bytes 589856 | tf_op jit(solution)/shard_map/ppermute | solution.py:66
  84.2 0.0 collective-permute-done.13.refs_1_
  84.2 1.3 %shard_map.35.refs_3_ = f32[8,64,128]{2,1,0:T(8,128)S(1)} custom-call(f32[32,4608]{1,0:T(8,128)S(1)} %collective-permute-done.10.refs_0_, f32[32,4608]{1,0:T(8,128)S(1)} %collective-permute-done.13.refs_1_, f32[4608,128]{1,0:T(8,128)S(1)} %shard_map.28.refs_2_, f32[8,64,128]{2,1,0:T(8,128)S(1)} %shard_map.34.refs_3_), custom_call_target="tpu_custom_call", output_to_operand_aliasing={{}: (3, {})} | custom-call | tf_op jit(solution)/shard_map/pallas_call | solution.py:41
  85.5 11.3 %collective-permute-done.3.refs_0_ = f32[32,4608]{1,0:T(8,128)S(1)} collective-permute-done((f32[32,4608]{1,0:T(8,128)S(1)}, f32[32,4608]{1,0:T(8,128)S(1)}, u32[]{:S(2)}, u32[]{:S(2)}) %collective-permute-start.3) | collective-permute-done | bytes 589856 | tf_op jit(solution)/shard_map/ppermute | solution.py:69
  96.9 0.0 collective-permute-done.7.refs_1_
  96.9 1.3 %shard_map.36 = f32[8,64,128]{2,1,0:T(8,128)S(1)} custom-call(f32[32,4608]{1,0:T(8,128)S(1)} %collective-permute-done.3.refs_0_, f32[32,4608]{1,0:T(8,128)S(1)} %collective-permute-done.7.refs_1_, f32[4608,128]{1,0:T(8,128)S(1)} %shard_map.28.refs_2_, f32[8,64,128]{2,1,0:T(8,128)S(1)} %shard_map.35.refs_3_), custom_call_target="tpu_custom_call", output_to_operand_aliasing={{}: (3, {})} | custom-call | tf_op jit(solution)/shard_map/pallas_call | solution.py:41
  98.2 16.9 %all_to_all.5 = f32[32,16,128]{2,1,0:T(8,128)S(1)} all-to-all(f32[32,16,128]{2,1,0:T(8,128)S(1)} %bitcast.1), channel_id=1, replica_groups=mesh['row'=8,'col'=8,'layer'=4] {'row','layer'}, dimensions={0} | all-to-all | bytes 524288 | tf_op jit(solution)/shard_map/all_to_all | solution.py:76
  115.1 0.6 reduce_sum.9
  (1 shorter events, 0.0 us)
Async XLA Ops:
  0.0 74.3 %copy-start = (f32[128,4608]{1,0:T(8,128)S(1)}, f32[128,4608]{1,0:T(8,128)}, u32[]{:S(2)}) copy-start(f32[128,4608]{1,0:T(8,128)} %src.1) | copy-start | bytes 7077892
  1.5 19.5 %collective-permute-start = (f32[32,4608]{1,0:T(8,128)S(1)}, f32[32,4608]{1,0:T(8,128)S(1)}, u32[]{:S(2)}, u32[]{:S(2)}) collective-permute-start(f32[32,4608]{1,0:T(8,128)S(1)} %get-tuple-element.7.refs_0_), channel_id=1, source_target_pairs={{0,4},{4,8},{8,12},{12,16},{16,20},{20,24},{24,28},{28,0},{1,5},{5... | collective-permute-start | bytes 1769480 | tf_op jit(solution)/shard_map/ppermute | solution.py:66
  4.0 17.0 %collective-permute-start.4 = (f32[32,4608]{1,0:T(8,128)S(1)}, f32[32,4608]{1,0:T(8,128)S(1)}, u32[]{:S(2)}, u32[]{:S(2)}) collective-permute-start(f32[32,4608]{1,0:T(8,128)S(1)} %get-tuple-element.8.refs_1_), channel_id=1, source_target_pairs={{0,28},{4,0},{8,4},{12,8},{16,12},{20,16},{24,20},{28,24},{1,29},{... | collective-permute-start | bytes 1769480 | tf_op jit(solution)/shard_map/ppermute | solution.py:67
  8.1 25.6 %collective-permute-start.8 = (f32[32,4608]{1,0:T(8,128)S(1)}, f32[32,4608]{1,0:T(8,128)S(1)}, u32[]{:S(2)}, u32[]{:S(2)}) collective-permute-start(f32[32,4608]{1,0:T(8,128)S(1)} %get-tuple-element.8.refs_1_), channel_id=1, source_target_pairs={{0,4},{4,8},{8,12},{12,16},{16,20},{20,24},{24,28},{28,0},{1,5},{5... | collective-permute-start | bytes 1769480 | tf_op jit(solution)/shard_map/ppermute | solution.py:66
  8.1 25.6 %collective-permute-start.11 = (f32[32,4608]{1,0:T(8,128)S(1)}, f32[32,4608]{1,0:T(8,128)S(1)}, u32[]{:S(2)}, u32[]{:S(2)}) collective-permute-start(f32[32,4608]{1,0:T(8,128)S(1)} %get-tuple-element.7.refs_0_), channel_id=1, source_target_pairs={{0,28},{4,0},{8,4},{12,8},{16,12},{20,16},{24,20},{28,24},{1,29},{... | collective-permute-start | bytes 1769480 | tf_op jit(solution)/shard_map/ppermute | solution.py:67
  21.0 25.3 %collective-permute-start.1 = (f32[32,4608]{1,0:T(8,128)S(1)}, f32[32,4608]{1,0:T(8,128)S(1)}, u32[]{:S(2)}, u32[]{:S(2)}) collective-permute-start(f32[32,4608]{1,0:T(8,128)S(1)} %collective-permute-done.refs_0_), channel_id=1, source_target_pairs={{0,4},{4,8},{8,12},{12,16},{16,20},{20,24},{24,28},{28,0},{1,5},{5... | collective-permute-start | bytes 1769480 | tf_op jit(solution)/shard_map/ppermute | solution.py:66
  21.0 25.3 %collective-permute-start.5 = (f32[32,4608]{1,0:T(8,128)S(1)}, f32[32,4608]{1,0:T(8,128)S(1)}, u32[]{:S(2)}, u32[]{:S(2)}) collective-permute-start(f32[32,4608]{1,0:T(8,128)S(1)} %collective-permute-done.4.refs_1_), channel_id=1, source_target_pairs={{0,28},{4,0},{8,4},{12,8},{16,12},{20,16},{24,20},{28,24},{1,29},{... | collective-permute-start | bytes 1769480 | tf_op jit(solution)/shard_map/ppermute | solution.py:67
  33.7 25.3 %collective-permute-start.9 = (f32[32,4608]{1,0:T(8,128)S(1)}, f32[32,4608]{1,0:T(8,128)S(1)}, u32[]{:S(2)}, u32[]{:S(2)}) collective-permute-start(f32[32,4608]{1,0:T(8,128)S(1)} %collective-permute-done.8.refs_0_), channel_id=1, source_target_pairs={{0,4},{4,8},{8,12},{12,16},{16,20},{20,24},{24,28},{28,0},{1,5},{5... | collective-permute-start | bytes 1769480 | tf_op jit(solution)/shard_map/ppermute | solution.py:66
  33.7 25.3 %collective-permute-start.12 = (f32[32,4608]{1,0:T(8,128)S(1)}, f32[32,4608]{1,0:T(8,128)S(1)}, u32[]{:S(2)}, u32[]{:S(2)}) collective-permute-start(f32[32,4608]{1,0:T(8,128)S(1)} %collective-permute-done.11.refs_1_), channel_id=1, source_target_pairs={{0,28},{4,0},{8,4},{12,8},{16,12},{20,16},{24,20},{28,24},{1,29},{... | collective-permute-start | bytes 1769480 | tf_op jit(solution)/shard_map/ppermute | solution.py:67
  46.3 25.3 %collective-permute-start.2 = (f32[32,4608]{1,0:T(8,128)S(1)}, f32[32,4608]{1,0:T(8,128)S(1)}, u32[]{:S(2)}, u32[]{:S(2)}) collective-permute-start(f32[32,4608]{1,0:T(8,128)S(1)} %collective-permute-done.1.refs_0_), channel_id=1, source_target_pairs={{0,4},{4,8},{8,12},{12,16},{16,20},{20,24},{24,28},{28,0},{1,5},{5... | collective-permute-start | bytes 1769480 | tf_op jit(solution)/shard_map/ppermute | solution.py:66
  46.3 25.3 %collective-permute-start.6 = (f32[32,4608]{1,0:T(8,128)S(1)}, f32[32,4608]{1,0:T(8,128)S(1)}, u32[]{:S(2)}, u32[]{:S(2)}) collective-permute-start(f32[32,4608]{1,0:T(8,128)S(1)} %collective-permute-done.5.refs_1_), channel_id=1, source_target_pairs={{0,28},{4,0},{8,4},{12,8},{16,12},{20,16},{24,20},{28,24},{1,29},{... | collective-permute-start | bytes 1769480 | tf_op jit(solution)/shard_map/ppermute | solution.py:67
  58.9 25.3 %collective-permute-start.10 = (f32[32,4608]{1,0:T(8,128)S(1)}, f32[32,4608]{1,0:T(8,128)S(1)}, u32[]{:S(2)}, u32[]{:S(2)}) collective-permute-start(f32[32,4608]{1,0:T(8,128)S(1)} %collective-permute-done.9.refs_0_), channel_id=1, source_target_pairs={{0,4},{4,8},{8,12},{12,16},{16,20},{20,24},{24,28},{28,0},{1,5},{5... | collective-permute-start | bytes 1769480 | tf_op jit(solution)/shard_map/ppermute | solution.py:66
  58.9 25.3 %collective-permute-start.13 = (f32[32,4608]{1,0:T(8,128)S(1)}, f32[32,4608]{1,0:T(8,128)S(1)}, u32[]{:S(2)}, u32[]{:S(2)}) collective-permute-start(f32[32,4608]{1,0:T(8,128)S(1)} %collective-permute-done.12.refs_1_), channel_id=1, source_target_pairs={{0,28},{4,0},{8,4},{12,8},{16,12},{20,16},{24,20},{28,24},{1,29},{... | collective-permute-start | bytes 1769480 | tf_op jit(solution)/shard_map/ppermute | solution.py:67
  71.6 25.3 %collective-permute-start.3 = (f32[32,4608]{1,0:T(8,128)S(1)}, f32[32,4608]{1,0:T(8,128)S(1)}, u32[]{:S(2)}, u32[]{:S(2)}) collective-permute-start(f32[32,4608]{1,0:T(8,128)S(1)} %collective-permute-done.2.refs_0_), channel_id=1, source_target_pairs={{0,4},{4,8},{8,12},{12,16},{16,20},{20,24},{24,28},{28,0},{1,5},{5... | collective-permute-start | bytes 1769480 | tf_op jit(solution)/shard_map/ppermute | solution.py:69
  71.6 25.3 %collective-permute-start.7 = (f32[32,4608]{1,0:T(8,128)S(1)}, f32[32,4608]{1,0:T(8,128)S(1)}, u32[]{:S(2)}, u32[]{:S(2)}) collective-permute-start(f32[32,4608]{1,0:T(8,128)S(1)} %collective-permute-done.6.refs_1_), channel_id=1, source_target_pairs={{0,28},{4,0},{8,4},{12,8},{16,12},{20,16},{24,20},{28,24},{1,29},{... | collective-permute-start | bytes 1769480 | tf_op jit(solution)/shard_map/ppermute | solution.py:70

commit v5 on v0

v5 whole, which is shorter than its diff:
```python
import jax
import jax.numpy as jnp
from jax import lax
from jax.experimental import pallas as pl
from jax.experimental.pallas import tpu as pltpu
from jax.sharding import Mesh
from jax.sharding import PartitionSpec as P

LEVELS = 8
EARLY = 48
COL = ("zhi", "zlo")
VMEM = pl.BlockSpec(memory_space=pltpu.VMEM)
SWAP_1 = [(i, i ^ 1) for i in range(LEVELS)]
SWAP_2 = [((i + 1) % LEVELS, (j + 1) % LEVELS) for i, j in SWAP_1]


def swap_1(array):
    return lax.ppermute(array, COL, SWAP_1)


def swap_2(array):
    return lax.ppermute(array, COL, SWAP_2)


def after(done, *payloads):
    return lax.optimization_barrier((*payloads, *done))[: len(payloads)]


def dot(left, right):
    return 0.5 * jnp.dot(
        left, right, precision=lax.Precision.HIGHEST, preferred_element_type=jnp.float32
    )


def transposed(array):
    def kernel(src, out):
        out[...] = src[...].T

    return pl.pallas_call(
        kernel,
        out_shape=jax.ShapeDtypeStruct(array.shape[::-1], array.dtype),
        in_specs=[VMEM],
        out_specs=VMEM,
        compiler_params=pltpu.CompilerParams(vmem_limit_bytes=16 * 1024 * 1024),
    )(array)


def row_level(level, distance):
    away = jnp.where(lax.rem(level, 2) == 0, distance % LEVELS, -distance % LEVELS)
    return lax.rem(level + away, LEVELS)


def multiply(blocks, distances, b, before):
    count = len(blocks)

    def kernel(*refs):
        b_ref, old, out = refs[count:]
        level = lax.axis_index("zhi") * 2 + lax.axis_index("zlo")
        out[...] = old[...]
        for ref, distance in zip(refs, distances):
            out[lax.axis_index("zlo"), row_level(level, distance)] = dot(ref[...], b_ref[...])

    return pl.pallas_call(
        kernel,
        out_shape=jax.ShapeDtypeStruct(before.shape, jnp.float32),
        in_specs=[VMEM] * (count + 2),
        out_specs=VMEM,
        input_output_aliases={count + 1: 0},
        compiler_params=pltpu.CompilerParams(vmem_limit_bytes=24 * 1024 * 1024),
    )(*blocks, b, before)


def split(array):
    high = array.astype(jnp.bfloat16)
    return high, (array - high.astype(jnp.float32)).astype(jnp.bfloat16)


def split_stack(blocks):
    count, (rows, width) = len(blocks), blocks[0].shape

    def kernel(*refs):
        high, low = refs[count:]
        for i, ref in enumerate(refs[:count]):
            place = slice(i * rows, (i + 1) * rows)
            high[place, :], low[place, :] = split(ref[...])

    return pl.pallas_call(
        kernel,
        out_shape=[jax.ShapeDtypeStruct((count * rows, width), jnp.bfloat16)] * 2,
        in_specs=[VMEM] * count,
        out_specs=[VMEM] * 2,
        compiler_params=pltpu.CompilerParams(vmem_limit_bytes=24 * 1024 * 1024),
    )(*blocks)


def finish(last, b, before, stack, distances, pair_b):
    rows = last.shape[0]

    def kernel(last_ref, b_ref, high, low, *refs):
        pair_refs, old, out = refs[:-2], refs[-2], refs[-1]
        odd = lax.axis_index("zlo")
        level = lax.axis_index("zhi") * 2 + odd
        out[...] = old[...]
        block = last_ref[...]
        out[odd, row_level(level, LEVELS // 2)] = dot(block, b_ref[...])
        b_high, b_low = split(jnp.concatenate([ref[...] for ref in pair_refs], axis=0).T)

        def product(a_high, a_low):
            terms = [(a_low, b_high), (a_high, b_low), (a_high, b_high)]
            return 0.5 * sum(jnp.dot(*t, preferred_element_type=jnp.float32) for t in terms)

        early = product(high[...], low[...])
        for i, distance in enumerate(distances):
            out[1 - odd, row_level(level, distance)] = early[i * rows : (i + 1) * rows]
        out[1 - odd, row_level(level, LEVELS // 2)] = product(*split(block))

    return pl.pallas_call(
        kernel,
        out_shape=jax.ShapeDtypeStruct(before.shape, jnp.float32),
        in_specs=[VMEM] * (5 + len(pair_b)),
        out_specs=VMEM,
        input_output_aliases={4 + len(pair_b): 0},
        compiler_params=pltpu.CompilerParams(vmem_limit_bytes=24 * 1024 * 1024),
    )(last, b, *stack, *pair_b, before)


def on_device(amplitudes, integrals):
    level = lax.axis_index("zhi") * 2 + lax.axis_index("zlo")
    held = (level + 1) // 2 % 2
    rows, columns = amplitudes.shape[0], integrals.shape[0]
    half = amplitudes.shape[1] // 2

    def halves(array):
        low, high = array[:, :half], array[:, half:]
        return jnp.where(held == 0, low, high), jnp.where(held == 0, high, low)

    a_own, a_other = lax.optimization_barrier(halves(amplitudes))
    b_own, b_other = halves(integrals)

    far_1, far_2 = swap_1(a_own), swap_2(a_other)
    a_1, a_2 = swap_1(a_other), swap_2(a_own)
    a_3, far_2 = swap_1(far_2), swap_2(far_1)
    b_early, a_1_on = after((a_1, a_2), b_other[:EARLY], a_1)
    pair_early, a_4 = swap_1(b_early), swap_2(a_1_on)
    a_5, a_6 = swap_1(far_2), swap_2(a_3)
    (b_late,) = after((pair_early, a_4), b_other[EARLY:])
    a_7, pair_late = swap_2(a_5), swap_1(b_late)

    b = transposed(b_own)
    product = jnp.zeros((2, LEVELS, rows, columns), jnp.float32)
    early, distances = [a_own, a_1, a_2, a_3, a_4, a_6, a_5], [0, 1, -1, 2, -2, -3, 3]
    for part in (slice(0, 3), slice(3, 5), slice(5, 7)):
        product = multiply(early[part], distances[part], b, product)
    pair_b = [pair_early, pair_late]
    product = finish(a_7, b, product, split_stack(early), distances, pair_b)

    axes = ("zlo", "row", "layer")
    blocks = product.reshape(lax.axis_size(axes), -1, columns)
    return lax.all_to_all(blocks, axes, 0, 0).sum(0)


def solution(mesh):
    rows, _, layers = mesh.devices.shape
    fine = Mesh(mesh.devices.reshape(rows, -1, 2, layers), ("row", "zhi", "zlo", "layer"))
    split = ("row", "layer")
    return jax.shard_map(
        on_device,
        mesh=fine,
        in_specs=(P(COL, split), P(COL, split)),
        out_specs=P(split, COL),
        check_vma=False,
    )
```

time: 217 us -> 112 us (0.52)
  waiting for transfers between devices: 192 us -> 53 us
  starting transfers between devices: 0.04 us -> 25.1 us
  blocking collectives: 0 us -> 23 us
  between operations: 13.4 us -> 0.1 us
  matrix products: 10.7 us -> 0 us
  Pallas kernels: 0 us -> 8.61 us
  other arithmetic: 0 us -> 2.29 us
    all_gather x1 -> x0, waiting for transfers between devices: 110 us -> none  [on_device(): lax.all_gather(amplitudes, 'col', axis=0, tiled=True)]
    reduce_scatter x1 -> x0, waiting for transfers between devices: 81.2 us -> none  [on_device(): lax.psum_scatter(0.5 * partial_sum, ('row', 'layer'), scatter_dimension=0...]
    ppermute x0 -> x12, waiting for transfers between devices: none -> 53 us  [the longest x6 29.9 us: swap_1(): return lax.ppermute(array, COL, SWAP_1)]
    ppermute x0 -> x12, starting transfers between devices: none -> 25.1 us  [the longest x6 21 us: swap_2(): return lax.ppermute(array, COL, SWAP_2)]
    all_to_all x0 -> x1, blocking collectives: none -> 23 us  [on_device(): return lax.all_to_all(blocks, axes, 0, 0).sum(0)]
    dot_general x1 -> x0, matrix products: 10.7 us -> none  [contract_last(): lax.dot_general(left, right, (((1,), (1,)), ((), ())), precision=lax.Prec...]
    pallas_call x0 -> x6, Pallas kernels: none -> 8.61 us  [the longest x3 4.75 us: multiply(): pl.pallas_call(kernel, out_shape=jax.ShapeDtypeStruct(before.shape, jnp.f...]
  transfers between devices with their start and end apart: 2 -> 12, of which waited for: 2 -> 6; matrix products, arithmetic and copies ran while one was open for 0% -> 0% of each run, Pallas kernels for 0% -> 5%
where the time goes in v5:
time: 112 us
  waiting for transfers between devices  53 us (47%)
  starting transfers between devices  25.1 us (22%)
  blocking collectives  23 us (21%)
  Pallas kernels  8.61 us (8%)
  other arithmetic  2.29 us (2%)
    ppermute x6, waiting for transfers between devices, swap_1(): return lax.ppermute(array, COL, SWAP_1)  29.9 us
    ppermute x6, waiting for transfers between devices, swap_2(): return lax.ppermute(array, COL, SWAP_2)  23 us
    all_to_all x1, blocking collectives, on_device(): return lax.all_to_all(blocks, axes, 0, 0).sum(0)  23 us
    ppermute x6, starting transfers between devices, swap_2(): return lax.ppermute(array, COL, SWAP_2)  21 us
    pallas_call x3, Pallas kernels, multiply(): pl.pallas_call(kernel, out_shape=jax.ShapeDtypeStruct(before.shape, jnp.f...  4.75 us
    ppermute x6, starting transfers between devices, swap_1(): return lax.ppermute(array, COL, SWAP_1)  4.03 us
    pallas_call x1, Pallas kernels, finish(): pl.pallas_call(kernel, out_shape=jax.ShapeDtypeStruct(before.shape, jnp.f...  2.74 us
  transfers between devices with their start and end apart: 12, of which 6 were waited for; matrix products, arithmetic and copies ran while one was open for 0% of the time, Pallas kernels for 5%

profile of v5, /device:TPU:1, one launch (start us, length us, event | category | flops | bytes accessed | tf_op | source)
XLA Modules:
  0.0 112.2 jit_solution(12945689899084213187)
XLA Ops:
  0.0 0.0 copy-start
  0.0 1.5 %slice_select_fusion.2 = (f32[64,2304]{1,0:T(8,128)S(1)}, f32[64,2304]{1,0:T(8,128)S(1)}) fusion(f32[64,4608]{1,0:T(8,128)} %param.2, pred[]{:T(512)S(6)} %eq.4), kind=kLoop, calls=%fused_computation.2 | loop fusion | flops 294912 | bytes 2359297 | tf_op jit(solution)/shard_map/jit(_where)/select_n | solution.py:135
  1.5 2.6 %collective-permute-start = (f32[64,2304]{1,0:T(8,128)S(1)}, f32[64,2304]{1,0:T(8,128)S(1)}, u32[]{:S(2)}, u32[]{:S(2)}) collective-permute-start(f32[64,2304]{1,0:T(8,128)S(1)} %get-tuple-element.12.refs_0_), channel_id=1, source_target_pairs={{0,4},{4,0},{8,12},{12,8},{16,20},{20,16},{24,28},{28,24},{1,5},{5... | collective-permute-start | bytes 1769480 | tf_op jit(solution)/shard_map/ppermute | solution.py:18
  4.0 4.7 %collective-permute-start.5 = (f32[64,2304]{1,0:T(8,128)S(1)}, f32[64,2304]{1,0:T(8,128)S(1)}, u32[]{:S(2)}, u32[]{:S(2)}) collective-permute-start(f32[64,2304]{1,0:T(8,128)S(1)} %get-tuple-element.12.refs_0_), channel_id=1, source_target_pairs={{4,8},{8,4},{12,16},{16,12},{20,24},{24,20},{28,0},{0,28},{5,9},{9... | collective-permute-start | bytes 1769480 | tf_op jit(solution)/shard_map/ppermute | solution.py:22
  8.7 0.0 collective-permute-start.4
  8.7 1.5 %collective-permute-start.6 = (f32[64,2304]{1,0:T(8,128)S(1)}, f32[64,2304]{1,0:T(8,128)S(1)}, u32[]{:S(2)}, u32[]{:S(2)}) collective-permute-start(f32[64,2304]{1,0:T(8,128)S(1)} %get-tuple-element.13), channel_id=1, source_target_pairs={{4,8},{8,4},{12,16},{16,12},{20,24},{24,20},{28,0},{0,28},{5,9},{9... | collective-permute-start | bytes 1769480 | tf_op jit(solution)/shard_map/ppermute | solution.py:22
  10.2 5.9 %collective-permute-done = f32[64,2304]{1,0:T(8,128)S(1)} collective-permute-done((f32[64,2304]{1,0:T(8,128)S(1)}, f32[64,2304]{1,0:T(8,128)S(1)}, u32[]{:S(2)}, u32[]{:S(2)}) %collective-permute-start) | collective-permute-done | bytes 589856 | tf_op jit(solution)/shard_map/ppermute | solution.py:18
  16.0 6.1 %collective-permute-start.1 = (f32[64,2304]{1,0:T(8,128)S(1)}, f32[64,2304]{1,0:T(8,128)S(1)}, u32[]{:S(2)}, u32[]{:S(2)}) collective-permute-start(f32[64,2304]{1,0:T(8,128)S(1)} %collective-permute-done), channel_id=1, source_target_pairs={{4,8},{8,4},{12,16},{16,12},{20,24},{24,20},{28,0},{0,28},{5,9},{9... | collective-permute-start | bytes 1769480 | tf_op jit(solution)/shard_map/ppermute | solution.py:22
  22.2 0.0 copy-done
  22.2 0.2 slice_select_fusion
  22.4 6.3 %collective-permute-done.4.refs_1_ = f32[64,2304]{1,0:T(8,128)S(1)} collective-permute-done((f32[64,2304]{1,0:T(8,128)S(1)}, f32[64,2304]{1,0:T(8,128)S(1)}, u32[]{:S(2)}, u32[]{:S(2)}) %collective-permute-start.4) | collective-permute-done | bytes 589856 | tf_op jit(solution)/shard_map/ppermute | solution.py:18
  28.7 0.0 collective-permute-done.5.refs_2_
  28.7 6.1 %collective-permute-start.8 = (f32[64,2304]{1,0:T(8,128)S(1)}, f32[64,2304]{1,0:T(8,128)S(1)}, u32[]{:S(2)}, u32[]{:S(2)}) collective-permute-start(f32[64,2304]{1,0:T(8,128)S(1)} %collective-permute-done.4.refs_1_), channel_id=1, source_target_pairs={{4,8},{8,4},{12,16},{16,12},{20,24},{24,20},{28,0},{0,28},{5,9},{9... | collective-permute-start | bytes 1769480 | tf_op jit(solution)/shard_map/ppermute | solution.py:22
  34.8 0.0 collective-permute-start.10
  34.8 0.0 collective-permute-done.6
  34.8 1.5 %collective-permute-start.7 = (f32[64,2304]{1,0:T(8,128)S(1)}, f32[64,2304]{1,0:T(8,128)S(1)}, u32[]{:S(2)}, u32[]{:S(2)}) collective-permute-start(f32[64,2304]{1,0:T(8,128)S(1)} %collective-permute-done.6), channel_id=1, source_target_pairs={{0,4},{4,0},{8,12},{12,8},{16,20},{20,16},{24,28},{28,24},{1,5},{5... | collective-permute-start | bytes 1769480 | tf_op jit(solution)/shard_map/ppermute | solution.py:18
  36.3 10.4 %collective-permute-done.1 = f32[64,2304]{1,0:T(8,128)S(1)} collective-permute-done((f32[64,2304]{1,0:T(8,128)S(1)}, f32[64,2304]{1,0:T(8,128)S(1)}, u32[]{:S(2)}, u32[]{:S(2)}) %collective-permute-start.1) | collective-permute-done | bytes 589856 | tf_op jit(solution)/shard_map/ppermute | solution.py:22
  46.7 0.0 collective-permute-start.2
  46.8 0.0 collective-permute-done.10.refs_0_
  46.8 12.6 %collective-permute-done.8.refs_4_.refs_1_ = f32[64,2304]{1,0:T(8,128)S(1)} collective-permute-done((f32[64,2304]{1,0:T(8,128)S(1)}, f32[64,2304]{1,0:T(8,128)S(1)}, u32[]{:S(2)}, u32[]{:S(2)}) %collective-permute-start.8) | collective-permute-done | bytes 589856 | tf_op jit(solution)/shard_map/ppermute | solution.py:22
  59.4 0.0 collective-permute-start.11
  59.4 0.0 collective-permute-done.7.refs_3_.refs_0_
  59.4 2.4 %collective-permute-start.9 = (f32[64,2304]{1,0:T(8,128)S(1)}, f32[64,2304]{1,0:T(8,128)S(1)}, u32[]{:S(2)}, u32[]{:S(2)}) collective-permute-start(f32[64,2304]{1,0:T(8,128)S(1)} %collective-permute-done.7.refs_3_.refs_0_), channel_id=1, source_target_pairs={{4,8},{8,4},{12,16},{16,12},{20,24},{24,20},{28,0},{0,28},{5,9},{9... | collective-permute-start | bytes 1769480 | tf_op jit(solution)/shard_map/ppermute | solution.py:22
  61.7 8.2 %collective-permute-done.2.refs_6_.refs_1_ = f32[64,2304]{1,0:T(8,128)S(1)} collective-permute-done((f32[64,2304]{1,0:T(8,128)S(1)}, f32[64,2304]{1,0:T(8,128)S(1)}, u32[]{:S(2)}, u32[]{:S(2)}) %collective-permute-start.2) | collective-permute-done | bytes 589856 | tf_op jit(solution)/shard_map/ppermute | solution.py:18
  69.9 0.3 collective-permute-start.3
  70.2 0.4 shard_map.28.refs_3_.refs_2_.b_ref
  70.6 2.0 %shard_map.30.refs_3_ = f32[2,8,64,128]{3,2,1,0:T(8,128)S(1)} custom-call(f32[64,2304]{1,0:T(8,128)S(1)} %get-tuple-element.12.refs_0_, f32[64,2304]{1,0:T(8,128)S(1)} %collective-permute-done.4.refs_1_, f32[64,2304]{1,0:T(8,128)S(1)} %collective-permute-done.5.refs_2_, ...), custom_call_target="tpu_custom_call", output_to_operand_aliasing={{}: (4, {})} | custom-call | tf_op jit(solution)/shard_map/pallas_call | solution.py:63
  72.6 1.4 %shard_map.31.refs_3_ = f32[2,8,64,128]{3,2,1,0:T(8,128)S(1)} custom-call(f32[64,2304]{1,0:T(8,128)S(1)} %collective-permute-done.7.refs_3_.refs_0_, f32[64,2304]{1,0:T(8,128)S(1)} %collective-permute-done.8.refs_4_.refs_1_, f32[2304,128]{1,0:T(8,128)S(1)} %shard_map.28.refs_3_.refs_2_.b_ref, ...), custom_call_target="tpu_custom_call", output_to_operand_aliasing={{}: (3, {})} | custom-call | tf_op jit(solution)/shard_map/pallas_call | solution.py:63
  74.0 0.0 collective-permute-done.9.refs_5_.refs_0_
  74.0 0.8 shard_map.29
  74.8 1.4 %shard_map.32.refs_2_ = f32[2,8,64,128]{3,2,1,0:T(8,128)S(1)} custom-call(f32[64,2304]{1,0:T(8,128)S(1)} %collective-permute-done.9.refs_5_.refs_0_, f32[64,2304]{1,0:T(8,128)S(1)} %collective-permute-done.2.refs_6_.refs_1_, f32[2304,128]{1,0:T(8,128)S(1)} %shard_map.28.refs_3_.refs_2_.b_ref, ...), custom_call_target="tpu_custom_call", output_to_operand_aliasing={{}: (3, {})} | custom-call | tf_op jit(solution)/shard_map/pallas_call | solution.py:63
  76.2 9.6 %collective-permute-done.11.refs_1_ = f32[80,2304]{1,0:T(8,128)S(1)} collective-permute-done((f32[80,2304]{1,0:T(8,128)S(1)}, f32[80,2304]{1,0:T(8,128)S(1)}, u32[]{:S(2)}, u32[]{:S(2)}) %collective-permute-start.11) | collective-permute-done | bytes 737312 | tf_op jit(solution)/shard_map/ppermute | solution.py:18
  85.7 0.0 collective-permute-done.3.last_ref
  85.7 2.7 %shard_map.33 = f32[2,8,64,128]{3,2,1,0:T(8,128)S(1)} custom-call(f32[64,2304]{1,0:T(8,128)S(1)} %collective-permute-done.3.last_ref, f32[2304,128]{1,0:T(8,128)S(1)} %shard_map.28.refs_3_.refs_2_.b_ref, bf16[448,2304]{1,0:T(8,128)(2,1)S(1)} %get-tuple-element.15.high, bf16[448,2304]{1,0:T(8,128)(2,1)S(1)} %get-tuple-element.16.low, ...), custom_call_target="tpu_custom_call", output_to_operand_aliasing={{}: (6, {})} | custom-call | tf_op jit(solution)/shard_map/pallas_call | solution.py:117
  88.5 23.0 %all_to_all.5 = f32[64,16,128]{2,1,0:T(8,128)S(1)} all-to-all(f32[64,16,128]{2,1,0:T(8,128)S(1)} %bitcast.1), channel_id=1, replica_groups=mesh['row'=8,'zhi'=4,'zlo'=2,'layer'=4] {'zlo','row','layer'}, dimensions={0} | all-to-all | bytes 1048576 | tf_op jit(solution)/shard_map/all_to_all | solution.py:159
  111.5 0.7 reduce_sum.9
  (3 shorter events, 0.1 us)
Async XLA Ops:
  0.0 22.2 %copy-start = (f32[128,4608]{1,0:T(8,128)S(1)}, f32[128,4608]{1,0:T(8,128)}, u32[]{:S(2)}) copy-start(f32[128,4608]{1,0:T(8,128)} %param.3) | copy-start | bytes 7077892
  1.5 14.6 %collective-permute-start = (f32[64,2304]{1,0:T(8,128)S(1)}, f32[64,2304]{1,0:T(8,128)S(1)}, u32[]{:S(2)}, u32[]{:S(2)}) collective-permute-start(f32[64,2304]{1,0:T(8,128)S(1)} %get-tuple-element.12.refs_0_), channel_id=1, source_target_pairs={{0,4},{4,0},{8,12},{12,8},{16,20},{20,16},{24,28},{28,24},{1,5},{5... | collective-permute-start | bytes 1769480 | tf_op jit(solution)/shard_map/ppermute | solution.py:18
  4.0 24.6 %collective-permute-start.5 = (f32[64,2304]{1,0:T(8,128)S(1)}, f32[64,2304]{1,0:T(8,128)S(1)}, u32[]{:S(2)}, u32[]{:S(2)}) collective-permute-start(f32[64,2304]{1,0:T(8,128)S(1)} %get-tuple-element.12.refs_0_), channel_id=1, source_target_pairs={{4,8},{8,4},{12,16},{16,12},{20,24},{24,20},{28,0},{0,28},{5,9},{9... | collective-permute-start | bytes 1769480 | tf_op jit(solution)/shard_map/ppermute | solution.py:22
  8.7 20.0 %collective-permute-start.4 = (f32[64,2304]{1,0:T(8,128)S(1)}, f32[64,2304]{1,0:T(8,128)S(1)}, u32[]{:S(2)}, u32[]{:S(2)}) collective-permute-start(f32[64,2304]{1,0:T(8,128)S(1)} %get-tuple-element.13), channel_id=1, source_target_pairs={{0,4},{4,0},{8,12},{12,8},{16,20},{20,16},{24,28},{28,24},{1,5},{5... | collective-permute-start | bytes 1769480 | tf_op jit(solution)/shard_map/ppermute | solution.py:18
  8.7 26.1 %collective-permute-start.6 = (f32[64,2304]{1,0:T(8,128)S(1)}, f32[64,2304]{1,0:T(8,128)S(1)}, u32[]{:S(2)}, u32[]{:S(2)}) collective-permute-start(f32[64,2304]{1,0:T(8,128)S(1)} %get-tuple-element.13), channel_id=1, source_target_pairs={{4,8},{8,4},{12,16},{16,12},{20,24},{24,20},{28,0},{0,28},{5,9},{9... | collective-permute-start | bytes 1769480 | tf_op jit(solution)/shard_map/ppermute | solution.py:22
  16.0 30.7 %collective-permute-start.1 = (f32[64,2304]{1,0:T(8,128)S(1)}, f32[64,2304]{1,0:T(8,128)S(1)}, u32[]{:S(2)}, u32[]{:S(2)}) collective-permute-start(f32[64,2304]{1,0:T(8,128)S(1)} %collective-permute-done), channel_id=1, source_target_pairs={{4,8},{8,4},{12,16},{16,12},{20,24},{24,20},{28,0},{0,28},{5,9},{9... | collective-permute-start | bytes 1769480 | tf_op jit(solution)/shard_map/ppermute | solution.py:22
  28.7 30.7 %collective-permute-start.8 = (f32[64,2304]{1,0:T(8,128)S(1)}, f32[64,2304]{1,0:T(8,128)S(1)}, u32[]{:S(2)}, u32[]{:S(2)}) collective-permute-start(f32[64,2304]{1,0:T(8,128)S(1)} %collective-permute-done.4.refs_1_), channel_id=1, source_target_pairs={{4,8},{8,4},{12,16},{16,12},{20,24},{24,20},{28,0},{0,28},{5,9},{9... | collective-permute-start | bytes 1769480 | tf_op jit(solution)/shard_map/ppermute | solution.py:22
  34.8 12.0 %collective-permute-start.10 = (f32[48,2304]{1,0:T(8,128)S(1)}, f32[48,2304]{1,0:T(8,128)S(1)}, u32[]{:S(2)}, u32[]{:S(2)}) collective-permute-start(f32[48,2304]{1,0:T(8,128)S(1)} %slice.24), channel_id=1, source_target_pairs={{0,4},{4,0},{8,12},{12,8},{16,20},{20,16},{24,28},{28,24},{1,5},{5... | collective-permute-start | bytes 1327112 | tf_op jit(solution)/shard_map/ppermute | solution.py:18
  34.8 24.5 %collective-permute-start.7 = (f32[64,2304]{1,0:T(8,128)S(1)}, f32[64,2304]{1,0:T(8,128)S(1)}, u32[]{:S(2)}, u32[]{:S(2)}) collective-permute-start(f32[64,2304]{1,0:T(8,128)S(1)} %collective-permute-done.6), channel_id=1, source_target_pairs={{0,4},{4,0},{8,12},{12,8},{16,20},{20,16},{24,28},{28,24},{1,5},{5... | collective-permute-start | bytes 1769480 | tf_op jit(solution)/shard_map/ppermute | solution.py:18
  46.7 23.2 %collective-permute-start.2 = (f32[64,2304]{1,0:T(8,128)S(1)}, f32[64,2304]{1,0:T(8,128)S(1)}, u32[]{:S(2)}, u32[]{:S(2)}) collective-permute-start(f32[64,2304]{1,0:T(8,128)S(1)} %collective-permute-done.1), channel_id=1, source_target_pairs={{0,4},{4,0},{8,12},{12,8},{16,20},{20,16},{24,28},{28,24},{1,5},{5... | collective-permute-start | bytes 1769480 | tf_op jit(solution)/shard_map/ppermute | solution.py:18
  59.4 26.4 %collective-permute-start.11 = (f32[80,2304]{1,0:T(8,128)S(1)}, f32[80,2304]{1,0:T(8,128)S(1)}, u32[]{:S(2)}, u32[]{:S(2)}) collective-permute-start(f32[80,2304]{1,0:T(8,128)S(1)} %slice.25), channel_id=1, source_target_pairs={{0,4},{4,0},{8,12},{12,8},{16,20},{20,16},{24,28},{28,24},{1,5},{5... | collective-permute-start | bytes 2211848 | tf_op jit(solution)/shard_map/ppermute | solution.py:18
  59.4 14.6 %collective-permute-start.9 = (f32[64,2304]{1,0:T(8,128)S(1)}, f32[64,2304]{1,0:T(8,128)S(1)}, u32[]{:S(2)}, u32[]{:S(2)}) collective-permute-start(f32[64,2304]{1,0:T(8,128)S(1)} %collective-permute-done.7.refs_3_.refs_0_), channel_id=1, source_target_pairs={{4,8},{8,4},{12,16},{16,12},{20,24},{24,20},{28,0},{0,28},{5,9},{9... | collective-permute-start | bytes 1769480 | tf_op jit(solution)/shard_map/ppermute | solution.py:22
  69.9 15.8 %collective-permute-start.3 = (f32[64,2304]{1,0:T(8,128)S(1)}, f32[64,2304]{1,0:T(8,128)S(1)}, u32[]{:S(2)}, u32[]{:S(2)}) collective-permute-start(f32[64,2304]{1,0:T(8,128)S(1)} %collective-permute-done.2.refs_6_.refs_1_), channel_id=1, source_target_pairs={{4,8},{8,4},{12,16},{16,12},{20,24},{24,20},{28,0},{0,28},{5,9},{9... | collective-permute-start | bytes 1769480 | tf_op jit(solution)/shard_map/ppermute | solution.py:22

commit v6 on v5

--- a/solution.py
+++ b/solution.py
@@ -58,7 +58,8 @@
         level = lax.axis_index("zhi") * 2 + lax.axis_index("zlo")
         out[...] = old[...]
         for ref, distance in zip(refs, distances):
-            out[lax.axis_index("zlo"), row_level(level, distance)] = dot(ref[...], b_ref[...])
+            source = row_level(level, distance)
+            out[lax.rem(source, 2), lax.axis_index("zlo"), source // 2] = dot(ref[...], b_ref[...])
 
     return pl.pallas_call(
         kernel,
@@ -97,12 +98,25 @@
     rows = last.shape[0]
 
     def kernel(last_ref, b_ref, high, low, *refs):
-        pair_refs, old, out = refs[:-2], refs[-2], refs[-1]
-        odd = lax.axis_index("zlo")
+        pair_refs, old, mine, other = refs[:-3], refs[-3], refs[-2], refs[-1]
+        core, odd = lax.axis_index("core"), lax.axis_index("zlo")
         level = lax.axis_index("zhi") * 2 + odd
-        out[...] = old[...]
+        mine[odd] = old[core, odd]
+        other[odd] = old[1 - core, odd]
+
+        def store(column, distance, product):
+            source = row_level(level, distance)
+
+            @pl.when(lax.rem(source, 2) == core)
+            def _():
+                mine[column, source // 2] = product
+
+            @pl.when(lax.rem(source, 2) != core)
+            def _():
+                other[column, source // 2] = product
+
         block = last_ref[...]
-        out[odd, row_level(level, LEVELS // 2)] = dot(block, b_ref[...])
+        store(odd, LEVELS // 2, dot(block, b_ref[...]))
         b_high, b_low = split(jnp.concatenate([ref[...] for ref in pair_refs], axis=0).T)
 
         def product(a_high, a_low):
@@ -111,15 +125,14 @@
 
         early = product(high[...], low[...])
         for i, distance in enumerate(distances):
-            out[1 - odd, row_level(level, distance)] = early[i * rows : (i + 1) * rows]
-        out[1 - odd, row_level(level, LEVELS // 2)] = product(*split(block))
+            store(1 - odd, distance, early[i * rows : (i + 1) * rows])
+        store(1 - odd, LEVELS // 2, product(*split(block)))
 
     return pl.pallas_call(
         kernel,
-        out_shape=jax.ShapeDtypeStruct(before.shape, jnp.float32),
+        out_shape=[jax.ShapeDtypeStruct(before.shape[1:], jnp.float32)] * 2,
         in_specs=[VMEM] * (5 + len(pair_b)),
-        out_specs=VMEM,
-        input_output_aliases={4 + len(pair_b): 0},
+        out_specs=[VMEM] * 2,
         compiler_params=pltpu.CompilerParams(vmem_limit_bytes=24 * 1024 * 1024),
     )(last, b, *stack, *pair_b, before)
 
@@ -139,34 +152,36 @@
 
     far_1, far_2 = swap_1(a_own), swap_2(a_other)
     a_1, a_2 = swap_1(a_other), swap_2(a_own)
-    a_3, far_2 = swap_1(far_2), swap_2(far_1)
+    a_3, far_3 = swap_1(far_2), swap_2(far_1)
     b_early, a_1_on = after((a_1, a_2), b_other[:EARLY], a_1)
     pair_early, a_4 = swap_1(b_early), swap_2(a_1_on)
-    a_5, a_6 = swap_1(far_2), swap_2(a_3)
+    a_5, a_6 = swap_1(far_3), swap_2(a_3)
     (b_late,) = after((pair_early, a_4), b_other[EARLY:])
     a_7, pair_late = swap_2(a_5), swap_1(b_late)
 
     b = transposed(b_own)
-    product = jnp.zeros((2, LEVELS, rows, columns), jnp.float32)
+    product = jnp.zeros((2, 2, LEVELS // 2, rows, columns), jnp.float32)
     early, distances = [a_own, a_1, a_2, a_3, a_4, a_6, a_5], [0, 1, -1, 2, -2, -3, 3]
     for part in (slice(0, 3), slice(3, 5), slice(5, 7)):
         product = multiply(early[part], distances[part], b, product)
     pair_b = [pair_early, pair_late]
-    product = finish(a_7, b, product, split_stack(early), distances, pair_b)
+    mine, other = finish(a_7, b, product, split_stack(early), distances, pair_b)
+    product = mine + lax.ppermute(other, "core", [(0, 1), (1, 0)])
 
-    axes = ("zlo", "row", "layer")
+    axes = ("zlo", "x", "layer")
     blocks = product.reshape(lax.axis_size(axes), -1, columns)
     return lax.all_to_all(blocks, axes, 0, 0).sum(0)
 
 
 def solution(mesh):
-    rows, _, layers = mesh.devices.shape
-    fine = Mesh(mesh.devices.reshape(rows, -1, 2, layers), ("row", "zhi", "zlo", "layer"))
-    split = ("row", "layer")
+    rows, levels, layers = mesh.devices.shape
+    shape = (rows // 2, 2, levels // 2, 2, layers)
+    fine = Mesh(mesh.devices.reshape(shape), ("x", "core", "zhi", "zlo", "layer"))
+    split_rows = ("x", "core", "layer")
     return jax.shard_map(
         on_device,
         mesh=fine,
-        in_specs=(P(COL, split), P(COL, split)),
-        out_specs=P(split, COL),
+        in_specs=(P(COL, split_rows), P(COL, split_rows)),
+        out_specs=P(split_rows, COL),
         check_vma=False,
     )

time: 112 us -> 109 us (0.973)
  blocking collectives: 23 us -> 14.8 us
  starting transfers between devices: 25.1 us -> 28.4 us
    all_to_all x1, blocking collectives: 23 us -> 14.8 us  [on_device(): return lax.all_to_all(blocks, axes, 0, 0).sum(0)]
    ppermute x0 -> x1, starting transfers between devices: none -> 3.31 us  [on_device(): product = mine + lax.ppermute(other, 'core', [(0, 1), (1, 0)])]
    ppermute x0 -> x1, waiting for transfers between devices: none -> 1.16 us  [on_device(): product = mine + lax.ppermute(other, 'core', [(0, 1), (1, 0)])]
  transfers between devices with their start and end apart: 12 -> 13, of which waited for: 6 -> 7; matrix products, arithmetic and copies ran while one was open for 0% -> 0% of each run, Pallas kernels for 5% -> 5%
where the time goes in v6:
time: 109 us
  waiting for transfers between devices  54.1 us (50%)
  starting transfers between devices  28.4 us (26%)
  blocking collectives  14.8 us (14%)
  Pallas kernels  9.4 us (9%)
  other arithmetic  2.3 us (2%)
    ppermute x6, waiting for transfers between devices, swap_1(): return lax.ppermute(array, COL, SWAP_1)  29.9 us
    ppermute x6, waiting for transfers between devices, swap_2(): return lax.ppermute(array, COL, SWAP_2)  23 us
    ppermute x6, starting transfers between devices, swap_2(): return lax.ppermute(array, COL, SWAP_2)  21 us
    all_to_all x1, blocking collectives, on_device(): return lax.all_to_all(blocks, axes, 0, 0).sum(0)  14.8 us
    pallas_call x3, Pallas kernels, multiply(): pl.pallas_call(kernel, out_shape=jax.ShapeDtypeStruct(before.shape, jnp.f...  4.76 us
    ppermute x6, starting transfers between devices, swap_1(): return lax.ppermute(array, COL, SWAP_1)  4.03 us
    pallas_call x1, Pallas kernels, finish(): pl.pallas_call(kernel, out_shape=[jax.ShapeDtypeStruct(before.shape[1:],...  3.53 us
    ppermute x1, starting transfers between devices, on_device(): product = mine + lax.ppermute(other, 'core', [(0, 1), (1, 0)])  3.31 us
  transfers between devices with their start and end apart: 13, of which 7 were waited for; matrix products, arithmetic and copies ran while one was open for 0% of the time, Pallas kernels for 5%

profile of v6, /device:TPU:1, one launch (start us, length us, event | category | flops | bytes accessed | tf_op | source)
XLA Modules:
  0.0 109.2 jit_solution(836744120753014750)
XLA Ops:
  0.0 0.0 copy-start
  0.0 1.5 %slice_select_fusion.2 = (f32[64,2304]{1,0:T(8,128)S(1)}, f32[64,2304]{1,0:T(8,128)S(1)}) fusion(f32[64,4608]{1,0:T(8,128)} %param.2, pred[]{:T(512)S(6)} %eq.4), kind=kLoop, calls=%fused_computation.2 | loop fusion | flops 294912 | bytes 2359297 | tf_op jit(solution)/shard_map/jit(_where)/select_n | solution.py:148
  1.5 2.6 %collective-permute-start = (f32[64,2304]{1,0:T(8,128)S(1)}, f32[64,2304]{1,0:T(8,128)S(1)}, u32[]{:S(2)}, u32[]{:S(2)}) collective-permute-start(f32[64,2304]{1,0:T(8,128)S(1)} %get-tuple-element.14.refs_0_), channel_id=1, source_target_pairs={{0,4},{4,0},{8,12},{12,8},{16,20},{20,16},{24,28},{28,24},{1,5},{5... | collective-permute-start | bytes 1769480 | tf_op jit(solution)/shard_map/ppermute | solution.py:18
  4.0 4.7 %collective-permute-start.5 = (f32[64,2304]{1,0:T(8,128)S(1)}, f32[64,2304]{1,0:T(8,128)S(1)}, u32[]{:S(2)}, u32[]{:S(2)}) collective-permute-start(f32[64,2304]{1,0:T(8,128)S(1)} %get-tuple-element.14.refs_0_), channel_id=1, source_target_pairs={{4,8},{8,4},{12,16},{16,12},{20,24},{24,20},{28,0},{0,28},{5,9},{9... | collective-permute-start | bytes 1769480 | tf_op jit(solution)/shard_map/ppermute | solution.py:22
  8.7 0.0 collective-permute-start.4
  8.7 1.5 %collective-permute-start.6 = (f32[64,2304]{1,0:T(8,128)S(1)}, f32[64,2304]{1,0:T(8,128)S(1)}, u32[]{:S(2)}, u32[]{:S(2)}) collective-permute-start(f32[64,2304]{1,0:T(8,128)S(1)} %get-tuple-element.15), channel_id=1, source_target_pairs={{4,8},{8,4},{12,16},{16,12},{20,24},{24,20},{28,0},{0,28},{5,9},{9... | collective-permute-start | bytes 1769480 | tf_op jit(solution)/shard_map/ppermute | solution.py:22
  10.2 5.9 %collective-permute-done = f32[64,2304]{1,0:T(8,128)S(1)} collective-permute-done((f32[64,2304]{1,0:T(8,128)S(1)}, f32[64,2304]{1,0:T(8,128)S(1)}, u32[]{:S(2)}, u32[]{:S(2)}) %collective-permute-start) | collective-permute-done | bytes 589856 | tf_op jit(solution)/shard_map/ppermute | solution.py:18
  16.0 6.1 %collective-permute-start.1 = (f32[64,2304]{1,0:T(8,128)S(1)}, f32[64,2304]{1,0:T(8,128)S(1)}, u32[]{:S(2)}, u32[]{:S(2)}) collective-permute-start(f32[64,2304]{1,0:T(8,128)S(1)} %collective-permute-done), channel_id=1, source_target_pairs={{4,8},{8,4},{12,16},{16,12},{20,24},{24,20},{28,0},{0,28},{5,9},{9... | collective-permute-start | bytes 1769480 | tf_op jit(solution)/shard_map/ppermute | solution.py:22
  22.2 0.0 copy-done
  22.2 0.2 slice_select_fusion
  22.4 6.3 %collective-permute-done.4.refs_1_ = f32[64,2304]{1,0:T(8,128)S(1)} collective-permute-done((f32[64,2304]{1,0:T(8,128)S(1)}, f32[64,2304]{1,0:T(8,128)S(1)}, u32[]{:S(2)}, u32[]{:S(2)}) %collective-permute-start.4) | collective-permute-done | bytes 589856 | tf_op jit(solution)/shard_map/ppermute | solution.py:18
  28.7 0.0 collective-permute-done.5.refs_2_
  28.7 6.1 %collective-permute-start.8 = (f32[64,2304]{1,0:T(8,128)S(1)}, f32[64,2304]{1,0:T(8,128)S(1)}, u32[]{:S(2)}, u32[]{:S(2)}) collective-permute-start(f32[64,2304]{1,0:T(8,128)S(1)} %collective-permute-done.4.refs_1_), channel_id=1, source_target_pairs={{4,8},{8,4},{12,16},{16,12},{20,24},{24,20},{28,0},{0,28},{5,9},{9... | collective-permute-start | bytes 1769480 | tf_op jit(solution)/shard_map/ppermute | solution.py:22
  34.8 0.0 collective-permute-start.10
  34.8 0.0 collective-permute-done.6
  34.8 1.5 %collective-permute-start.7 = (f32[64,2304]{1,0:T(8,128)S(1)}, f32[64,2304]{1,0:T(8,128)S(1)}, u32[]{:S(2)}, u32[]{:S(2)}) collective-permute-start(f32[64,2304]{1,0:T(8,128)S(1)} %collective-permute-done.6), channel_id=1, source_target_pairs={{0,4},{4,0},{8,12},{12,8},{16,20},{20,16},{24,28},{28,24},{1,5},{5... | collective-permute-start | bytes 1769480 | tf_op jit(solution)/shard_map/ppermute | solution.py:18
  36.3 10.4 %collective-permute-done.1 = f32[64,2304]{1,0:T(8,128)S(1)} collective-permute-done((f32[64,2304]{1,0:T(8,128)S(1)}, f32[64,2304]{1,0:T(8,128)S(1)}, u32[]{:S(2)}, u32[]{:S(2)}) %collective-permute-start.1) | collective-permute-done | bytes 589856 | tf_op jit(solution)/shard_map/ppermute | solution.py:22
  46.7 0.0 collective-permute-start.2
  46.8 0.0 collective-permute-done.10.refs_0_
  46.8 12.6 %collective-permute-done.8.refs_4_.refs_1_ = f32[64,2304]{1,0:T(8,128)S(1)} collective-permute-done((f32[64,2304]{1,0:T(8,128)S(1)}, f32[64,2304]{1,0:T(8,128)S(1)}, u32[]{:S(2)}, u32[]{:S(2)}) %collective-permute-start.8) | collective-permute-done | bytes 589856 | tf_op jit(solution)/shard_map/ppermute | solution.py:22
  59.4 0.0 collective-permute-start.11
  59.4 0.0 collective-permute-done.7.refs_3_.refs_0_
  59.4 2.4 %collective-permute-start.9 = (f32[64,2304]{1,0:T(8,128)S(1)}, f32[64,2304]{1,0:T(8,128)S(1)}, u32[]{:S(2)}, u32[]{:S(2)}) collective-permute-start(f32[64,2304]{1,0:T(8,128)S(1)} %collective-permute-done.7.refs_3_.refs_0_), channel_id=1, source_target_pairs={{4,8},{8,4},{12,16},{16,12},{20,24},{24,20},{28,0},{0,28},{5,9},{9... | collective-permute-start | bytes 1769480 | tf_op jit(solution)/shard_map/ppermute | solution.py:22
  61.7 8.2 %collective-permute-done.2.refs_6_.refs_1_ = f32[64,2304]{1,0:T(8,128)S(1)} collective-permute-done((f32[64,2304]{1,0:T(8,128)S(1)}, f32[64,2304]{1,0:T(8,128)S(1)}, u32[]{:S(2)}, u32[]{:S(2)}) %collective-permute-start.2) | collective-permute-done | bytes 589856 | tf_op jit(solution)/shard_map/ppermute | solution.py:18
  69.9 0.3 collective-permute-start.3
  70.2 0.4 shard_map.28.refs_3_.refs_2_.b_ref
  70.6 2.0 %shard_map.30.refs_3_ = f32[2,2,4,64,128]{4,3,2,1,0:T(8,128)S(1)} custom-call(f32[64,2304]{1,0:T(8,128)S(1)} %get-tuple-element.14.refs_0_, f32[64,2304]{1,0:T(8,128)S(1)} %collective-permute-done.4.refs_1_, f32[64,2304]{1,0:T(8,128)S(1)} %collective-permute-done.5.refs_2_, ...), custom_call_target="tpu_custom_call", output_to_operand_aliasing={{}: (4, {})} | custom-call | tf_op jit(solution)/shard_map/pallas_call | solution.py:64
  72.6 1.4 %shard_map.31.refs_3_ = f32[2,2,4,64,128]{4,3,2,1,0:T(8,128)S(1)} custom-call(f32[64,2304]{1,0:T(8,128)S(1)} %collective-permute-done.7.refs_3_.refs_0_, f32[64,2304]{1,0:T(8,128)S(1)} %collective-permute-done.8.refs_4_.refs_1_, f32[2304,128]{1,0:T(8,128)S(1)} %shard_map.28.refs_3_.refs_2_.b_ref, ...), custom_call_target="tpu_custom_call", output_to_operand_aliasing={{}: (3, {})} | custom-call | tf_op jit(solution)/shard_map/pallas_call | solution.py:64
  74.0 0.0 collective-permute-done.9.refs_5_.refs_0_
  74.0 0.8 shard_map.29
  74.8 1.4 %shard_map.32.refs_2_ = f32[2,2,4,64,128]{4,3,2,1,0:T(8,128)S(1)} custom-call(f32[64,2304]{1,0:T(8,128)S(1)} %collective-permute-done.9.refs_5_.refs_0_, f32[64,2304]{1,0:T(8,128)S(1)} %collective-permute-done.2.refs_6_.refs_1_, f32[2304,128]{1,0:T(8,128)S(1)} %shard_map.28.refs_3_.refs_2_.b_ref, ...), custom_call_target="tpu_custom_call", output_to_operand_aliasing={{}: (3, {})} | custom-call | tf_op jit(solution)/shard_map/pallas_call | solution.py:64
  76.2 9.5 %collective-permute-done.11.refs_1_ = f32[80,2304]{1,0:T(8,128)S(1)} collective-permute-done((f32[80,2304]{1,0:T(8,128)S(1)}, f32[80,2304]{1,0:T(8,128)S(1)}, u32[]{:S(2)}, u32[]{:S(2)}) %collective-permute-start.11) | collective-permute-done | bytes 737312 | tf_op jit(solution)/shard_map/ppermute | solution.py:18
  85.7 0.0 collective-permute-done.3.last_ref
  85.7 3.5 %shard_map.33 = (f32[2,4,64,128]{3,2,1,0:T(8,128)S(1)}, f32[2,4,64,128]{3,2,1,0:T(8,128)S(1)}) custom-call(f32[64,2304]{1,0:T(8,128)S(1)} %collective-permute-done.3.last_ref, f32[2304,128]{1,0:T(8,128)S(1)} %shard_map.28.refs_3_.refs_2_.b_ref, bf16[448,2304]{1,0:T(8,128)(2,1)S(1)} %get-tuple-element.17.high, bf16[448,2304]{1,0:T(8,128)(2,1)S(1)} %get-tuple-element.18.low, ...), custom_call_target="tpu_custom_call" | custom-call | tf_op jit(solution)/shard_map/pallas_call | solution.py:131
  89.3 3.3 %collective-permute-start.12 = (f32[2,4,64,128]{3,2,1,0:T(8,128)S(1)}, f32[2,4,64,128]{3,2,1,0:T(8,128)S(1)}, u32[]{:S(2)}, u32[]{:S(2)}) collective-permute-start(f32[2,4,64,128]{3,2,1,0:T(8,128)S(1)} %get-tuple-element.22), channel_id=1, source_target_pairs={{0,32},{32,0},{1,33},{33,1},{2,34},{34,2},{3,35},{35,3},{4,36},{36... | collective-permute-start | bytes 786440 | tf_op jit(solution)/shard_map/ppermute | solution.py:169
  92.6 1.2 %collective-permute-done.12 = f32[2,4,64,128]{3,2,1,0:T(8,128)S(1)} collective-permute-done((f32[2,4,64,128]{3,2,1,0:T(8,128)S(1)}, f32[2,4,64,128]{3,2,1,0:T(8,128)S(1)}, u32[]{:S(2)}, u32[]{:S(2)}) %collective-permute-start.12) | collective-permute-done | bytes 262176 | tf_op jit(solution)/shard_map/ppermute | solution.py:169
  93.8 14.8 %all_to_all.5 = f32[32,16,128]{2,1,0:T(8,128)S(1)} all-to-all(f32[32,16,128]{2,1,0:T(8,128)S(1)} %bitcast.1), channel_id=1, replica_groups=mesh['x'=4,'core'=2,'zhi'=4,'zlo'=2,'layer'=4] {'zlo','x','layer'}, dimensions={0} | all-to-all | bytes 524288 | tf_op jit(solution)/shard_map/all_to_all | solution.py:173
  108.6 0.6 reduce_sum.9
  (4 shorter events, 0.2 us)
Async XLA Ops:
  0.0 22.2 %copy-start = (f32[128,4608]{1,0:T(8,128)S(1)}, f32[128,4608]{1,0:T(8,128)}, u32[]{:S(2)}) copy-start(f32[128,4608]{1,0:T(8,128)} %param.3) | copy-start | bytes 7077892
  1.5 14.6 %collective-permute-start = (f32[64,2304]{1,0:T(8,128)S(1)}, f32[64,2304]{1,0:T(8,128)S(1)}, u32[]{:S(2)}, u32[]{:S(2)}) collective-permute-start(f32[64,2304]{1,0:T(8,128)S(1)} %get-tuple-element.14.refs_0_), channel_id=1, source_target_pairs={{0,4},{4,0},{8,12},{12,8},{16,20},{20,16},{24,28},{28,24},{1,5},{5... | collective-permute-start | bytes 1769480 | tf_op jit(solution)/shard_map/ppermute | solution.py:18
  4.0 24.6 %collective-permute-start.5 = (f32[64,2304]{1,0:T(8,128)S(1)}, f32[64,2304]{1,0:T(8,128)S(1)}, u32[]{:S(2)}, u32[]{:S(2)}) collective-permute-start(f32[64,2304]{1,0:T(8,128)S(1)} %get-tuple-element.14.refs_0_), channel_id=1, source_target_pairs={{4,8},{8,4},{12,16},{16,12},{20,24},{24,20},{28,0},{0,28},{5,9},{9... | collective-permute-start | bytes 1769480 | tf_op jit(solution)/shard_map/ppermute | solution.py:22
  8.7 20.0 %collective-permute-start.4 = (f32[64,2304]{1,0:T(8,128)S(1)}, f32[64,2304]{1,0:T(8,128)S(1)}, u32[]{:S(2)}, u32[]{:S(2)}) collective-permute-start(f32[64,2304]{1,0:T(8,128)S(1)} %get-tuple-element.15), channel_id=1, source_target_pairs={{0,4},{4,0},{8,12},{12,8},{16,20},{20,16},{24,28},{28,24},{1,5},{5... | collective-permute-start | bytes 1769480 | tf_op jit(solution)/shard_map/ppermute | solution.py:18
  8.7 26.1 %collective-permute-start.6 = (f32[64,2304]{1,0:T(8,128)S(1)}, f32[64,2304]{1,0:T(8,128)S(1)}, u32[]{:S(2)}, u32[]{:S(2)}) collective-permute-start(f32[64,2304]{1,0:T(8,128)S(1)} %get-tuple-element.15), channel_id=1, source_target_pairs={{4,8},{8,4},{12,16},{16,12},{20,24},{24,20},{28,0},{0,28},{5,9},{9... | collective-permute-start | bytes 1769480 | tf_op jit(solution)/shard_map/ppermute | solution.py:22
  16.0 30.7 %collective-permute-start.1 = (f32[64,2304]{1,0:T(8,128)S(1)}, f32[64,2304]{1,0:T(8,128)S(1)}, u32[]{:S(2)}, u32[]{:S(2)}) collective-permute-start(f32[64,2304]{1,0:T(8,128)S(1)} %collective-permute-done), channel_id=1, source_target_pairs={{4,8},{8,4},{12,16},{16,12},{20,24},{24,20},{28,0},{0,28},{5,9},{9... | collective-permute-start | bytes 1769480 | tf_op jit(solution)/shard_map/ppermute | solution.py:22
  28.7 30.7 %collective-permute-start.8 = (f32[64,2304]{1,0:T(8,128)S(1)}, f32[64,2304]{1,0:T(8,128)S(1)}, u32[]{:S(2)}, u32[]{:S(2)}) collective-permute-start(f32[64,2304]{1,0:T(8,128)S(1)} %collective-permute-done.4.refs_1_), channel_id=1, source_target_pairs={{4,8},{8,4},{12,16},{16,12},{20,24},{24,20},{28,0},{0,28},{5,9},{9... | collective-permute-start | bytes 1769480 | tf_op jit(solution)/shard_map/ppermute | solution.py:22
  34.8 12.0 %collective-permute-start.10 = (f32[48,2304]{1,0:T(8,128)S(1)}, f32[48,2304]{1,0:T(8,128)S(1)}, u32[]{:S(2)}, u32[]{:S(2)}) collective-permute-start(f32[48,2304]{1,0:T(8,128)S(1)} %slice.24), channel_id=1, source_target_pairs={{0,4},{4,0},{8,12},{12,8},{16,20},{20,16},{24,28},{28,24},{1,5},{5... | collective-permute-start | bytes 1327112 | tf_op jit(solution)/shard_map/ppermute | solution.py:18
  34.8 24.5 %collective-permute-start.7 = (f32[64,2304]{1,0:T(8,128)S(1)}, f32[64,2304]{1,0:T(8,128)S(1)}, u32[]{:S(2)}, u32[]{:S(2)}) collective-permute-start(f32[64,2304]{1,0:T(8,128)S(1)} %collective-permute-done.6), channel_id=1, source_target_pairs={{0,4},{4,0},{8,12},{12,8},{16,20},{20,16},{24,28},{28,24},{1,5},{5... | collective-permute-start | bytes 1769480 | tf_op jit(solution)/shard_map/ppermute | solution.py:18
  46.7 23.2 %collective-permute-start.2 = (f32[64,2304]{1,0:T(8,128)S(1)}, f32[64,2304]{1,0:T(8,128)S(1)}, u32[]{:S(2)}, u32[]{:S(2)}) collective-permute-start(f32[64,2304]{1,0:T(8,128)S(1)} %collective-permute-done.1), channel_id=1, source_target_pairs={{0,4},{4,0},{8,12},{12,8},{16,20},{20,16},{24,28},{28,24},{1,5},{5... | collective-permute-start | bytes 1769480 | tf_op jit(solution)/shard_map/ppermute | solution.py:18
  59.4 26.4 %collective-permute-start.11 = (f32[80,2304]{1,0:T(8,128)S(1)}, f32[80,2304]{1,0:T(8,128)S(1)}, u32[]{:S(2)}, u32[]{:S(2)}) collective-permute-start(f32[80,2304]{1,0:T(8,128)S(1)} %slice.25), channel_id=1, source_target_pairs={{0,4},{4,0},{8,12},{12,8},{16,20},{20,16},{24,28},{28,24},{1,5},{5... | collective-permute-start | bytes 2211848 | tf_op jit(solution)/shard_map/ppermute | solution.py:18
  59.4 14.6 %collective-permute-start.9 = (f32[64,2304]{1,0:T(8,128)S(1)}, f32[64,2304]{1,0:T(8,128)S(1)}, u32[]{:S(2)}, u32[]{:S(2)}) collective-permute-start(f32[64,2304]{1,0:T(8,128)S(1)} %collective-permute-done.7.refs_3_.refs_0_), channel_id=1, source_target_pairs={{4,8},{8,4},{12,16},{16,12},{20,24},{24,20},{28,0},{0,28},{5,9},{9... | collective-permute-start | bytes 1769480 | tf_op jit(solution)/shard_map/ppermute | solution.py:22
  69.9 15.8 %collective-permute-start.3 = (f32[64,2304]{1,0:T(8,128)S(1)}, f32[64,2304]{1,0:T(8,128)S(1)}, u32[]{:S(2)}, u32[]{:S(2)}) collective-permute-start(f32[64,2304]{1,0:T(8,128)S(1)} %collective-permute-done.2.refs_6_.refs_1_), channel_id=1, source_target_pairs={{4,8},{8,4},{12,16},{16,12},{20,24},{24,20},{28,0},{0,28},{5,9},{9... | collective-permute-start | bytes 1769480 | tf_op jit(solution)/shard_map/ppermute | solution.py:22
  89.3 4.5 %collective-permute-start.12 = (f32[2,4,64,128]{3,2,1,0:T(8,128)S(1)}, f32[2,4,64,128]{3,2,1,0:T(8,128)S(1)}, u32[]{:S(2)}, u32[]{:S(2)}) collective-permute-start(f32[2,4,64,128]{3,2,1,0:T(8,128)S(1)} %get-tuple-element.22), channel_id=1, source_target_pairs={{0,32},{32,0},{1,33},{33,1},{2,34},{34,2},{3,35},{35,3},{4,36},{36... | collective-permute-start | bytes 786440 | tf_op jit(solution)/shard_map/ppermute | solution.py:169

commit v7 on v6

--- a/solution.py
+++ b/solution.py
@@ -94,47 +94,70 @@
     )(*blocks)
 
 
-def finish(last, b, before, stack, distances, pair_b):
-    rows = last.shape[0]
-
-    def kernel(last_ref, b_ref, high, low, *refs):
-        pair_refs, old, mine, other = refs[:-3], refs[-3], refs[-2], refs[-1]
+def multiply_pair(stack, distances, b, pair_b, before):
+    rows = before.shape[-2]
+
+    def kernel(high, low, b_ref, *refs):
+        pair_refs, old, out, both = refs[:-3], refs[-3], refs[-2], refs[-1]
+        odd = lax.axis_index("zlo")
+        level = lax.axis_index("zhi") * 2 + odd
+        right = jnp.concatenate([ref[...] for ref in pair_refs], axis=0).T
+        both[...] = jnp.concatenate([b_ref[...], right], axis=1)
+        terms = jnp.concatenate(split(right), axis=1)
+        width = right.shape[1]
+        product = jnp.dot(high[...], terms, preferred_element_type=jnp.float32)
+        product = product[:, :width] + (
+            product[:, width:]
+            + jnp.dot(low[...], terms[:, :width], preferred_element_type=jnp.float32)
+        )
+        out[...] = old[...]
+        for i, distance in enumerate(distances):
+            source = row_level(level, distance)
+            block = product[i * rows : (i + 1) * rows]
+            out[lax.rem(source, 2), 1 - odd, source // 2] = 0.5 * block
+
+    return pl.pallas_call(
+        kernel,
+        out_shape=[
+            jax.ShapeDtypeStruct(before.shape, jnp.float32),
+            jax.ShapeDtypeStruct((b.shape[0], 2 * b.shape[1]), jnp.float32),
+        ],
+        in_specs=[VMEM] * (4 + len(pair_b)),
+        out_specs=[VMEM] * 2,
+        input_output_aliases={3 + len(pair_b): 0},
+        compiler_params=pltpu.CompilerParams(vmem_limit_bytes=24 * 1024 * 1024),
+    )(*stack, b, *pair_b, before)
+
+
+def finish(last, both, before):
+    def kernel(last_ref, both_ref, old, mine, other):
         core, odd = lax.axis_index("core"), lax.axis_index("zlo")
         level = lax.axis_index("zhi") * 2 + odd
-        mine[odd] = old[core, odd]
-        other[odd] = old[1 - core, odd]
-
-        def store(column, distance, product):
-            source = row_level(level, distance)
-
-            @pl.when(lax.rem(source, 2) == core)
-            def _():
-                mine[column, source // 2] = product
-
-            @pl.when(lax.rem(source, 2) != core)
-            def _():
-                other[column, source // 2] = product
-
-        block = last_ref[...]
-        store(odd, LEVELS // 2, dot(block, b_ref[...]))
-        b_high, b_low = split(jnp.concatenate([ref[...] for ref in pair_refs], axis=0).T)
-
-        def product(a_high, a_low):
-            terms = [(a_low, b_high), (a_high, b_low), (a_high, b_high)]
-            return 0.5 * sum(jnp.dot(*t, preferred_element_type=jnp.float32) for t in terms)
-
-        early = product(high[...], low[...])
-        for i, distance in enumerate(distances):
-            store(1 - odd, distance, early[i * rows : (i + 1) * rows])
-        store(1 - odd, LEVELS // 2, product(*split(block)))
+        mine[...] = old[core]
+        other[...] = old[1 - core]
+        product = dot(last_ref[...], both_ref[...])
+        width = product.shape[1] // 2
+        source = row_level(level, LEVELS // 2)
+
+        def store(out):
+            out[odd, source // 2] = product[:, :width]
+            out[1 - odd, source // 2] = product[:, width:]
+
+        @pl.when(lax.rem(source, 2) == core)
+        def _():
+            store(mine)
+
+        @pl.when(lax.rem(source, 2) != core)
+        def _():
+            store(other)
 
     return pl.pallas_call(
         kernel,
         out_shape=[jax.ShapeDtypeStruct(before.shape[1:], jnp.float32)] * 2,
-        in_specs=[VMEM] * (5 + len(pair_b)),
+        in_specs=[VMEM] * 3,
         out_specs=[VMEM] * 2,
         compiler_params=pltpu.CompilerParams(vmem_limit_bytes=24 * 1024 * 1024),
-    )(last, b, *stack, *pair_b, before)
+    )(last, both, before)
 
 
 def on_device(amplitudes, integrals):
@@ -153,10 +176,12 @@
     far_1, far_2 = swap_1(a_own), swap_2(a_other)
     a_1, a_2 = swap_1(a_other), swap_2(a_own)
     a_3, far_3 = swap_1(far_2), swap_2(far_1)
-    b_early, a_1_on = after((a_1, a_2), b_other[:EARLY], a_1)
-    pair_early, a_4 = swap_1(b_early), swap_2(a_1_on)
+    pair_early = swap_1(b_other[:EARLY])
+    (a_1_on,) = after((a_2,), a_1)
+    (far_3,) = after((pair_early,), far_3)
+    a_4 = swap_2(a_1_on)
     a_5, a_6 = swap_1(far_3), swap_2(a_3)
-    (b_late,) = after((pair_early, a_4), b_other[EARLY:])
+    (b_late,) = after((a_4,), b_other[EARLY:])
     a_7, pair_late = swap_2(a_5), swap_1(b_late)
 
     b = transposed(b_own)
@@ -165,7 +190,8 @@
     for part in (slice(0, 3), slice(3, 5), slice(5, 7)):
         product = multiply(early[part], distances[part], b, product)
     pair_b = [pair_early, pair_late]
-    mine, other = finish(a_7, b, product, split_stack(early), distances, pair_b)
+    product, both = multiply_pair(split_stack(early), distances, b, pair_b, product)
+    mine, other = finish(a_7, both, product)
     product = mine + lax.ppermute(other, "core", [(0, 1), (1, 0)])
 
     axes = ("zlo", "x", "layer")

time: 109 us -> 107 us (0.982)
  waiting for transfers between devices: 54.1 us -> 52.5 us
    ppermute x6, waiting for transfers between devices: 29.9 us -> 18 us  [swap_1(): return lax.ppermute(array, COL, SWAP_1)]
    ppermute x6, waiting for transfers between devices: 23 us -> 33.3 us  [swap_2(): return lax.ppermute(array, COL, SWAP_2)]
    ppermute x6, starting transfers between devices: 21 us -> 23.5 us  [swap_2(): return lax.ppermute(array, COL, SWAP_2)]
    pallas_call x1, Pallas kernels: 3.53 us -> 1.43 us  [finish(): pl.pallas_call(kernel, out_shape=[jax.ShapeDtypeStruct(before.shape[1:],...]
    ppermute x6, starting transfers between devices: 4.03 us -> 2.66 us  [swap_1(): return lax.ppermute(array, COL, SWAP_1)]
    pallas_call x0 -> x1, Pallas kernels: none -> 1.36 us  [multiply_pair(): pl.pallas_call(kernel, out_shape=[jax.ShapeDtypeStruct(before.shape, jnp....]
  transfers between devices with their start and end apart: 13 -> 13, of which waited for: 7 -> 11; matrix products, arithmetic and copies ran while one was open for 0% -> 0% of each run, Pallas kernels for 5% -> 7%
where the time goes in v7:
time: 107 us
  waiting for transfers between devices  52.5 us (49%)
  starting transfers between devices  28.7 us (27%)
  blocking collectives  14.8 us (14%)
  Pallas kernels  8.67 us (8%)
  other arithmetic  2.3 us (2%)
    ppermute x6, waiting for transfers between devices, swap_2(): return lax.ppermute(array, COL, SWAP_2)  33.3 us
    ppermute x6, starting transfers between devices, swap_2(): return lax.ppermute(array, COL, SWAP_2)  23.5 us
    ppermute x6, waiting for transfers between devices, swap_1(): return lax.ppermute(array, COL, SWAP_1)  18 us
    all_to_all x1, blocking collectives, on_device(): return lax.all_to_all(blocks, axes, 0, 0).sum(0)  14.8 us
    pallas_call x3, Pallas kernels, multiply(): pl.pallas_call(kernel, out_shape=jax.ShapeDtypeStruct(before.shape, jnp.f...  4.76 us
    ppermute x6, starting transfers between devices, swap_1(): return lax.ppermute(array, COL, SWAP_1)  2.66 us
    ppermute x1, starting transfers between devices, on_device(): product = mine + lax.ppermute(other, 'core', [(0, 1), (1, 0)])  2.56 us
  transfers between devices with their start and end apart: 13, of which 11 were waited for; matrix products, arithmetic and copies ran while one was open for 0% of the time, Pallas kernels for 7%

profile of v7, /device:TPU:1, one launch (start us, length us, event | category | flops | bytes accessed | tf_op | source)
XLA Modules:
  0.0 107.1 jit_solution(2645246133718642660)
XLA Ops:
  0.0 0.0 copy-start
  0.0 1.5 %slice_select_fusion.2 = (f32[64,2304]{1,0:T(8,128)S(1)}, f32[64,2304]{1,0:T(8,128)S(1)}) fusion(f32[64,4608]{1,0:T(8,128)} %param.2, pred[]{:T(512)S(6)} %eq.4), kind=kLoop, calls=%fused_computation.2 | loop fusion | flops 294912 | bytes 2359297 | tf_op jit(solution)/shard_map/jit(_where)/select_n | solution.py:171
  1.5 2.6 %collective-permute-start = (f32[64,2304]{1,0:T(8,128)S(1)}, f32[64,2304]{1,0:T(8,128)S(1)}, u32[]{:S(2)}, u32[]{:S(2)}) collective-permute-start(f32[64,2304]{1,0:T(8,128)S(1)} %get-tuple-element.16.refs_0_), channel_id=1, source_target_pairs={{0,4},{4,0},{8,12},{12,8},{16,20},{20,16},{24,28},{28,24},{1,5},{5... | collective-permute-start | bytes 1769480 | tf_op jit(solution)/shard_map/ppermute | solution.py:18
  4.0 4.7 %collective-permute-start.7 = (f32[64,2304]{1,0:T(8,128)S(1)}, f32[64,2304]{1,0:T(8,128)S(1)}, u32[]{:S(2)}, u32[]{:S(2)}) collective-permute-start(f32[64,2304]{1,0:T(8,128)S(1)} %get-tuple-element.18), channel_id=1, source_target_pairs={{4,8},{8,4},{12,16},{16,12},{20,24},{24,20},{28,0},{0,28},{5,9},{9... | collective-permute-start | bytes 1769480 | tf_op jit(solution)/shard_map/ppermute | solution.py:22
  8.7 0.0 collective-permute-start.5
  8.7 1.5 %collective-permute-start.6 = (f32[64,2304]{1,0:T(8,128)S(1)}, f32[64,2304]{1,0:T(8,128)S(1)}, u32[]{:S(2)}, u32[]{:S(2)}) collective-permute-start(f32[64,2304]{1,0:T(8,128)S(1)} %get-tuple-element.16.refs_0_), channel_id=1, source_target_pairs={{4,8},{8,4},{12,16},{16,12},{20,24},{24,20},{28,0},{0,28},{5,9},{9... | collective-permute-start | bytes 1769480 | tf_op jit(solution)/shard_map/ppermute | solution.py:22
  10.2 5.9 %collective-permute-done = f32[64,2304]{1,0:T(8,128)S(1)} collective-permute-done((f32[64,2304]{1,0:T(8,128)S(1)}, f32[64,2304]{1,0:T(8,128)S(1)}, u32[]{:S(2)}, u32[]{:S(2)}) %collective-permute-start) | collective-permute-done | bytes 589856 | tf_op jit(solution)/shard_map/ppermute | solution.py:18
  16.0 6.1 %collective-permute-start.1 = (f32[64,2304]{1,0:T(8,128)S(1)}, f32[64,2304]{1,0:T(8,128)S(1)}, u32[]{:S(2)}, u32[]{:S(2)}) collective-permute-start(f32[64,2304]{1,0:T(8,128)S(1)} %collective-permute-done), channel_id=1, source_target_pairs={{4,8},{8,4},{12,16},{16,12},{20,24},{24,20},{28,0},{0,28},{5,9},{9... | collective-permute-start | bytes 1769480 | tf_op jit(solution)/shard_map/ppermute | solution.py:22
  22.2 0.0 copy-done
  22.2 0.2 slice_select_fusion
  22.4 0.1 collective-permute-start.2
  22.5 6.2 %collective-permute-done.5.refs_1_ = f32[64,2304]{1,0:T(8,128)S(1)} collective-permute-done((f32[64,2304]{1,0:T(8,128)S(1)}, f32[64,2304]{1,0:T(8,128)S(1)}, u32[]{:S(2)}, u32[]{:S(2)}) %collective-permute-start.5) | collective-permute-done | bytes 589856 | tf_op jit(solution)/shard_map/ppermute | solution.py:18
  28.7 5.4 %collective-permute-done.6.refs_2_ = f32[64,2304]{1,0:T(8,128)S(1)} collective-permute-done((f32[64,2304]{1,0:T(8,128)S(1)}, f32[64,2304]{1,0:T(8,128)S(1)}, u32[]{:S(2)}, u32[]{:S(2)}) %collective-permute-start.6) | collective-permute-done | bytes 589856 | tf_op jit(solution)/shard_map/ppermute | solution.py:22
  34.1 2.4 %collective-permute-start.9 = (f32[64,2304]{1,0:T(8,128)S(1)}, f32[64,2304]{1,0:T(8,128)S(1)}, u32[]{:S(2)}, u32[]{:S(2)}) collective-permute-start(f32[64,2304]{1,0:T(8,128)S(1)} %collective-permute-done.5.refs_1_), channel_id=1, source_target_pairs={{4,8},{8,4},{12,16},{16,12},{20,24},{24,20},{28,0},{0,28},{5,9},{9... | collective-permute-start | bytes 1769480 | tf_op jit(solution)/shard_map/ppermute | solution.py:22
  36.4 0.0 collective-permute-done.7
  36.4 0.0 collective-permute-start.8
  36.4 1.7 %collective-permute-done.2.refs_0_ = f32[48,2304]{1,0:T(8,128)S(1)} collective-permute-done((f32[48,2304]{1,0:T(8,128)S(1)}, f32[48,2304]{1,0:T(8,128)S(1)}, u32[]{:S(2)}, u32[]{:S(2)}) %collective-permute-start.2) | collective-permute-done | bytes 442400 | tf_op jit(solution)/shard_map/ppermute | solution.py:18
  38.1 8.6 %collective-permute-done.1 = f32[64,2304]{1,0:T(8,128)S(1)} collective-permute-done((f32[64,2304]{1,0:T(8,128)S(1)}, f32[64,2304]{1,0:T(8,128)S(1)}, u32[]{:S(2)}, u32[]{:S(2)}) %collective-permute-start.1) | collective-permute-done | bytes 589856 | tf_op jit(solution)/shard_map/ppermute | solution.py:22
  46.7 0.0 collective-permute-start.3
  46.8 12.6 %collective-permute-done.9.refs_4_.refs_1_ = f32[64,2304]{1,0:T(8,128)S(1)} collective-permute-done((f32[64,2304]{1,0:T(8,128)S(1)}, f32[64,2304]{1,0:T(8,128)S(1)}, u32[]{:S(2)}, u32[]{:S(2)}) %collective-permute-start.9) | collective-permute-done | bytes 589856 | tf_op jit(solution)/shard_map/ppermute | solution.py:22
  59.4 0.0 collective-permute-start.11
  59.4 0.0 collective-permute-done.8.refs_3_.refs_0_
  59.4 2.4 %collective-permute-start.10 = (f32[64,2304]{1,0:T(8,128)S(1)}, f32[64,2304]{1,0:T(8,128)S(1)}, u32[]{:S(2)}, u32[]{:S(2)}) collective-permute-start(f32[64,2304]{1,0:T(8,128)S(1)} %collective-permute-done.8.refs_3_.refs_0_), channel_id=1, source_target_pairs={{4,8},{8,4},{12,16},{16,12},{20,24},{24,20},{28,0},{0,28},{5,9},{9... | collective-permute-start | bytes 1769480 | tf_op jit(solution)/shard_map/ppermute | solution.py:22
  61.7 1.4 %collective-permute-done.3.refs_6_.refs_1_ = f32[64,2304]{1,0:T(8,128)S(1)} collective-permute-done((f32[64,2304]{1,0:T(8,128)S(1)}, f32[64,2304]{1,0:T(8,128)S(1)}, u32[]{:S(2)}, u32[]{:S(2)}) %collective-permute-start.3) | collective-permute-done | bytes 589856 | tf_op jit(solution)/shard_map/ppermute | solution.py:18
  63.1 6.5 %collective-permute-start.4 = (f32[64,2304]{1,0:T(8,128)S(1)}, f32[64,2304]{1,0:T(8,128)S(1)}, u32[]{:S(2)}, u32[]{:S(2)}) collective-permute-start(f32[64,2304]{1,0:T(8,128)S(1)} %collective-permute-done.3.refs_6_.refs_1_), channel_id=1, source_target_pairs={{4,8},{8,4},{12,16},{16,12},{20,24},{24,20},{28,0},{0,28},{5,9},{9... | collective-permute-start | bytes 1769480 | tf_op jit(solution)/shard_map/ppermute | solution.py:22
  69.6 0.4 shard_map.29.refs_3_.refs_2_.b_ref
  70.0 2.0 %shard_map.30.refs_3_ = f32[2,2,4,64,128]{4,3,2,1,0:T(8,128)S(1)} custom-call(f32[64,2304]{1,0:T(8,128)S(1)} %get-tuple-element.16.refs_0_, f32[64,2304]{1,0:T(8,128)S(1)} %collective-permute-done.5.refs_1_, f32[64,2304]{1,0:T(8,128)S(1)} %collective-permute-done.6.refs_2_, ...), custom_call_target="tpu_custom_call", output_to_operand_aliasing={{}: (4, {})} | custom-call | tf_op jit(solution)/shard_map/pallas_call | solution.py:64
  72.0 1.4 %shard_map.31.refs_3_ = f32[2,2,4,64,128]{4,3,2,1,0:T(8,128)S(1)} custom-call(f32[64,2304]{1,0:T(8,128)S(1)} %collective-permute-done.8.refs_3_.refs_0_, f32[64,2304]{1,0:T(8,128)S(1)} %collective-permute-done.9.refs_4_.refs_1_, f32[2304,128]{1,0:T(8,128)S(1)} %shard_map.29.refs_3_.refs_2_.b_ref, ...), custom_call_target="tpu_custom_call", output_to_operand_aliasing={{}: (3, {})} | custom-call | tf_op jit(solution)/shard_map/pallas_call | solution.py:64
  73.4 0.5 collective-permute-done.10.refs_5_.refs_0_
  73.8 0.8 shard_map.28
  74.6 1.4 %shard_map.32.refs_2_ = f32[2,2,4,64,128]{4,3,2,1,0:T(8,128)S(1)} custom-call(f32[64,2304]{1,0:T(8,128)S(1)} %collective-permute-done.10.refs_5_.refs_0_, f32[64,2304]{1,0:T(8,128)S(1)} %collective-permute-done.3.refs_6_.refs_1_, f32[2304,128]{1,0:T(8,128)S(1)} %shard_map.29.refs_3_.refs_2_.b_ref, ...), custom_call_target="tpu_custom_call", output_to_operand_aliasing={{}: (3, {})} | custom-call | tf_op jit(solution)/shard_map/pallas_call | solution.py:64
  76.0 2.9 %collective-permute-done.11.refs_1_ = f32[80,2304]{1,0:T(8,128)S(1)} collective-permute-done((f32[80,2304]{1,0:T(8,128)S(1)}, f32[80,2304]{1,0:T(8,128)S(1)}, u32[]{:S(2)}, u32[]{:S(2)}) %collective-permute-start.11) | collective-permute-done | bytes 737312 | tf_op jit(solution)/shard_map/ppermute | solution.py:18
  78.9 1.4 %shard_map.33 = (f32[2,2,4,64,128]{4,3,2,1,0:T(8,128)S(1)}, f32[2304,256]{1,0:T(8,128)S(1)}) custom-call(bf16[448,2304]{1,0:T(8,128)(2,1)S(1)} %get-tuple-element.20.high, bf16[448,2304]{1,0:T(8,128)(2,1)S(1)} %get-tuple-element.21.low, f32[2304,128]{1,0:T(8,128)S(1)} %shard_map.29.refs_3_.refs_2_.b_ref, ...), custom_call_target="tpu_custom_call", output_to_operand_aliasing={{0}: (5, {})} | custom-call | tf_op jit(solution)/shard_map/pallas_call | solution.py:119
  80.2 6.2 %collective-permute-done.4.last_ref = f32[64,2304]{1,0:T(8,128)S(1)} collective-permute-done((f32[64,2304]{1,0:T(8,128)S(1)}, f32[64,2304]{1,0:T(8,128)S(1)}, u32[]{:S(2)}, u32[]{:S(2)}) %collective-permute-start.4) | collective-permute-done | bytes 589856 | tf_op jit(solution)/shard_map/ppermute | solution.py:22
  86.5 1.4 %shard_map.34 = (f32[2,4,64,128]{3,2,1,0:T(8,128)S(1)}, f32[2,4,64,128]{3,2,1,0:T(8,128)S(1)}) custom-call(f32[64,2304]{1,0:T(8,128)S(1)} %collective-permute-done.4.last_ref, f32[2304,256]{1,0:T(8,128)S(1)} %get-tuple-element.23.both_ref, f32[2,2,4,64,128]{4,3,2,1,0:T(8,128)S(1)} %get-tuple-element.24.old), custom_call_target="tpu_custom_call" | custom-call | tf_op jit(solution)/shard_map/pallas_call | solution.py:154
  87.9 2.6 %collective-permute-start.12 = (f32[2,4,64,128]{3,2,1,0:T(8,128)S(1)}, f32[2,4,64,128]{3,2,1,0:T(8,128)S(1)}, u32[]{:S(2)}, u32[]{:S(2)}) collective-permute-start(f32[2,4,64,128]{3,2,1,0:T(8,128)S(1)} %get-tuple-element.26), channel_id=1, source_target_pairs={{0,32},{32,0},{1,33},{33,1},{2,34},{34,2},{3,35},{35,3},{4,36},{36... | collective-permute-start | bytes 786440 | tf_op jit(solution)/shard_map/ppermute | solution.py:195
  90.5 1.2 %collective-permute-done.12 = f32[2,4,64,128]{3,2,1,0:T(8,128)S(1)} collective-permute-done((f32[2,4,64,128]{3,2,1,0:T(8,128)S(1)}, f32[2,4,64,128]{3,2,1,0:T(8,128)S(1)}, u32[]{:S(2)}, u32[]{:S(2)}) %collective-permute-start.12) | collective-permute-done | bytes 262176 | tf_op jit(solution)/shard_map/ppermute | solution.py:195
  91.7 14.8 %all_to_all.5 = f32[32,16,128]{2,1,0:T(8,128)S(1)} all-to-all(f32[32,16,128]{2,1,0:T(8,128)S(1)} %bitcast.1), channel_id=1, replica_groups=mesh['x'=4,'core'=2,'zhi'=4,'zlo'=2,'layer'=4] {'zlo','x','layer'}, dimensions={0} | all-to-all | bytes 524288 | tf_op jit(solution)/shard_map/all_to_all | solution.py:199
  106.5 0.6 reduce_sum.9
  (4 shorter events, 0.2 us)
Async XLA Ops:
  0.0 22.2 %copy-start = (f32[128,4608]{1,0:T(8,128)S(1)}, f32[128,4608]{1,0:T(8,128)}, u32[]{:S(2)}) copy-start(f32[128,4608]{1,0:T(8,128)} %param.3) | copy-start | bytes 7077892
  1.5 14.6 %collective-permute-start = (f32[64,2304]{1,0:T(8,128)S(1)}, f32[64,2304]{1,0:T(8,128)S(1)}, u32[]{:S(2)}, u32[]{:S(2)}) collective-permute-start(f32[64,2304]{1,0:T(8,128)S(1)} %get-tuple-element.16.refs_0_), channel_id=1, source_target_pairs={{0,4},{4,0},{8,12},{12,8},{16,20},{20,16},{24,28},{28,24},{1,5},{5... | collective-permute-start | bytes 1769480 | tf_op jit(solution)/shard_map/ppermute | solution.py:18
  4.0 32.4 %collective-permute-start.7 = (f32[64,2304]{1,0:T(8,128)S(1)}, f32[64,2304]{1,0:T(8,128)S(1)}, u32[]{:S(2)}, u32[]{:S(2)}) collective-permute-start(f32[64,2304]{1,0:T(8,128)S(1)} %get-tuple-element.18), channel_id=1, source_target_pairs={{4,8},{8,4},{12,16},{16,12},{20,24},{24,20},{28,0},{0,28},{5,9},{9... | collective-permute-start | bytes 1769480 | tf_op jit(solution)/shard_map/ppermute | solution.py:22
  8.7 20.0 %collective-permute-start.5 = (f32[64,2304]{1,0:T(8,128)S(1)}, f32[64,2304]{1,0:T(8,128)S(1)}, u32[]{:S(2)}, u32[]{:S(2)}) collective-permute-start(f32[64,2304]{1,0:T(8,128)S(1)} %get-tuple-element.18), channel_id=1, source_target_pairs={{0,4},{4,0},{8,12},{12,8},{16,20},{20,16},{24,28},{28,24},{1,5},{5... | collective-permute-start | bytes 1769480 | tf_op jit(solution)/shard_map/ppermute | solution.py:18
  8.7 25.4 %collective-permute-start.6 = (f32[64,2304]{1,0:T(8,128)S(1)}, f32[64,2304]{1,0:T(8,128)S(1)}, u32[]{:S(2)}, u32[]{:S(2)}) collective-permute-start(f32[64,2304]{1,0:T(8,128)S(1)} %get-tuple-element.16.refs_0_), channel_id=1, source_target_pairs={{4,8},{8,4},{12,16},{16,12},{20,24},{24,20},{28,0},{0,28},{5,9},{9... | collective-permute-start | bytes 1769480 | tf_op jit(solution)/shard_map/ppermute | solution.py:22
  16.0 30.7 %collective-permute-start.1 = (f32[64,2304]{1,0:T(8,128)S(1)}, f32[64,2304]{1,0:T(8,128)S(1)}, u32[]{:S(2)}, u32[]{:S(2)}) collective-permute-start(f32[64,2304]{1,0:T(8,128)S(1)} %collective-permute-done), channel_id=1, source_target_pairs={{4,8},{8,4},{12,16},{16,12},{20,24},{24,20},{28,0},{0,28},{5,9},{9... | collective-permute-start | bytes 1769480 | tf_op jit(solution)/shard_map/ppermute | solution.py:22
  22.4 15.8 %collective-permute-start.2 = (f32[48,2304]{1,0:T(8,128)S(1)}, f32[48,2304]{1,0:T(8,128)S(1)}, u32[]{:S(2)}, u32[]{:S(2)}) collective-permute-start(f32[48,2304]{1,0:T(8,128)S(1)} %slice.24), channel_id=1, source_target_pairs={{0,4},{4,0},{8,12},{12,8},{16,20},{20,16},{24,28},{28,24},{1,5},{5... | collective-permute-start | bytes 1327112 | tf_op jit(solution)/shard_map/ppermute | solution.py:18
  34.1 25.3 %collective-permute-start.9 = (f32[64,2304]{1,0:T(8,128)S(1)}, f32[64,2304]{1,0:T(8,128)S(1)}, u32[]{:S(2)}, u32[]{:S(2)}) collective-permute-start(f32[64,2304]{1,0:T(8,128)S(1)} %collective-permute-done.5.refs_1_), channel_id=1, source_target_pairs={{4,8},{8,4},{12,16},{16,12},{20,24},{24,20},{28,0},{0,28},{5,9},{9... | collective-permute-start | bytes 1769480 | tf_op jit(solution)/shard_map/ppermute | solution.py:22
  36.4 22.9 %collective-permute-start.8 = (f32[64,2304]{1,0:T(8,128)S(1)}, f32[64,2304]{1,0:T(8,128)S(1)}, u32[]{:S(2)}, u32[]{:S(2)}) collective-permute-start(f32[64,2304]{1,0:T(8,128)S(1)} %collective-permute-done.7), channel_id=1, source_target_pairs={{0,4},{4,0},{8,12},{12,8},{16,20},{20,16},{24,28},{28,24},{1,5},{5... | collective-permute-start | bytes 1769480 | tf_op jit(solution)/shard_map/ppermute | solution.py:18
  46.7 16.4 %collective-permute-start.3 = (f32[64,2304]{1,0:T(8,128)S(1)}, f32[64,2304]{1,0:T(8,128)S(1)}, u32[]{:S(2)}, u32[]{:S(2)}) collective-permute-start(f32[64,2304]{1,0:T(8,128)S(1)} %collective-permute-done.1), channel_id=1, source_target_pairs={{0,4},{4,0},{8,12},{12,8},{16,20},{20,16},{24,28},{28,24},{1,5},{5... | collective-permute-start | bytes 1769480 | tf_op jit(solution)/shard_map/ppermute | solution.py:18
  59.4 19.5 %collective-permute-start.11 = (f32[80,2304]{1,0:T(8,128)S(1)}, f32[80,2304]{1,0:T(8,128)S(1)}, u32[]{:S(2)}, u32[]{:S(2)}) collective-permute-start(f32[80,2304]{1,0:T(8,128)S(1)} %slice.25), channel_id=1, source_target_pairs={{0,4},{4,0},{8,12},{12,8},{16,20},{20,16},{24,28},{28,24},{1,5},{5... | collective-permute-start | bytes 2211848 | tf_op jit(solution)/shard_map/ppermute | solution.py:18
  59.4 14.5 %collective-permute-start.10 = (f32[64,2304]{1,0:T(8,128)S(1)}, f32[64,2304]{1,0:T(8,128)S(1)}, u32[]{:S(2)}, u32[]{:S(2)}) collective-permute-start(f32[64,2304]{1,0:T(8,128)S(1)} %collective-permute-done.8.refs_3_.refs_0_), channel_id=1, source_target_pairs={{4,8},{8,4},{12,16},{16,12},{20,24},{24,20},{28,0},{0,28},{5,9},{9... | collective-permute-start | bytes 1769480 | tf_op jit(solution)/shard_map/ppermute | solution.py:22
  63.1 23.4 %collective-permute-start.4 = (f32[64,2304]{1,0:T(8,128)S(1)}, f32[64,2304]{1,0:T(8,128)S(1)}, u32[]{:S(2)}, u32[]{:S(2)}) collective-permute-start(f32[64,2304]{1,0:T(8,128)S(1)} %collective-permute-done.3.refs_6_.refs_1_), channel_id=1, source_target_pairs={{4,8},{8,4},{12,16},{16,12},{20,24},{24,20},{28,0},{0,28},{5,9},{9... | collective-permute-start | bytes 1769480 | tf_op jit(solution)/shard_map/ppermute | solution.py:22
  87.9 3.7 %collective-permute-start.12 = (f32[2,4,64,128]{3,2,1,0:T(8,128)S(1)}, f32[2,4,64,128]{3,2,1,0:T(8,128)S(1)}, u32[]{:S(2)}, u32[]{:S(2)}) collective-permute-start(f32[2,4,64,128]{3,2,1,0:T(8,128)S(1)} %get-tuple-element.26), channel_id=1, source_target_pairs={{0,32},{32,0},{1,33},{33,1},{2,34},{34,2},{3,35},{35,3},{4,36},{36... | collective-permute-start | bytes 786440 | tf_op jit(solution)/shard_map/ppermute | solution.py:195

commit v8 on v7

--- a/solution.py
+++ b/solution.py
@@ -71,62 +71,35 @@
     )(*blocks, b, before)
 
 
-def split(array):
-    high = array.astype(jnp.bfloat16)
-    return high, (array - high.astype(jnp.float32)).astype(jnp.bfloat16)
-
-
-def split_stack(blocks):
-    count, (rows, width) = len(blocks), blocks[0].shape
+def multiply_pair(blocks, distances, b, pair_b, before):
+    count, rows = len(blocks), before.shape[-2]
 
     def kernel(*refs):
-        high, low = refs[count:]
-        for i, ref in enumerate(refs[:count]):
-            place = slice(i * rows, (i + 1) * rows)
-            high[place, :], low[place, :] = split(ref[...])
-
-    return pl.pallas_call(
-        kernel,
-        out_shape=[jax.ShapeDtypeStruct((count * rows, width), jnp.bfloat16)] * 2,
-        in_specs=[VMEM] * count,
-        out_specs=[VMEM] * 2,
-        compiler_params=pltpu.CompilerParams(vmem_limit_bytes=24 * 1024 * 1024),
-    )(*blocks)
-
-
-def multiply_pair(stack, distances, b, pair_b, before):
-    rows = before.shape[-2]
-
-    def kernel(high, low, b_ref, *refs):
-        pair_refs, old, out, both = refs[:-3], refs[-3], refs[-2], refs[-1]
+        b_ref, pair_refs = refs[count], refs[count + 1 : -3]
+        old, out, both = refs[-3:]
         odd = lax.axis_index("zlo")
         level = lax.axis_index("zhi") * 2 + odd
         right = jnp.concatenate([ref[...] for ref in pair_refs], axis=0).T
         both[...] = jnp.concatenate([b_ref[...], right], axis=1)
-        terms = jnp.concatenate(split(right), axis=1)
-        width = right.shape[1]
-        product = jnp.dot(high[...], terms, preferred_element_type=jnp.float32)
-        product = product[:, :width] + (
-            product[:, width:]
-            + jnp.dot(low[...], terms[:, :width], preferred_element_type=jnp.float32)
-        )
+        product = dot(jnp.concatenate([ref[...] for ref in refs[:count]], axis=0), right)
         out[...] = old[...]
         for i, distance in enumerate(distances):
             source = row_level(level, distance)
             block = product[i * rows : (i + 1) * rows]
-            out[lax.rem(source, 2), 1 - odd, source // 2] = 0.5 * block
+            out[lax.rem(source, 2), 1 - odd, source // 2] = block
 
+    n_in = count + 1 + len(pair_b)
     return pl.pallas_call(
         kernel,
         out_shape=[
             jax.ShapeDtypeStruct(before.shape, jnp.float32),
             jax.ShapeDtypeStruct((b.shape[0], 2 * b.shape[1]), jnp.float32),
         ],
-        in_specs=[VMEM] * (4 + len(pair_b)),
+        in_specs=[VMEM] * (n_in + 1),
         out_specs=[VMEM] * 2,
-        input_output_aliases={3 + len(pair_b): 0},
-        compiler_params=pltpu.CompilerParams(vmem_limit_bytes=24 * 1024 * 1024),
-    )(*stack, b, *pair_b, before)
+        input_output_aliases={n_in: 0},
+        compiler_params=pltpu.CompilerParams(vmem_limit_bytes=32 * 1024 * 1024),
+    )(*blocks, b, *pair_b, before)
 
 
 def finish(last, both, before):
@@ -190,7 +163,7 @@
     for part in (slice(0, 3), slice(3, 5), slice(5, 7)):
         product = multiply(early[part], distances[part], b, product)
     pair_b = [pair_early, pair_late]
-    product, both = multiply_pair(split_stack(early), distances, b, pair_b, product)
+    product, both = multiply_pair(early, distances, b, pair_b, product)
     mine, other = finish(a_7, both, product)
     product = mine + lax.ppermute(other, "core", [(0, 1), (1, 0)])
 

time: 107 us -> 107 us (level)
  waiting for transfers between devices: 52.5 us -> 47.5 us
  starting transfers between devices: 28.7 us -> 32.1 us
  Pallas kernels: 8.67 us -> 10.1 us
    ppermute x6, waiting for transfers between devices: 33.3 us -> 25.3 us  [swap_2(): return lax.ppermute(array, COL, SWAP_2)]
    ppermute x6, starting transfers between devices: 23.5 us -> 26.9 us  [swap_2(): return lax.ppermute(array, COL, SWAP_2)]
    ppermute x6, waiting for transfers between devices: 18 us -> 21.1 us  [swap_1(): return lax.ppermute(array, COL, SWAP_1)]
    pallas_call x1, Pallas kernels: 1.36 us -> 3.6 us  [multiply_pair(): pl.pallas_call(kernel, out_shape=[jax.ShapeDtypeStruct(before.shape, jnp....]
  transfers between devices with their start and end apart: 13 -> 13, of which waited for: 11 -> 10; matrix products, arithmetic and copies ran while one was open for 0% -> 0% of each run, Pallas kernels for 7% -> 8%
where the time goes in v8:
time: 107 us
  waiting for transfers between devices  47.5 us (44%)
  starting transfers between devices  32.1 us (30%)
  blocking collectives  14.8 us (14%)
  Pallas kernels  10.1 us (9%)
  other arithmetic  2.3 us (2%)
    ppermute x6, starting transfers between devices, swap_2(): return lax.ppermute(array, COL, SWAP_2)  26.9 us
    ppermute x6, waiting for transfers between devices, swap_2(): return lax.ppermute(array, COL, SWAP_2)  25.3 us
    ppermute x6, waiting for transfers between devices, swap_1(): return lax.ppermute(array, COL, SWAP_1)  21.1 us
    all_to_all x1, blocking collectives, on_device(): return lax.all_to_all(blocks, axes, 0, 0).sum(0)  14.8 us
    pallas_call x3, Pallas kernels, multiply(): pl.pallas_call(kernel, out_shape=jax.ShapeDtypeStruct(before.shape, jnp.f...  4.76 us
    pallas_call x1, Pallas kernels, multiply_pair(): pl.pallas_call(kernel, out_shape=[jax.ShapeDtypeStruct(before.shape, jnp....  3.6 us
    ppermute x6, starting transfers between devices, swap_1(): return lax.ppermute(array, COL, SWAP_1)  2.66 us
    ppermute x1, starting transfers between devices, on_device(): product = mine + lax.ppermute(other, 'core', [(0, 1), (1, 0)])  2.56 us
  transfers between devices with their start and end apart: 13, of which 10 were waited for; matrix products, arithmetic and copies ran while one was open for 0% of the time, Pallas kernels for 8%

profile of v8, /device:TPU:1, one launch (start us, length us, event | category | flops | bytes accessed | tf_op | source)
XLA Modules:
  0.0 107.1 jit_solution(9130207647846819193)
XLA Ops:
  0.0 0.0 copy-start
  0.0 1.5 %slice_select_fusion.2 = (f32[64,2304]{1,0:T(8,128)S(1)}, f32[64,2304]{1,0:T(8,128)S(1)}) fusion(f32[64,4608]{1,0:T(8,128)} %param.2, pred[]{:T(512)S(6)} %eq.4), kind=kLoop, calls=%fused_computation.2 | loop fusion | flops 294912 | bytes 2359297 | tf_op jit(solution)/shard_map/jit(_where)/select_n | solution.py:144
  1.5 2.6 %collective-permute-start = (f32[64,2304]{1,0:T(8,128)S(1)}, f32[64,2304]{1,0:T(8,128)S(1)}, u32[]{:S(2)}, u32[]{:S(2)}) collective-permute-start(f32[64,2304]{1,0:T(8,128)S(1)} %get-tuple-element.14.refs_0_), channel_id=1, source_target_pairs={{0,4},{4,0},{8,12},{12,8},{16,20},{20,16},{24,28},{28,24},{1,5},{5... | collective-permute-start | bytes 1769480 | tf_op jit(solution)/shard_map/ppermute | solution.py:18
  4.0 4.7 %collective-permute-start.6 = (f32[64,2304]{1,0:T(8,128)S(1)}, f32[64,2304]{1,0:T(8,128)S(1)}, u32[]{:S(2)}, u32[]{:S(2)}) collective-permute-start(f32[64,2304]{1,0:T(8,128)S(1)} %get-tuple-element.14.refs_0_), channel_id=1, source_target_pairs={{4,8},{8,4},{12,16},{16,12},{20,24},{24,20},{28,0},{0,28},{5,9},{9... | collective-permute-start | bytes 1769480 | tf_op jit(solution)/shard_map/ppermute | solution.py:22
  8.7 0.0 collective-permute-start.5
  8.7 1.5 %collective-permute-start.7 = (f32[64,2304]{1,0:T(8,128)S(1)}, f32[64,2304]{1,0:T(8,128)S(1)}, u32[]{:S(2)}, u32[]{:S(2)}) collective-permute-start(f32[64,2304]{1,0:T(8,128)S(1)} %get-tuple-element.16), channel_id=1, source_target_pairs={{4,8},{8,4},{12,16},{16,12},{20,24},{24,20},{28,0},{0,28},{5,9},{9... | collective-permute-start | bytes 1769480 | tf_op jit(solution)/shard_map/ppermute | solution.py:22
  10.2 5.9 %collective-permute-done = f32[64,2304]{1,0:T(8,128)S(1)} collective-permute-done((f32[64,2304]{1,0:T(8,128)S(1)}, f32[64,2304]{1,0:T(8,128)S(1)}, u32[]{:S(2)}, u32[]{:S(2)}) %collective-permute-start) | collective-permute-done | bytes 589856 | tf_op jit(solution)/shard_map/ppermute | solution.py:18
  16.0 6.1 %collective-permute-start.1 = (f32[64,2304]{1,0:T(8,128)S(1)}, f32[64,2304]{1,0:T(8,128)S(1)}, u32[]{:S(2)}, u32[]{:S(2)}) collective-permute-start(f32[64,2304]{1,0:T(8,128)S(1)} %collective-permute-done), channel_id=1, source_target_pairs={{4,8},{8,4},{12,16},{16,12},{20,24},{24,20},{28,0},{0,28},{5,9},{9... | collective-permute-start | bytes 1769480 | tf_op jit(solution)/shard_map/ppermute | solution.py:22
  22.2 0.0 copy-done
  22.2 0.2 slice_select_fusion
  22.4 0.1 collective-permute-start.2
  22.5 6.2 %collective-permute-done.5.refs_1_ = f32[64,2304]{1,0:T(8,128)S(1)} collective-permute-done((f32[64,2304]{1,0:T(8,128)S(1)}, f32[64,2304]{1,0:T(8,128)S(1)}, u32[]{:S(2)}, u32[]{:S(2)}) %collective-permute-start.5) | collective-permute-done | bytes 589856 | tf_op jit(solution)/shard_map/ppermute | solution.py:18
  28.7 0.0 collective-permute-done.6.refs_2_
  28.7 6.1 %collective-permute-start.9 = (f32[64,2304]{1,0:T(8,128)S(1)}, f32[64,2304]{1,0:T(8,128)S(1)}, u32[]{:S(2)}, u32[]{:S(2)}) collective-permute-start(f32[64,2304]{1,0:T(8,128)S(1)} %collective-permute-done.5.refs_1_), channel_id=1, source_target_pairs={{4,8},{8,4},{12,16},{16,12},{20,24},{24,20},{28,0},{0,28},{5,9},{9... | collective-permute-start | bytes 1769480 | tf_op jit(solution)/shard_map/ppermute | solution.py:22
  34.8 0.0 collective-permute-done.7
  34.8 0.0 collective-permute-start.8
  34.8 3.3 %collective-permute-done.2.refs_8_ = f32[48,2304]{1,0:T(8,128)S(1)} collective-permute-done((f32[48,2304]{1,0:T(8,128)S(1)}, f32[48,2304]{1,0:T(8,128)S(1)}, u32[]{:S(2)}, u32[]{:S(2)}) %collective-permute-start.2) | collective-permute-done | bytes 442400 | tf_op jit(solution)/shard_map/ppermute | solution.py:18
  38.1 8.6 %collective-permute-done.1 = f32[64,2304]{1,0:T(8,128)S(1)} collective-permute-done((f32[64,2304]{1,0:T(8,128)S(1)}, f32[64,2304]{1,0:T(8,128)S(1)}, u32[]{:S(2)}, u32[]{:S(2)}) %collective-permute-start.1) | collective-permute-done | bytes 589856 | tf_op jit(solution)/shard_map/ppermute | solution.py:22
  46.7 0.0 collective-permute-start.3
  46.8 12.6 %collective-permute-done.9.refs_1_.refs_4_ = f32[64,2304]{1,0:T(8,128)S(1)} collective-permute-done((f32[64,2304]{1,0:T(8,128)S(1)}, f32[64,2304]{1,0:T(8,128)S(1)}, u32[]{:S(2)}, u32[]{:S(2)}) %collective-permute-start.9) | collective-permute-done | bytes 589856 | tf_op jit(solution)/shard_map/ppermute | solution.py:22
  59.4 0.0 collective-permute-start.11
  59.4 0.0 collective-permute-done.8.refs_0_.refs_3_
  59.4 2.4 %collective-permute-start.10 = (f32[64,2304]{1,0:T(8,128)S(1)}, f32[64,2304]{1,0:T(8,128)S(1)}, u32[]{:S(2)}, u32[]{:S(2)}) collective-permute-start(f32[64,2304]{1,0:T(8,128)S(1)} %collective-permute-done.8.refs_0_.refs_3_), channel_id=1, source_target_pairs={{4,8},{8,4},{12,16},{16,12},{20,24},{24,20},{28,0},{0,28},{5,9},{9... | collective-permute-start | bytes 1769480 | tf_op jit(solution)/shard_map/ppermute | solution.py:22
  61.7 1.7 %collective-permute-done.3.refs_1_.refs_6_ = f32[64,2304]{1,0:T(8,128)S(1)} collective-permute-done((f32[64,2304]{1,0:T(8,128)S(1)}, f32[64,2304]{1,0:T(8,128)S(1)}, u32[]{:S(2)}, u32[]{:S(2)}) %collective-permute-start.3) | collective-permute-done | bytes 589856 | tf_op jit(solution)/shard_map/ppermute | solution.py:18
  63.4 6.1 %collective-permute-start.4 = (f32[64,2304]{1,0:T(8,128)S(1)}, f32[64,2304]{1,0:T(8,128)S(1)}, u32[]{:S(2)}, u32[]{:S(2)}) collective-permute-start(f32[64,2304]{1,0:T(8,128)S(1)} %collective-permute-done.3.refs_1_.refs_6_), channel_id=1, source_target_pairs={{4,8},{8,4},{12,16},{16,12},{20,24},{24,20},{28,0},{0,28},{5,9},{9... | collective-permute-start | bytes 1769480 | tf_op jit(solution)/shard_map/ppermute | solution.py:22
  69.6 0.4 shard_map.28.refs_3_.refs_2_.refs_7_
  70.0 2.0 %shard_map.29.refs_3_ = f32[2,2,4,64,128]{4,3,2,1,0:T(8,128)S(1)} custom-call(f32[64,2304]{1,0:T(8,128)S(1)} %get-tuple-element.14.refs_0_, f32[64,2304]{1,0:T(8,128)S(1)} %collective-permute-done.5.refs_1_, f32[64,2304]{1,0:T(8,128)S(1)} %collective-permute-done.6.refs_2_, ...), custom_call_target="tpu_custom_call", output_to_operand_aliasing={{}: (4, {})} | custom-call | tf_op jit(solution)/shard_map/pallas_call | solution.py:64
  72.0 1.4 %shard_map.30.refs_3_ = f32[2,2,4,64,128]{4,3,2,1,0:T(8,128)S(1)} custom-call(f32[64,2304]{1,0:T(8,128)S(1)} %collective-permute-done.8.refs_0_.refs_3_, f32[64,2304]{1,0:T(8,128)S(1)} %collective-permute-done.9.refs_1_.refs_4_, f32[2304,128]{1,0:T(8,128)S(1)} %shard_map.28.refs_3_.refs_2_.refs_7_, ...), custom_call_target="tpu_custom_call", output_to_operand_aliasing={{}: (3, {})} | custom-call | tf_op jit(solution)/shard_map/pallas_call | solution.py:64
  73.4 0.5 collective-permute-done.10.refs_0_.refs_5_
  73.8 1.4 %shard_map.31.refs_10_ = f32[2,2,4,64,128]{4,3,2,1,0:T(8,128)S(1)} custom-call(f32[64,2304]{1,0:T(8,128)S(1)} %collective-permute-done.10.refs_0_.refs_5_, f32[64,2304]{1,0:T(8,128)S(1)} %collective-permute-done.3.refs_1_.refs_6_, f32[2304,128]{1,0:T(8,128)S(1)} %shard_map.28.refs_3_.refs_2_.refs_7_, ...), custom_call_target="tpu_custom_call", output_to_operand_aliasing={{}: (3, {})} | custom-call | tf_op jit(solution)/shard_map/pallas_call | solution.py:64
  75.2 4.0 %collective-permute-done.11.refs_9_ = f32[80,2304]{1,0:T(8,128)S(1)} collective-permute-done((f32[80,2304]{1,0:T(8,128)S(1)}, f32[80,2304]{1,0:T(8,128)S(1)}, u32[]{:S(2)}, u32[]{:S(2)}) %collective-permute-start.11) | collective-permute-done | bytes 737312 | tf_op jit(solution)/shard_map/ppermute | solution.py:18
  79.2 3.6 %shard_map.32 = (f32[2,2,4,64,128]{4,3,2,1,0:T(8,128)S(1)}, f32[2304,256]{1,0:T(8,128)S(1)}) custom-call(f32[64,2304]{1,0:T(8,128)S(1)} %get-tuple-element.14.refs_0_, f32[64,2304]{1,0:T(8,128)S(1)} %collective-permute-done.5.refs_1_, f32[64,2304]{1,0:T(8,128)S(1)} %collective-permute-done.6.refs_2_, ...), custom_call_target="tpu_custom_call", output_to_operand_aliasing={{0}: (10, {})} | custom-call | tf_op jit(solution)/shard_map/pallas_call | solution.py:92
  82.8 3.7 %collective-permute-done.4.last_ref = f32[64,2304]{1,0:T(8,128)S(1)} collective-permute-done((f32[64,2304]{1,0:T(8,128)S(1)}, f32[64,2304]{1,0:T(8,128)S(1)}, u32[]{:S(2)}, u32[]{:S(2)}) %collective-permute-start.4) | collective-permute-done | bytes 589856 | tf_op jit(solution)/shard_map/ppermute | solution.py:22
  86.5 1.4 %shard_map.33 = (f32[2,4,64,128]{3,2,1,0:T(8,128)S(1)}, f32[2,4,64,128]{3,2,1,0:T(8,128)S(1)}) custom-call(f32[64,2304]{1,0:T(8,128)S(1)} %collective-permute-done.4.last_ref, f32[2304,256]{1,0:T(8,128)S(1)} %get-tuple-element.19.both_ref, f32[2,2,4,64,128]{4,3,2,1,0:T(8,128)S(1)} %get-tuple-element.20.old), custom_call_target="tpu_custom_call" | custom-call | tf_op jit(solution)/shard_map/pallas_call | solution.py:127
  87.9 2.6 %collective-permute-start.12 = (f32[2,4,64,128]{3,2,1,0:T(8,128)S(1)}, f32[2,4,64,128]{3,2,1,0:T(8,128)S(1)}, u32[]{:S(2)}, u32[]{:S(2)}) collective-permute-start(f32[2,4,64,128]{3,2,1,0:T(8,128)S(1)} %get-tuple-element.22), channel_id=1, source_target_pairs={{0,32},{32,0},{1,33},{33,1},{2,34},{34,2},{3,35},{35,3},{4,36},{36... | collective-permute-start | bytes 786440 | tf_op jit(solution)/shard_map/ppermute | solution.py:168
  90.5 1.2 %collective-permute-done.12 = f32[2,4,64,128]{3,2,1,0:T(8,128)S(1)} collective-permute-done((f32[2,4,64,128]{3,2,1,0:T(8,128)S(1)}, f32[2,4,64,128]{3,2,1,0:T(8,128)S(1)}, u32[]{:S(2)}, u32[]{:S(2)}) %collective-permute-start.12) | collective-permute-done | bytes 262176 | tf_op jit(solution)/shard_map/ppermute | solution.py:168
  91.7 14.8 %all_to_all.5 = f32[32,16,128]{2,1,0:T(8,128)S(1)} all-to-all(f32[32,16,128]{2,1,0:T(8,128)S(1)} %bitcast.1), channel_id=1, replica_groups=mesh['x'=4,'core'=2,'zhi'=4,'zlo'=2,'layer'=4] {'zlo','x','layer'}, dimensions={0} | all-to-all | bytes 524288 | tf_op jit(solution)/shard_map/all_to_all | solution.py:172
  106.5 0.6 reduce_sum.9
  (4 shorter events, 0.2 us)
Async XLA Ops:
  0.0 22.2 %copy-start = (f32[128,4608]{1,0:T(8,128)S(1)}, f32[128,4608]{1,0:T(8,128)}, u32[]{:S(2)}) copy-start(f32[128,4608]{1,0:T(8,128)} %param.3) | copy-start | bytes 7077892
  1.5 14.6 %collective-permute-start = (f32[64,2304]{1,0:T(8,128)S(1)}, f32[64,2304]{1,0:T(8,128)S(1)}, u32[]{:S(2)}, u32[]{:S(2)}) collective-permute-start(f32[64,2304]{1,0:T(8,128)S(1)} %get-tuple-element.14.refs_0_), channel_id=1, source_target_pairs={{0,4},{4,0},{8,12},{12,8},{16,20},{20,16},{24,28},{28,24},{1,5},{5... | collective-permute-start | bytes 1769480 | tf_op jit(solution)/shard_map/ppermute | solution.py:18
  4.0 24.6 %collective-permute-start.6 = (f32[64,2304]{1,0:T(8,128)S(1)}, f32[64,2304]{1,0:T(8,128)S(1)}, u32[]{:S(2)}, u32[]{:S(2)}) collective-permute-start(f32[64,2304]{1,0:T(8,128)S(1)} %get-tuple-element.14.refs_0_), channel_id=1, source_target_pairs={{4,8},{8,4},{12,16},{16,12},{20,24},{24,20},{28,0},{0,28},{5,9},{9... | collective-permute-start | bytes 1769480 | tf_op jit(solution)/shard_map/ppermute | solution.py:22
  8.7 20.0 %collective-permute-start.5 = (f32[64,2304]{1,0:T(8,128)S(1)}, f32[64,2304]{1,0:T(8,128)S(1)}, u32[]{:S(2)}, u32[]{:S(2)}) collective-permute-start(f32[64,2304]{1,0:T(8,128)S(1)} %get-tuple-element.16), channel_id=1, source_target_pairs={{0,4},{4,0},{8,12},{12,8},{16,20},{20,16},{24,28},{28,24},{1,5},{5... | collective-permute-start | bytes 1769480 | tf_op jit(solution)/shard_map/ppermute | solution.py:18
  8.7 26.1 %collective-permute-start.7 = (f32[64,2304]{1,0:T(8,128)S(1)}, f32[64,2304]{1,0:T(8,128)S(1)}, u32[]{:S(2)}, u32[]{:S(2)}) collective-permute-start(f32[64,2304]{1,0:T(8,128)S(1)} %get-tuple-element.16), channel_id=1, source_target_pairs={{4,8},{8,4},{12,16},{16,12},{20,24},{24,20},{28,0},{0,28},{5,9},{9... | collective-permute-start | bytes 1769480 | tf_op jit(solution)/shard_map/ppermute | solution.py:22
  16.0 30.7 %collective-permute-start.1 = (f32[64,2304]{1,0:T(8,128)S(1)}, f32[64,2304]{1,0:T(8,128)S(1)}, u32[]{:S(2)}, u32[]{:S(2)}) collective-permute-start(f32[64,2304]{1,0:T(8,128)S(1)} %collective-permute-done), channel_id=1, source_target_pairs={{4,8},{8,4},{12,16},{16,12},{20,24},{24,20},{28,0},{0,28},{5,9},{9... | collective-permute-start | bytes 1769480 | tf_op jit(solution)/shard_map/ppermute | solution.py:22
  22.4 15.8 %collective-permute-start.2 = (f32[48,2304]{1,0:T(8,128)S(1)}, f32[48,2304]{1,0:T(8,128)S(1)}, u32[]{:S(2)}, u32[]{:S(2)}) collective-permute-start(f32[48,2304]{1,0:T(8,128)S(1)} %slice.24), channel_id=1, source_target_pairs={{0,4},{4,0},{8,12},{12,8},{16,20},{20,16},{24,28},{28,24},{1,5},{5... | collective-permute-start | bytes 1327112 | tf_op jit(solution)/shard_map/ppermute | solution.py:18
  28.7 30.7 %collective-permute-start.9 = (f32[64,2304]{1,0:T(8,128)S(1)}, f32[64,2304]{1,0:T(8,128)S(1)}, u32[]{:S(2)}, u32[]{:S(2)}) collective-permute-start(f32[64,2304]{1,0:T(8,128)S(1)} %collective-permute-done.5.refs_1_), channel_id=1, source_target_pairs={{4,8},{8,4},{12,16},{16,12},{20,24},{24,20},{28,0},{0,28},{5,9},{9... | collective-permute-start | bytes 1769480 | tf_op jit(solution)/shard_map/ppermute | solution.py:22
  34.8 24.5 %collective-permute-start.8 = (f32[64,2304]{1,0:T(8,128)S(1)}, f32[64,2304]{1,0:T(8,128)S(1)}, u32[]{:S(2)}, u32[]{:S(2)}) collective-permute-start(f32[64,2304]{1,0:T(8,128)S(1)} %collective-permute-done.7), channel_id=1, source_target_pairs={{0,4},{4,0},{8,12},{12,8},{16,20},{20,16},{24,28},{28,24},{1,5},{5... | collective-permute-start | bytes 1769480 | tf_op jit(solution)/shard_map/ppermute | solution.py:18
  46.7 16.7 %collective-permute-start.3 = (f32[64,2304]{1,0:T(8,128)S(1)}, f32[64,2304]{1,0:T(8,128)S(1)}, u32[]{:S(2)}, u32[]{:S(2)}) collective-permute-start(f32[64,2304]{1,0:T(8,128)S(1)} %collective-permute-done.1), channel_id=1, source_target_pairs={{0,4},{4,0},{8,12},{12,8},{16,20},{20,16},{24,28},{28,24},{1,5},{5... | collective-permute-start | bytes 1769480 | tf_op jit(solution)/shard_map/ppermute | solution.py:18
  59.4 19.9 %collective-permute-start.11 = (f32[80,2304]{1,0:T(8,128)S(1)}, f32[80,2304]{1,0:T(8,128)S(1)}, u32[]{:S(2)}, u32[]{:S(2)}) collective-permute-start(f32[80,2304]{1,0:T(8,128)S(1)} %slice.25), channel_id=1, source_target_pairs={{0,4},{4,0},{8,12},{12,8},{16,20},{20,16},{24,28},{28,24},{1,5},{5... | collective-permute-start | bytes 2211848 | tf_op jit(solution)/shard_map/ppermute | solution.py:18
  59.4 14.5 %collective-permute-start.10 = (f32[64,2304]{1,0:T(8,128)S(1)}, f32[64,2304]{1,0:T(8,128)S(1)}, u32[]{:S(2)}, u32[]{:S(2)}) collective-permute-start(f32[64,2304]{1,0:T(8,128)S(1)} %collective-permute-done.8.refs_0_.refs_3_), channel_id=1, source_target_pairs={{4,8},{8,4},{12,16},{16,12},{20,24},{24,20},{28,0},{0,28},{5,9},{9... | collective-permute-start | bytes 1769480 | tf_op jit(solution)/shard_map/ppermute | solution.py:22
  63.4 23.1 %collective-permute-start.4 = (f32[64,2304]{1,0:T(8,128)S(1)}, f32[64,2304]{1,0:T(8,128)S(1)}, u32[]{:S(2)}, u32[]{:S(2)}) collective-permute-start(f32[64,2304]{1,0:T(8,128)S(1)} %collective-permute-done.3.refs_1_.refs_6_), channel_id=1, source_target_pairs={{4,8},{8,4},{12,16},{16,12},{20,24},{24,20},{28,0},{0,28},{5,9},{9... | collective-permute-start | bytes 1769480 | tf_op jit(solution)/shard_map/ppermute | solution.py:22
  87.9 3.7 %collective-permute-start.12 = (f32[2,4,64,128]{3,2,1,0:T(8,128)S(1)}, f32[2,4,64,128]{3,2,1,0:T(8,128)S(1)}, u32[]{:S(2)}, u32[]{:S(2)}) collective-permute-start(f32[2,4,64,128]{3,2,1,0:T(8,128)S(1)} %get-tuple-element.22), channel_id=1, source_target_pairs={{0,32},{32,0},{1,33},{33,1},{2,34},{34,2},{3,35},{35,3},{4,36},{36... | collective-permute-start | bytes 786440 | tf_op jit(solution)/shard_map/ppermute | solution.py:168

commit v9 on v8

--- a/solution.py
+++ b/solution.py
@@ -7,7 +7,7 @@
 from jax.sharding import PartitionSpec as P
 
 LEVELS = 8
-EARLY = 48
+EARLY = 40
 COL = ("zhi", "zlo")
 VMEM = pl.BlockSpec(memory_space=pltpu.VMEM)
 SWAP_1 = [(i, i ^ 1) for i in range(LEVELS)]

time: 107 us -> 107 us (level)
    ppermute x6, waiting for transfers between devices: 25.3 us -> 28.2 us  [swap_2(): return lax.ppermute(array, COL, SWAP_2)]
    ppermute x6, waiting for transfers between devices: 21.1 us -> 18.5 us  [swap_1(): return lax.ppermute(array, COL, SWAP_1)]
where the time goes in v9:
time: 107 us
  waiting for transfers between devices  47.8 us (45%)
  starting transfers between devices  31.8 us (30%)
  blocking collectives  14.8 us (14%)
  Pallas kernels  10.1 us (9%)
  other arithmetic  2.3 us (2%)
    ppermute x6, waiting for transfers between devices, swap_2(): return lax.ppermute(array, COL, SWAP_2)  28.2 us
    ppermute x6, starting transfers between devices, swap_2(): return lax.ppermute(array, COL, SWAP_2)  26.6 us
    ppermute x6, waiting for transfers between devices, swap_1(): return lax.ppermute(array, COL, SWAP_1)  18.5 us
    all_to_all x1, blocking collectives, on_device(): return lax.all_to_all(blocks, axes, 0, 0).sum(0)  14.8 us
    pallas_call x3, Pallas kernels, multiply(): pl.pallas_call(kernel, out_shape=jax.ShapeDtypeStruct(before.shape, jnp.f...  4.76 us
    pallas_call x1, Pallas kernels, multiply_pair(): pl.pallas_call(kernel, out_shape=[jax.ShapeDtypeStruct(before.shape, jnp....  3.6 us
    ppermute x6, starting transfers between devices, swap_1(): return lax.ppermute(array, COL, SWAP_1)  2.66 us
    ppermute x1, starting transfers between devices, on_device(): product = mine + lax.ppermute(other, 'core', [(0, 1), (1, 0)])  2.56 us
  transfers between devices with their start and end apart: 13, of which 10 were waited for; matrix products, arithmetic and copies ran while one was open for 0% of the time, Pallas kernels for 8%

profile of v9, /device:TPU:1, one launch (start us, length us, event | category | flops | bytes accessed | tf_op | source)
XLA Modules:
  0.0 107.1 jit_solution(6919107067073921394)
XLA Ops:
  0.0 0.0 copy-start
  0.0 1.5 %slice_select_fusion.2 = (f32[64,2304]{1,0:T(8,128)S(1)}, f32[64,2304]{1,0:T(8,128)S(1)}) fusion(f32[64,4608]{1,0:T(8,128)} %param.2, pred[]{:T(512)S(6)} %eq.4), kind=kLoop, calls=%fused_computation.2 | loop fusion | flops 294912 | bytes 2359297 | tf_op jit(solution)/shard_map/jit(_where)/select_n | solution.py:144
  1.5 2.6 %collective-permute-start = (f32[64,2304]{1,0:T(8,128)S(1)}, f32[64,2304]{1,0:T(8,128)S(1)}, u32[]{:S(2)}, u32[]{:S(2)}) collective-permute-start(f32[64,2304]{1,0:T(8,128)S(1)} %get-tuple-element.14.refs_0_), channel_id=1, source_target_pairs={{0,4},{4,0},{8,12},{12,8},{16,20},{20,16},{24,28},{28,24},{1,5},{5... | collective-permute-start | bytes 1769480 | tf_op jit(solution)/shard_map/ppermute | solution.py:18
  4.0 4.7 %collective-permute-start.6 = (f32[64,2304]{1,0:T(8,128)S(1)}, f32[64,2304]{1,0:T(8,128)S(1)}, u32[]{:S(2)}, u32[]{:S(2)}) collective-permute-start(f32[64,2304]{1,0:T(8,128)S(1)} %get-tuple-element.14.refs_0_), channel_id=1, source_target_pairs={{4,8},{8,4},{12,16},{16,12},{20,24},{24,20},{28,0},{0,28},{5,9},{9... | collective-permute-start | bytes 1769480 | tf_op jit(solution)/shard_map/ppermute | solution.py:22
  8.7 0.0 collective-permute-start.5
  8.7 1.5 %collective-permute-start.7 = (f32[64,2304]{1,0:T(8,128)S(1)}, f32[64,2304]{1,0:T(8,128)S(1)}, u32[]{:S(2)}, u32[]{:S(2)}) collective-permute-start(f32[64,2304]{1,0:T(8,128)S(1)} %get-tuple-element.16), channel_id=1, source_target_pairs={{4,8},{8,4},{12,16},{16,12},{20,24},{24,20},{28,0},{0,28},{5,9},{9... | collective-permute-start | bytes 1769480 | tf_op jit(solution)/shard_map/ppermute | solution.py:22
  10.2 5.9 %collective-permute-done = f32[64,2304]{1,0:T(8,128)S(1)} collective-permute-done((f32[64,2304]{1,0:T(8,128)S(1)}, f32[64,2304]{1,0:T(8,128)S(1)}, u32[]{:S(2)}, u32[]{:S(2)}) %collective-permute-start) | collective-permute-done | bytes 589856 | tf_op jit(solution)/shard_map/ppermute | solution.py:18
  16.0 6.1 %collective-permute-start.1 = (f32[64,2304]{1,0:T(8,128)S(1)}, f32[64,2304]{1,0:T(8,128)S(1)}, u32[]{:S(2)}, u32[]{:S(2)}) collective-permute-start(f32[64,2304]{1,0:T(8,128)S(1)} %collective-permute-done), channel_id=1, source_target_pairs={{4,8},{8,4},{12,16},{16,12},{20,24},{24,20},{28,0},{0,28},{5,9},{9... | collective-permute-start | bytes 1769480 | tf_op jit(solution)/shard_map/ppermute | solution.py:22
  22.2 0.0 copy-done
  22.2 0.2 slice_select_fusion
  22.4 0.1 collective-permute-start.2
  22.5 6.2 %collective-permute-done.5.refs_1_ = f32[64,2304]{1,0:T(8,128)S(1)} collective-permute-done((f32[64,2304]{1,0:T(8,128)S(1)}, f32[64,2304]{1,0:T(8,128)S(1)}, u32[]{:S(2)}, u32[]{:S(2)}) %collective-permute-start.5) | collective-permute-done | bytes 589856 | tf_op jit(solution)/shard_map/ppermute | solution.py:18
  28.7 0.0 collective-permute-done.6.refs_2_
  28.7 6.1 %collective-permute-start.9 = (f32[64,2304]{1,0:T(8,128)S(1)}, f32[64,2304]{1,0:T(8,128)S(1)}, u32[]{:S(2)}, u32[]{:S(2)}) collective-permute-start(f32[64,2304]{1,0:T(8,128)S(1)} %collective-permute-done.5.refs_1_), channel_id=1, source_target_pairs={{4,8},{8,4},{12,16},{16,12},{20,24},{24,20},{28,0},{0,28},{5,9},{9... | collective-permute-start | bytes 1769480 | tf_op jit(solution)/shard_map/ppermute | solution.py:22
  34.8 0.0 collective-permute-done.7
  34.8 0.0 collective-permute-start.8
  34.8 1.8 %collective-permute-done.2.refs_8_ = f32[40,2304]{1,0:T(8,128)S(1)} collective-permute-done((f32[40,2304]{1,0:T(8,128)S(1)}, f32[40,2304]{1,0:T(8,128)S(1)}, u32[]{:S(2)}, u32[]{:S(2)}) %collective-permute-start.2) | collective-permute-done | bytes 368672 | tf_op jit(solution)/shard_map/ppermute | solution.py:18
  36.6 10.1 %collective-permute-done.1 = f32[64,2304]{1,0:T(8,128)S(1)} collective-permute-done((f32[64,2304]{1,0:T(8,128)S(1)}, f32[64,2304]{1,0:T(8,128)S(1)}, u32[]{:S(2)}, u32[]{:S(2)}) %collective-permute-start.1) | collective-permute-done | bytes 589856 | tf_op jit(solution)/shard_map/ppermute | solution.py:22
  46.7 0.0 collective-permute-start.3
  46.7 0.1 slice.25
  46.8 12.6 %collective-permute-done.9.refs_1_.refs_4_ = f32[64,2304]{1,0:T(8,128)S(1)} collective-permute-done((f32[64,2304]{1,0:T(8,128)S(1)}, f32[64,2304]{1,0:T(8,128)S(1)}, u32[]{:S(2)}, u32[]{:S(2)}) %collective-permute-start.9) | collective-permute-done | bytes 589856 | tf_op jit(solution)/shard_map/ppermute | solution.py:22
  59.4 0.0 collective-permute-start.11
  59.4 0.0 collective-permute-done.8.refs_0_.refs_3_
  59.4 2.4 %collective-permute-start.10 = (f32[64,2304]{1,0:T(8,128)S(1)}, f32[64,2304]{1,0:T(8,128)S(1)}, u32[]{:S(2)}, u32[]{:S(2)}) collective-permute-start(f32[64,2304]{1,0:T(8,128)S(1)} %collective-permute-done.8.refs_0_.refs_3_), channel_id=1, source_target_pairs={{4,8},{8,4},{12,16},{16,12},{20,24},{24,20},{28,0},{0,28},{5,9},{9... | collective-permute-start | bytes 1769480 | tf_op jit(solution)/shard_map/ppermute | solution.py:22
  61.7 0.4 collective-permute-done.3.refs_1_.refs_6_
  62.1 5.9 %collective-permute-start.4 = (f32[64,2304]{1,0:T(8,128)S(1)}, f32[64,2304]{1,0:T(8,128)S(1)}, u32[]{:S(2)}, u32[]{:S(2)}) collective-permute-start(f32[64,2304]{1,0:T(8,128)S(1)} %collective-permute-done.3.refs_1_.refs_6_), channel_id=1, source_target_pairs={{4,8},{8,4},{12,16},{16,12},{20,24},{24,20},{28,0},{0,28},{5,9},{9... | collective-permute-start | bytes 1769480 | tf_op jit(solution)/shard_map/ppermute | solution.py:22
  68.0 0.4 shard_map.28.refs_3_.refs_2_.refs_7_
  68.4 2.0 %shard_map.29.refs_3_ = f32[2,2,4,64,128]{4,3,2,1,0:T(8,128)S(1)} custom-call(f32[64,2304]{1,0:T(8,128)S(1)} %get-tuple-element.14.refs_0_, f32[64,2304]{1,0:T(8,128)S(1)} %collective-permute-done.5.refs_1_, f32[64,2304]{1,0:T(8,128)S(1)} %collective-permute-done.6.refs_2_, ...), custom_call_target="tpu_custom_call", output_to_operand_aliasing={{}: (4, {})} | custom-call | tf_op jit(solution)/shard_map/pallas_call | solution.py:64
  70.4 1.4 %shard_map.30.refs_3_ = f32[2,2,4,64,128]{4,3,2,1,0:T(8,128)S(1)} custom-call(f32[64,2304]{1,0:T(8,128)S(1)} %collective-permute-done.8.refs_0_.refs_3_, f32[64,2304]{1,0:T(8,128)S(1)} %collective-permute-done.9.refs_1_.refs_4_, f32[2304,128]{1,0:T(8,128)S(1)} %shard_map.28.refs_3_.refs_2_.refs_7_, ...), custom_call_target="tpu_custom_call", output_to_operand_aliasing={{}: (3, {})} | custom-call | tf_op jit(solution)/shard_map/pallas_call | solution.py:64
  71.8 2.1 %collective-permute-done.10.refs_0_.refs_5_ = f32[64,2304]{1,0:T(8,128)S(1)} collective-permute-done((f32[64,2304]{1,0:T(8,128)S(1)}, f32[64,2304]{1,0:T(8,128)S(1)}, u32[]{:S(2)}, u32[]{:S(2)}) %collective-permute-start.10) | collective-permute-done | bytes 589856 | tf_op jit(solution)/shard_map/ppermute | solution.py:22
  73.8 1.4 %shard_map.31.refs_10_ = f32[2,2,4,64,128]{4,3,2,1,0:T(8,128)S(1)} custom-call(f32[64,2304]{1,0:T(8,128)S(1)} %collective-permute-done.10.refs_0_.refs_5_, f32[64,2304]{1,0:T(8,128)S(1)} %collective-permute-done.3.refs_1_.refs_6_, f32[2304,128]{1,0:T(8,128)S(1)} %shard_map.28.refs_3_.refs_2_.refs_7_, ...), custom_call_target="tpu_custom_call", output_to_operand_aliasing={{}: (3, {})} | custom-call | tf_op jit(solution)/shard_map/pallas_call | solution.py:64
  75.2 4.3 %collective-permute-done.11.refs_9_ = f32[88,2304]{1,0:T(8,128)S(1)} collective-permute-done((f32[88,2304]{1,0:T(8,128)S(1)}, f32[88,2304]{1,0:T(8,128)S(1)}, u32[]{:S(2)}, u32[]{:S(2)}) %collective-permute-start.11) | collective-permute-done | bytes 811040 | tf_op jit(solution)/shard_map/ppermute | solution.py:18
  79.5 3.6 %shard_map.32 = (f32[2,2,4,64,128]{4,3,2,1,0:T(8,128)S(1)}, f32[2304,256]{1,0:T(8,128)S(1)}) custom-call(f32[64,2304]{1,0:T(8,128)S(1)} %get-tuple-element.14.refs_0_, f32[64,2304]{1,0:T(8,128)S(1)} %collective-permute-done.5.refs_1_, f32[64,2304]{1,0:T(8,128)S(1)} %collective-permute-done.6.refs_2_, ...), custom_call_target="tpu_custom_call", output_to_operand_aliasing={{0}: (10, {})} | custom-call | tf_op jit(solution)/shard_map/pallas_call | solution.py:92
  83.1 3.4 %collective-permute-done.4.last_ref = f32[64,2304]{1,0:T(8,128)S(1)} collective-permute-done((f32[64,2304]{1,0:T(8,128)S(1)}, f32[64,2304]{1,0:T(8,128)S(1)}, u32[]{:S(2)}, u32[]{:S(2)}) %collective-permute-start.4) | collective-permute-done | bytes 589856 | tf_op jit(solution)/shard_map/ppermute | solution.py:22
  86.5 1.4 %shard_map.33 = (f32[2,4,64,128]{3,2,1,0:T(8,128)S(1)}, f32[2,4,64,128]{3,2,1,0:T(8,128)S(1)}) custom-call(f32[64,2304]{1,0:T(8,128)S(1)} %collective-permute-done.4.last_ref, f32[2304,256]{1,0:T(8,128)S(1)} %get-tuple-element.19.both_ref, f32[2,2,4,64,128]{4,3,2,1,0:T(8,128)S(1)} %get-tuple-element.20.old), custom_call_target="tpu_custom_call" | custom-call | tf_op jit(solution)/shard_map/pallas_call | solution.py:127
  87.9 2.6 %collective-permute-start.12 = (f32[2,4,64,128]{3,2,1,0:T(8,128)S(1)}, f32[2,4,64,128]{3,2,1,0:T(8,128)S(1)}, u32[]{:S(2)}, u32[]{:S(2)}) collective-permute-start(f32[2,4,64,128]{3,2,1,0:T(8,128)S(1)} %get-tuple-element.22), channel_id=1, source_target_pairs={{0,32},{32,0},{1,33},{33,1},{2,34},{34,2},{3,35},{35,3},{4,36},{36... | collective-permute-start | bytes 786440 | tf_op jit(solution)/shard_map/ppermute | solution.py:168
  90.5 1.2 %collective-permute-done.12 = f32[2,4,64,128]{3,2,1,0:T(8,128)S(1)} collective-permute-done((f32[2,4,64,128]{3,2,1,0:T(8,128)S(1)}, f32[2,4,64,128]{3,2,1,0:T(8,128)S(1)}, u32[]{:S(2)}, u32[]{:S(2)}) %collective-permute-start.12) | collective-permute-done | bytes 262176 | tf_op jit(solution)/shard_map/ppermute | solution.py:168
  91.7 14.8 %all_to_all.5 = f32[32,16,128]{2,1,0:T(8,128)S(1)} all-to-all(f32[32,16,128]{2,1,0:T(8,128)S(1)} %bitcast.1), channel_id=1, replica_groups=mesh['x'=4,'core'=2,'zhi'=4,'zlo'=2,'layer'=4] {'zlo','x','layer'}, dimensions={0} | all-to-all | bytes 524288 | tf_op jit(solution)/shard_map/all_to_all | solution.py:172
  106.5 0.6 reduce_sum.9
  (3 shorter events, 0.1 us)
Async XLA Ops:
  0.0 22.2 %copy-start = (f32[128,4608]{1,0:T(8,128)S(1)}, f32[128,4608]{1,0:T(8,128)}, u32[]{:S(2)}) copy-start(f32[128,4608]{1,0:T(8,128)} %param.3) | copy-start | bytes 7077892
  1.5 14.6 %collective-permute-start = (f32[64,2304]{1,0:T(8,128)S(1)}, f32[64,2304]{1,0:T(8,128)S(1)}, u32[]{:S(2)}, u32[]{:S(2)}) collective-permute-start(f32[64,2304]{1,0:T(8,128)S(1)} %get-tuple-element.14.refs_0_), channel_id=1, source_target_pairs={{0,4},{4,0},{8,12},{12,8},{16,20},{20,16},{24,28},{28,24},{1,5},{5... | collective-permute-start | bytes 1769480 | tf_op jit(solution)/shard_map/ppermute | solution.py:18
  4.0 24.6 %collective-permute-start.6 = (f32[64,2304]{1,0:T(8,128)S(1)}, f32[64,2304]{1,0:T(8,128)S(1)}, u32[]{:S(2)}, u32[]{:S(2)}) collective-permute-start(f32[64,2304]{1,0:T(8,128)S(1)} %get-tuple-element.14.refs_0_), channel_id=1, source_target_pairs={{4,8},{8,4},{12,16},{16,12},{20,24},{24,20},{28,0},{0,28},{5,9},{9... | collective-permute-start | bytes 1769480 | tf_op jit(solution)/shard_map/ppermute | solution.py:22
  8.7 20.0 %collective-permute-start.5 = (f32[64,2304]{1,0:T(8,128)S(1)}, f32[64,2304]{1,0:T(8,128)S(1)}, u32[]{:S(2)}, u32[]{:S(2)}) collective-permute-start(f32[64,2304]{1,0:T(8,128)S(1)} %get-tuple-element.16), channel_id=1, source_target_pairs={{0,4},{4,0},{8,12},{12,8},{16,20},{20,16},{24,28},{28,24},{1,5},{5... | collective-permute-start | bytes 1769480 | tf_op jit(solution)/shard_map/ppermute | solution.py:18
  8.7 26.1 %collective-permute-start.7 = (f32[64,2304]{1,0:T(8,128)S(1)}, f32[64,2304]{1,0:T(8,128)S(1)}, u32[]{:S(2)}, u32[]{:S(2)}) collective-permute-start(f32[64,2304]{1,0:T(8,128)S(1)} %get-tuple-element.16), channel_id=1, source_target_pairs={{4,8},{8,4},{12,16},{16,12},{20,24},{24,20},{28,0},{0,28},{5,9},{9... | collective-permute-start | bytes 1769480 | tf_op jit(solution)/shard_map/ppermute | solution.py:22
  16.0 30.7 %collective-permute-start.1 = (f32[64,2304]{1,0:T(8,128)S(1)}, f32[64,2304]{1,0:T(8,128)S(1)}, u32[]{:S(2)}, u32[]{:S(2)}) collective-permute-start(f32[64,2304]{1,0:T(8,128)S(1)} %collective-permute-done), channel_id=1, source_target_pairs={{4,8},{8,4},{12,16},{16,12},{20,24},{24,20},{28,0},{0,28},{5,9},{9... | collective-permute-start | bytes 1769480 | tf_op jit(solution)/shard_map/ppermute | solution.py:22
  22.4 14.2 %collective-permute-start.2 = (f32[40,2304]{1,0:T(8,128)S(1)}, f32[40,2304]{1,0:T(8,128)S(1)}, u32[]{:S(2)}, u32[]{:S(2)}) collective-permute-start(f32[40,2304]{1,0:T(8,128)S(1)} %slice.24), channel_id=1, source_target_pairs={{0,4},{4,0},{8,12},{12,8},{16,20},{20,16},{24,28},{28,24},{1,5},{5... | collective-permute-start | bytes 1105928 | tf_op jit(solution)/shard_map/ppermute | solution.py:18
  28.7 30.7 %collective-permute-start.9 = (f32[64,2304]{1,0:T(8,128)S(1)}, f32[64,2304]{1,0:T(8,128)S(1)}, u32[]{:S(2)}, u32[]{:S(2)}) collective-permute-start(f32[64,2304]{1,0:T(8,128)S(1)} %collective-permute-done.5.refs_1_), channel_id=1, source_target_pairs={{4,8},{8,4},{12,16},{16,12},{20,24},{24,20},{28,0},{0,28},{5,9},{9... | collective-permute-start | bytes 1769480 | tf_op jit(solution)/shard_map/ppermute | solution.py:22
  34.8 24.5 %collective-permute-start.8 = (f32[64,2304]{1,0:T(8,128)S(1)}, f32[64,2304]{1,0:T(8,128)S(1)}, u32[]{:S(2)}, u32[]{:S(2)}) collective-permute-start(f32[64,2304]{1,0:T(8,128)S(1)} %collective-permute-done.7), channel_id=1, source_target_pairs={{0,4},{4,0},{8,12},{12,8},{16,20},{20,16},{24,28},{28,24},{1,5},{5... | collective-permute-start | bytes 1769480 | tf_op jit(solution)/shard_map/ppermute | solution.py:18
  46.7 15.4 %collective-permute-start.3 = (f32[64,2304]{1,0:T(8,128)S(1)}, f32[64,2304]{1,0:T(8,128)S(1)}, u32[]{:S(2)}, u32[]{:S(2)}) collective-permute-start(f32[64,2304]{1,0:T(8,128)S(1)} %collective-permute-done.1), channel_id=1, source_target_pairs={{0,4},{4,0},{8,12},{12,8},{16,20},{20,16},{24,28},{28,24},{1,5},{5... | collective-permute-start | bytes 1769480 | tf_op jit(solution)/shard_map/ppermute | solution.py:18
  59.4 20.1 %collective-permute-start.11 = (f32[88,2304]{1,0:T(8,128)S(1)}, f32[88,2304]{1,0:T(8,128)S(1)}, u32[]{:S(2)}, u32[]{:S(2)}) collective-permute-start(f32[88,2304]{1,0:T(8,128)S(1)} %slice.25), channel_id=1, source_target_pairs={{0,4},{4,0},{8,12},{12,8},{16,20},{20,16},{24,28},{28,24},{1,5},{5... | collective-permute-start | bytes 2433032 | tf_op jit(solution)/shard_map/ppermute | solution.py:18
  59.4 14.5 %collective-permute-start.10 = (f32[64,2304]{1,0:T(8,128)S(1)}, f32[64,2304]{1,0:T(8,128)S(1)}, u32[]{:S(2)}, u32[]{:S(2)}) collective-permute-start(f32[64,2304]{1,0:T(8,128)S(1)} %collective-permute-done.8.refs_0_.refs_3_), channel_id=1, source_target_pairs={{4,8},{8,4},{12,16},{16,12},{20,24},{24,20},{28,0},{0,28},{5,9},{9... | collective-permute-start | bytes 1769480 | tf_op jit(solution)/shard_map/ppermute | solution.py:22
  62.1 24.4 %collective-permute-start.4 = (f32[64,2304]{1,0:T(8,128)S(1)}, f32[64,2304]{1,0:T(8,128)S(1)}, u32[]{:S(2)}, u32[]{:S(2)}) collective-permute-start(f32[64,2304]{1,0:T(8,128)S(1)} %collective-permute-done.3.refs_1_.refs_6_), channel_id=1, source_target_pairs={{4,8},{8,4},{12,16},{16,12},{20,24},{24,20},{28,0},{0,28},{5,9},{9... | collective-permute-start | bytes 1769480 | tf_op jit(solution)/shard_map/ppermute | solution.py:22
  87.9 3.7 %collective-permute-start.12 = (f32[2,4,64,128]{3,2,1,0:T(8,128)S(1)}, f32[2,4,64,128]{3,2,1,0:T(8,128)S(1)}, u32[]{:S(2)}, u32[]{:S(2)}) collective-permute-start(f32[2,4,64,128]{3,2,1,0:T(8,128)S(1)} %get-tuple-element.22), channel_id=1, source_target_pairs={{0,32},{32,0},{1,33},{33,1},{2,34},{34,2},{3,35},{35,3},{4,36},{36... | collective-permute-start | bytes 786440 | tf_op jit(solution)/shard_map/ppermute | solution.py:168

commit v10 on v8

--- a/solution.py
+++ b/solution.py
@@ -143,7 +143,7 @@
         low, high = array[:, :half], array[:, half:]
         return jnp.where(held == 0, low, high), jnp.where(held == 0, high, low)
 
-    a_own, a_other = lax.optimization_barrier(halves(amplitudes))
+    a_own, a_other = halves(amplitudes)
     b_own, b_other = halves(integrals)
 
     far_1, far_2 = swap_1(a_own), swap_2(a_other)

time: 107 us -> 107 us (level)
  no operation moved by 1% of the time
where the time goes in v10:
time: 107 us
  waiting for transfers between devices  47.5 us (44%)
  starting transfers between devices  32.1 us (30%)
  blocking collectives  14.8 us (14%)
  Pallas kernels  10.1 us (9%)
  other arithmetic  2.3 us (2%)
    ppermute x6, starting transfers between devices, swap_2(): return lax.ppermute(array, COL, SWAP_2)  26.9 us
    ppermute x6, waiting for transfers between devices, swap_2(): return lax.ppermute(array, COL, SWAP_2)  25.3 us
    ppermute x6, waiting for transfers between devices, swap_1(): return lax.ppermute(array, COL, SWAP_1)  21.1 us
    all_to_all x1, blocking collectives, on_device(): return lax.all_to_all(blocks, axes, 0, 0).sum(0)  14.8 us
    pallas_call x3, Pallas kernels, multiply(): pl.pallas_call(kernel, out_shape=jax.ShapeDtypeStruct(before.shape, jnp.f...  4.76 us
    pallas_call x1, Pallas kernels, multiply_pair(): pl.pallas_call(kernel, out_shape=[jax.ShapeDtypeStruct(before.shape, jnp....  3.6 us
    ppermute x6, starting transfers between devices, swap_1(): return lax.ppermute(array, COL, SWAP_1)  2.66 us
    ppermute x1, starting transfers between devices, on_device(): product = mine + lax.ppermute(other, 'core', [(0, 1), (1, 0)])  2.56 us
  transfers between devices with their start and end apart: 13, of which 10 were waited for; matrix products, arithmetic and copies ran while one was open for 0% of the time, Pallas kernels for 8%

profile of v10, /device:TPU:1, one launch (start us, length us, event | category | flops | bytes accessed | tf_op | source)
XLA Modules:
  0.0 107.1 jit_solution(12551410159410051120)
XLA Ops:
  0.0 0.0 copy-start
  0.0 1.5 %slice_select_fusion.2 = (f32[64,2304]{1,0:T(8,128)S(1)}, f32[64,2304]{1,0:T(8,128)S(1)}) fusion(f32[64,4608]{1,0:T(8,128)} %param.2, pred[]{:T(512)S(6)} %eq.4), kind=kLoop, calls=%fused_computation.2 | loop fusion | flops 294912 | bytes 2359297 | tf_op jit(solution)/shard_map/jit(_where)/select_n | solution.py:144
  1.5 2.6 %collective-permute-start = (f32[64,2304]{1,0:T(8,128)S(1)}, f32[64,2304]{1,0:T(8,128)S(1)}, u32[]{:S(2)}, u32[]{:S(2)}) collective-permute-start(f32[64,2304]{1,0:T(8,128)S(1)} %get-tuple-element.22.refs_0_), channel_id=1, source_target_pairs={{0,4},{4,0},{8,12},{12,8},{16,20},{20,16},{24,28},{28,24},{1,5},{5... | collective-permute-start | bytes 1769480 | tf_op jit(solution)/shard_map/ppermute | solution.py:18
  4.0 4.7 %collective-permute-start.6 = (f32[64,2304]{1,0:T(8,128)S(1)}, f32[64,2304]{1,0:T(8,128)S(1)}, u32[]{:S(2)}, u32[]{:S(2)}) collective-permute-start(f32[64,2304]{1,0:T(8,128)S(1)} %get-tuple-element.22.refs_0_), channel_id=1, source_target_pairs={{4,8},{8,4},{12,16},{16,12},{20,24},{24,20},{28,0},{0,28},{5,9},{9... | collective-permute-start | bytes 1769480 | tf_op jit(solution)/shard_map/ppermute | solution.py:22
  8.7 0.0 collective-permute-start.5
  8.7 1.5 %collective-permute-start.7 = (f32[64,2304]{1,0:T(8,128)S(1)}, f32[64,2304]{1,0:T(8,128)S(1)}, u32[]{:S(2)}, u32[]{:S(2)}) collective-permute-start(f32[64,2304]{1,0:T(8,128)S(1)} %get-tuple-element.21), channel_id=1, source_target_pairs={{4,8},{8,4},{12,16},{16,12},{20,24},{24,20},{28,0},{0,28},{5,9},{9... | collective-permute-start | bytes 1769480 | tf_op jit(solution)/shard_map/ppermute | solution.py:22
  10.2 5.9 %collective-permute-done = f32[64,2304]{1,0:T(8,128)S(1)} collective-permute-done((f32[64,2304]{1,0:T(8,128)S(1)}, f32[64,2304]{1,0:T(8,128)S(1)}, u32[]{:S(2)}, u32[]{:S(2)}) %collective-permute-start) | collective-permute-done | bytes 589856 | tf_op jit(solution)/shard_map/ppermute | solution.py:18
  16.0 6.1 %collective-permute-start.1 = (f32[64,2304]{1,0:T(8,128)S(1)}, f32[64,2304]{1,0:T(8,128)S(1)}, u32[]{:S(2)}, u32[]{:S(2)}) collective-permute-start(f32[64,2304]{1,0:T(8,128)S(1)} %collective-permute-done), channel_id=1, source_target_pairs={{4,8},{8,4},{12,16},{16,12},{20,24},{24,20},{28,0},{0,28},{5,9},{9... | collective-permute-start | bytes 1769480 | tf_op jit(solution)/shard_map/ppermute | solution.py:22
  22.2 0.0 copy-done
  22.2 0.2 slice_select_fusion
  22.4 0.1 collective-permute-start.2
  22.5 6.2 %collective-permute-done.5.refs_1_ = f32[64,2304]{1,0:T(8,128)S(1)} collective-permute-done((f32[64,2304]{1,0:T(8,128)S(1)}, f32[64,2304]{1,0:T(8,128)S(1)}, u32[]{:S(2)}, u32[]{:S(2)}) %collective-permute-start.5) | collective-permute-done | bytes 589856 | tf_op jit(solution)/shard_map/ppermute | solution.py:18
  28.7 0.0 collective-permute-done.6.refs_2_
  28.7 6.1 %collective-permute-start.9 = (f32[64,2304]{1,0:T(8,128)S(1)}, f32[64,2304]{1,0:T(8,128)S(1)}, u32[]{:S(2)}, u32[]{:S(2)}) collective-permute-start(f32[64,2304]{1,0:T(8,128)S(1)} %collective-permute-done.5.refs_1_), channel_id=1, source_target_pairs={{4,8},{8,4},{12,16},{16,12},{20,24},{24,20},{28,0},{0,28},{5,9},{9... | collective-permute-start | bytes 1769480 | tf_op jit(solution)/shard_map/ppermute | solution.py:22
  34.8 0.0 collective-permute-done.7
  34.8 0.0 collective-permute-start.8
  34.8 3.3 %collective-permute-done.2.refs_8_ = f32[48,2304]{1,0:T(8,128)S(1)} collective-permute-done((f32[48,2304]{1,0:T(8,128)S(1)}, f32[48,2304]{1,0:T(8,128)S(1)}, u32[]{:S(2)}, u32[]{:S(2)}) %collective-permute-start.2) | collective-permute-done | bytes 442400 | tf_op jit(solution)/shard_map/ppermute | solution.py:18
  38.1 8.6 %collective-permute-done.1 = f32[64,2304]{1,0:T(8,128)S(1)} collective-permute-done((f32[64,2304]{1,0:T(8,128)S(1)}, f32[64,2304]{1,0:T(8,128)S(1)}, u32[]{:S(2)}, u32[]{:S(2)}) %collective-permute-start.1) | collective-permute-done | bytes 589856 | tf_op jit(solution)/shard_map/ppermute | solution.py:22
  46.7 0.0 collective-permute-start.3
  46.8 12.6 %collective-permute-done.9.refs_1_.refs_4_ = f32[64,2304]{1,0:T(8,128)S(1)} collective-permute-done((f32[64,2304]{1,0:T(8,128)S(1)}, f32[64,2304]{1,0:T(8,128)S(1)}, u32[]{:S(2)}, u32[]{:S(2)}) %collective-permute-start.9) | collective-permute-done | bytes 589856 | tf_op jit(solution)/shard_map/ppermute | solution.py:22
  59.4 0.0 collective-permute-start.11
  59.4 0.0 collective-permute-done.8.refs_0_.refs_3_
  59.4 2.4 %collective-permute-start.10 = (f32[64,2304]{1,0:T(8,128)S(1)}, f32[64,2304]{1,0:T(8,128)S(1)}, u32[]{:S(2)}, u32[]{:S(2)}) collective-permute-start(f32[64,2304]{1,0:T(8,128)S(1)} %collective-permute-done.8.refs_0_.refs_3_), channel_id=1, source_target_pairs={{4,8},{8,4},{12,16},{16,12},{20,24},{24,20},{28,0},{0,28},{5,9},{9... | collective-permute-start | bytes 1769480 | tf_op jit(solution)/shard_map/ppermute | solution.py:22
  61.7 1.7 %collective-permute-done.3.refs_1_.refs_6_ = f32[64,2304]{1,0:T(8,128)S(1)} collective-permute-done((f32[64,2304]{1,0:T(8,128)S(1)}, f32[64,2304]{1,0:T(8,128)S(1)}, u32[]{:S(2)}, u32[]{:S(2)}) %collective-permute-start.3) | collective-permute-done | bytes 589856 | tf_op jit(solution)/shard_map/ppermute | solution.py:18
  63.4 6.1 %collective-permute-start.4 = (f32[64,2304]{1,0:T(8,128)S(1)}, f32[64,2304]{1,0:T(8,128)S(1)}, u32[]{:S(2)}, u32[]{:S(2)}) collective-permute-start(f32[64,2304]{1,0:T(8,128)S(1)} %collective-permute-done.3.refs_1_.refs_6_), channel_id=1, source_target_pairs={{4,8},{8,4},{12,16},{16,12},{20,24},{24,20},{28,0},{0,28},{5,9},{9... | collective-permute-start | bytes 1769480 | tf_op jit(solution)/shard_map/ppermute | solution.py:22
  69.6 0.4 shard_map.28.refs_3_.refs_2_.refs_7_
  70.0 2.0 %shard_map.29.refs_3_ = f32[2,2,4,64,128]{4,3,2,1,0:T(8,128)S(1)} custom-call(f32[64,2304]{1,0:T(8,128)S(1)} %get-tuple-element.22.refs_0_, f32[64,2304]{1,0:T(8,128)S(1)} %collective-permute-done.5.refs_1_, f32[64,2304]{1,0:T(8,128)S(1)} %collective-permute-done.6.refs_2_, ...), custom_call_target="tpu_custom_call", output_to_operand_aliasing={{}: (4, {})} | custom-call | tf_op jit(solution)/shard_map/pallas_call | solution.py:64
  72.0 1.4 %shard_map.30.refs_3_ = f32[2,2,4,64,128]{4,3,2,1,0:T(8,128)S(1)} custom-call(f32[64,2304]{1,0:T(8,128)S(1)} %collective-permute-done.8.refs_0_.refs_3_, f32[64,2304]{1,0:T(8,128)S(1)} %collective-permute-done.9.refs_1_.refs_4_, f32[2304,128]{1,0:T(8,128)S(1)} %shard_map.28.refs_3_.refs_2_.refs_7_, ...), custom_call_target="tpu_custom_call", output_to_operand_aliasing={{}: (3, {})} | custom-call | tf_op jit(solution)/shard_map/pallas_call | solution.py:64
  73.4 0.5 collective-permute-done.10.refs_0_.refs_5_
  73.8 1.4 %shard_map.31.refs_10_ = f32[2,2,4,64,128]{4,3,2,1,0:T(8,128)S(1)} custom-call(f32[64,2304]{1,0:T(8,128)S(1)} %collective-permute-done.10.refs_0_.refs_5_, f32[64,2304]{1,0:T(8,128)S(1)} %collective-permute-done.3.refs_1_.refs_6_, f32[2304,128]{1,0:T(8,128)S(1)} %shard_map.28.refs_3_.refs_2_.refs_7_, ...), custom_call_target="tpu_custom_call", output_to_operand_aliasing={{}: (3, {})} | custom-call | tf_op jit(solution)/shard_map/pallas_call | solution.py:64
  75.2 4.0 %collective-permute-done.11.refs_9_ = f32[80,2304]{1,0:T(8,128)S(1)} collective-permute-done((f32[80,2304]{1,0:T(8,128)S(1)}, f32[80,2304]{1,0:T(8,128)S(1)}, u32[]{:S(2)}, u32[]{:S(2)}) %collective-permute-start.11) | collective-permute-done | bytes 737312 | tf_op jit(solution)/shard_map/ppermute | solution.py:18
  79.2 3.6 %shard_map.32 = (f32[2,2,4,64,128]{4,3,2,1,0:T(8,128)S(1)}, f32[2304,256]{1,0:T(8,128)S(1)}) custom-call(f32[64,2304]{1,0:T(8,128)S(1)} %get-tuple-element.22.refs_0_, f32[64,2304]{1,0:T(8,128)S(1)} %collective-permute-done.5.refs_1_, f32[64,2304]{1,0:T(8,128)S(1)} %collective-permute-done.6.refs_2_, ...), custom_call_target="tpu_custom_call", output_to_operand_aliasing={{0}: (10, {})} | custom-call | tf_op jit(solution)/shard_map/pallas_call | solution.py:92
  82.8 3.7 %collective-permute-done.4.last_ref = f32[64,2304]{1,0:T(8,128)S(1)} collective-permute-done((f32[64,2304]{1,0:T(8,128)S(1)}, f32[64,2304]{1,0:T(8,128)S(1)}, u32[]{:S(2)}, u32[]{:S(2)}) %collective-permute-start.4) | collective-permute-done | bytes 589856 | tf_op jit(solution)/shard_map/ppermute | solution.py:22
  86.5 1.4 %shard_map.33 = (f32[2,4,64,128]{3,2,1,0:T(8,128)S(1)}, f32[2,4,64,128]{3,2,1,0:T(8,128)S(1)}) custom-call(f32[64,2304]{1,0:T(8,128)S(1)} %collective-permute-done.4.last_ref, f32[2304,256]{1,0:T(8,128)S(1)} %get-tuple-element.15.both_ref, f32[2,2,4,64,128]{4,3,2,1,0:T(8,128)S(1)} %get-tuple-element.16.old), custom_call_target="tpu_custom_call" | custom-call | tf_op jit(solution)/shard_map/pallas_call | solution.py:127
  87.9 2.6 %collective-permute-start.12 = (f32[2,4,64,128]{3,2,1,0:T(8,128)S(1)}, f32[2,4,64,128]{3,2,1,0:T(8,128)S(1)}, u32[]{:S(2)}, u32[]{:S(2)}) collective-permute-start(f32[2,4,64,128]{3,2,1,0:T(8,128)S(1)} %get-tuple-element.18), channel_id=1, source_target_pairs={{0,32},{32,0},{1,33},{33,1},{2,34},{34,2},{3,35},{35,3},{4,36},{36... | collective-permute-start | bytes 786440 | tf_op jit(solution)/shard_map/ppermute | solution.py:168
  90.5 1.2 %collective-permute-done.12 = f32[2,4,64,128]{3,2,1,0:T(8,128)S(1)} collective-permute-done((f32[2,4,64,128]{3,2,1,0:T(8,128)S(1)}, f32[2,4,64,128]{3,2,1,0:T(8,128)S(1)}, u32[]{:S(2)}, u32[]{:S(2)}) %collective-permute-start.12) | collective-permute-done | bytes 262176 | tf_op jit(solution)/shard_map/ppermute | solution.py:168
  91.7 14.8 %all_to_all.5 = f32[32,16,128]{2,1,0:T(8,128)S(1)} all-to-all(f32[32,16,128]{2,1,0:T(8,128)S(1)} %bitcast.1), channel_id=1, replica_groups=mesh['x'=4,'core'=2,'zhi'=4,'zlo'=2,'layer'=4] {'zlo','x','layer'}, dimensions={0} | all-to-all | bytes 524288 | tf_op jit(solution)/shard_map/all_to_all | solution.py:172
  106.5 0.6 reduce_sum.9
  (4 shorter events, 0.2 us)
Async XLA Ops:
  0.0 22.2 %copy-start = (f32[128,4608]{1,0:T(8,128)S(1)}, f32[128,4608]{1,0:T(8,128)}, u32[]{:S(2)}) copy-start(f32[128,4608]{1,0:T(8,128)} %param.3) | copy-start | bytes 7077892
  1.5 14.6 %collective-permute-start = (f32[64,2304]{1,0:T(8,128)S(1)}, f32[64,2304]{1,0:T(8,128)S(1)}, u32[]{:S(2)}, u32[]{:S(2)}) collective-permute-start(f32[64,2304]{1,0:T(8,128)S(1)} %get-tuple-element.22.refs_0_), channel_id=1, source_target_pairs={{0,4},{4,0},{8,12},{12,8},{16,20},{20,16},{24,28},{28,24},{1,5},{5... | collective-permute-start | bytes 1769480 | tf_op jit(solution)/shard_map/ppermute | solution.py:18
  4.0 24.6 %collective-permute-start.6 = (f32[64,2304]{1,0:T(8,128)S(1)}, f32[64,2304]{1,0:T(8,128)S(1)}, u32[]{:S(2)}, u32[]{:S(2)}) collective-permute-start(f32[64,2304]{1,0:T(8,128)S(1)} %get-tuple-element.22.refs_0_), channel_id=1, source_target_pairs={{4,8},{8,4},{12,16},{16,12},{20,24},{24,20},{28,0},{0,28},{5,9},{9... | collective-permute-start | bytes 1769480 | tf_op jit(solution)/shard_map/ppermute | solution.py:22
  8.7 20.0 %collective-permute-start.5 = (f32[64,2304]{1,0:T(8,128)S(1)}, f32[64,2304]{1,0:T(8,128)S(1)}, u32[]{:S(2)}, u32[]{:S(2)}) collective-permute-start(f32[64,2304]{1,0:T(8,128)S(1)} %get-tuple-element.21), channel_id=1, source_target_pairs={{0,4},{4,0},{8,12},{12,8},{16,20},{20,16},{24,28},{28,24},{1,5},{5... | collective-permute-start | bytes 1769480 | tf_op jit(solution)/shard_map/ppermute | solution.py:18
  8.7 26.1 %collective-permute-start.7 = (f32[64,2304]{1,0:T(8,128)S(1)}, f32[64,2304]{1,0:T(8,128)S(1)}, u32[]{:S(2)}, u32[]{:S(2)}) collective-permute-start(f32[64,2304]{1,0:T(8,128)S(1)} %get-tuple-element.21), channel_id=1, source_target_pairs={{4,8},{8,4},{12,16},{16,12},{20,24},{24,20},{28,0},{0,28},{5,9},{9... | collective-permute-start | bytes 1769480 | tf_op jit(solution)/shard_map/ppermute | solution.py:22
  16.0 30.7 %collective-permute-start.1 = (f32[64,2304]{1,0:T(8,128)S(1)}, f32[64,2304]{1,0:T(8,128)S(1)}, u32[]{:S(2)}, u32[]{:S(2)}) collective-permute-start(f32[64,2304]{1,0:T(8,128)S(1)} %collective-permute-done), channel_id=1, source_target_pairs={{4,8},{8,4},{12,16},{16,12},{20,24},{24,20},{28,0},{0,28},{5,9},{9... | collective-permute-start | bytes 1769480 | tf_op jit(solution)/shard_map/ppermute | solution.py:22
  22.4 15.8 %collective-permute-start.2 = (f32[48,2304]{1,0:T(8,128)S(1)}, f32[48,2304]{1,0:T(8,128)S(1)}, u32[]{:S(2)}, u32[]{:S(2)}) collective-permute-start(f32[48,2304]{1,0:T(8,128)S(1)} %slice.24), channel_id=1, source_target_pairs={{0,4},{4,0},{8,12},{12,8},{16,20},{20,16},{24,28},{28,24},{1,5},{5... | collective-permute-start | bytes 1327112 | tf_op jit(solution)/shard_map/ppermute | solution.py:18
  28.7 30.7 %collective-permute-start.9 = (f32[64,2304]{1,0:T(8,128)S(1)}, f32[64,2304]{1,0:T(8,128)S(1)}, u32[]{:S(2)}, u32[]{:S(2)}) collective-permute-start(f32[64,2304]{1,0:T(8,128)S(1)} %collective-permute-done.5.refs_1_), channel_id=1, source_target_pairs={{4,8},{8,4},{12,16},{16,12},{20,24},{24,20},{28,0},{0,28},{5,9},{9... | collective-permute-start | bytes 1769480 | tf_op jit(solution)/shard_map/ppermute | solution.py:22
  34.8 24.5 %collective-permute-start.8 = (f32[64,2304]{1,0:T(8,128)S(1)}, f32[64,2304]{1,0:T(8,128)S(1)}, u32[]{:S(2)}, u32[]{:S(2)}) collective-permute-start(f32[64,2304]{1,0:T(8,128)S(1)} %collective-permute-done.7), channel_id=1, source_target_pairs={{0,4},{4,0},{8,12},{12,8},{16,20},{20,16},{24,28},{28,24},{1,5},{5... | collective-permute-start | bytes 1769480 | tf_op jit(solution)/shard_map/ppermute | solution.py:18
  46.7 16.7 %collective-permute-start.3 = (f32[64,2304]{1,0:T(8,128)S(1)}, f32[64,2304]{1,0:T(8,128)S(1)}, u32[]{:S(2)}, u32[]{:S(2)}) collective-permute-start(f32[64,2304]{1,0:T(8,128)S(1)} %collective-permute-done.1), channel_id=1, source_target_pairs={{0,4},{4,0},{8,12},{12,8},{16,20},{20,16},{24,28},{28,24},{1,5},{5... | collective-permute-start | bytes 1769480 | tf_op jit(solution)/shard_map/ppermute | solution.py:18
  59.4 19.9 %collective-permute-start.11 = (f32[80,2304]{1,0:T(8,128)S(1)}, f32[80,2304]{1,0:T(8,128)S(1)}, u32[]{:S(2)}, u32[]{:S(2)}) collective-permute-start(f32[80,2304]{1,0:T(8,128)S(1)} %slice.25), channel_id=1, source_target_pairs={{0,4},{4,0},{8,12},{12,8},{16,20},{20,16},{24,28},{28,24},{1,5},{5... | collective-permute-start | bytes 2211848 | tf_op jit(solution)/shard_map/ppermute | solution.py:18
  59.4 14.5 %collective-permute-start.10 = (f32[64,2304]{1,0:T(8,128)S(1)}, f32[64,2304]{1,0:T(8,128)S(1)}, u32[]{:S(2)}, u32[]{:S(2)}) collective-permute-start(f32[64,2304]{1,0:T(8,128)S(1)} %collective-permute-done.8.refs_0_.refs_3_), channel_id=1, source_target_pairs={{4,8},{8,4},{12,16},{16,12},{20,24},{24,20},{28,0},{0,28},{5,9},{9... | collective-permute-start | bytes 1769480 | tf_op jit(solution)/shard_map/ppermute | solution.py:22
  63.4 23.1 %collective-permute-start.4 = (f32[64,2304]{1,0:T(8,128)S(1)}, f32[64,2304]{1,0:T(8,128)S(1)}, u32[]{:S(2)}, u32[]{:S(2)}) collective-permute-start(f32[64,2304]{1,0:T(8,128)S(1)} %collective-permute-done.3.refs_1_.refs_6_), channel_id=1, source_target_pairs={{4,8},{8,4},{12,16},{16,12},{20,24},{24,20},{28,0},{0,28},{5,9},{9... | collective-permute-start | bytes 1769480 | tf_op jit(solution)/shard_map/ppermute | solution.py:22
  87.9 3.7 %collective-permute-start.12 = (f32[2,4,64,128]{3,2,1,0:T(8,128)S(1)}, f32[2,4,64,128]{3,2,1,0:T(8,128)S(1)}, u32[]{:S(2)}, u32[]{:S(2)}) collective-permute-start(f32[2,4,64,128]{3,2,1,0:T(8,128)S(1)} %get-tuple-element.18), channel_id=1, source_target_pairs={{0,32},{32,0},{1,33},{33,1},{2,34},{34,2},{3,35},{35,3},{4,36},{36... | collective-permute-start | bytes 786440 | tf_op jit(solution)/shard_map/ppermute | solution.py:168
